TPU v7x, 32 devices: a whole 2x2x4 slice. The times are simulated.
32 devices in a mesh: dp: 2 (over y), blk: 8 (over z, x), chan: 2 (over core).
Axes of the slice: x: 2, y: 2, z: 4, core: 2. Of those that a mesh axis runs over, the one named last changes fastest.
Arguments:
- features: bfloat16 [1024, 512], P(('dp', 'blk'), 'chan'), parts along dimension 0, may hold values from -6 to 6
- chrom_len: int32 [2], P('dp'), parts along dimension 0, may hold values from 320 to 512
- band_mask: int32 [16, 4], P('dp'), parts along dimension 0, may hold values 0 or 1
- conv_weight: bfloat16 [2, 3, 512, 512], P(None, None, None, 'chan'), may hold values from -0.15625 to 0.15625
- conv_bias: bfloat16 [2, 512], P(None, 'chan'), may hold values from -3 to 3
- proj_weight: bfloat16 [512, 128], replicated, may hold values from -0.25 to 0.25
- proj_bias: bfloat16 [128], replicated, may hold values from -3 to 3
- map_weight: bfloat16 [3, 3, 64, 64], P(None, None, 'chan'), may hold values from -0.25 to 0.25
- map_bias: bfloat16 [64], P('chan'), may hold values from -3 to 3
- head_weight: bfloat16 [64], P('chan'), may hold values from -0.75 to 0.75
Outputs:
- contact: float32 [1024, 256], P(('dp', 'blk'), 'chan'), parts along dimension 0
There are 2 independent parts, one for each index of `dp`. A program takes and returns all parts, laid end to end along the dimension named above; an argument that names none is the same for every part. Nothing has to cross between parts.
Inputs may be any that keep to these rules, and one draw needn't show every extreme that they name: Bins from chrom_len[0] on are padding. `band_mask`: 1 marks a predicted tile.
All inputs are finite; a program needn't handle non-finite values.
Results may differ from a plain program's by a relative error of at most 0.0053.
Values may be sent and summed in bfloat16 or wider, within the bound.
No kernel may reach another device: no remote copies, remote signals or barrier semaphores. Data moves between devices by JAX's collectives and lax.ppermute only.
A program may use at most 64 MiB of HBM per device.

v0:
```python
import jax
import jax.numpy as jnp
from jax import lax
from jax.experimental import pallas as pl
from jax.experimental.pallas import tpu as pltpu
from jax.sharding import PartitionSpec as P

F2 = 64
BAND = 3
CONV1 = 2
D2 = 2
HALO = 16
F32 = jnp.float32
BF16 = jnp.bfloat16


def chan_swap(value):
    return lax.ppermute(value, "chan", [(0, 1), (1, 0)])


def blk_permute(value, offset_0, offset_1):
    count = lax.axis_size("blk")
    pairs = []
    for i in range(count):
        pairs.append((((i + offset_0) % count) * 2, i * 2))
        pairs.append((((i + offset_1) % count) * 2 + 1, i * 2 + 1))
    return lax.ppermute(value, ("blk", "chan"), pairs)


def prep_kernel(
    length_ref,
    mask_ref,
    mw_own_ref,
    mw_oth_ref,
    mb_own_ref,
    mb_oth_ref,
    hw_own_ref,
    hw_oth_ref,
    cb_own_ref,
    cb_oth_ref,
    pb_ref,
    wbig_ref,
    col_mask_ref,
    valid_ref,
    small_ref,
    head_ref,
    wt_s,
    taps_s,
):
    rows = valid_ref.shape[0]
    columns = col_mask_ref.shape[1]
    bins = columns // 2
    half = mw_own_ref.shape[2]
    col_rows = columns + 2 * HALO
    count = lax.axis_size("blk")
    i = lax.axis_index("blk")
    c = lax.axis_index("chan")
    first = i * bins
    first_col = first + c * columns
    length = length_ref[...]

    for source, side in ((mw_own_ref, c), (mw_oth_ref, 1 - c)):
        at = pl.ds(pl.multiple_of(side * half, half), half)
        for s in range(3):
            for r in range(3):
                taps_s[3 * s + r, at, :] = source[s, r].astype(F32)
    blank = jnp.zeros((F2, F2), F32)
    for j in range(4):
        pieces = []
        for m in range(6):
            for r in range(3):
                pieces.append(taps_s[3 * (m - j) + r] if 0 <= m - j < 3 else blank)
        for tile in range(9):
            wt_s[j * F2 : (j + 1) * F2, tile * 2 * F2 : (tile + 1) * 2 * F2] = jnp.concatenate(
                pieces[2 * tile : 2 * tile + 2], axis=1
            )
    wbig_ref[...] = wt_s[...].T.astype(BF16)

    def spread(own_ref, oth_ref, repeats):
        o = lax.broadcasted_iota(jnp.int32, (half, repeats * F2), 0)
        lane = lax.broadcasted_iota(jnp.int32, (half, repeats * F2), 1) % F2
        total = jnp.zeros((16, repeats * F2), F32)
        for ref, side in ((own_ref, c), (oth_ref, 1 - c)):
            pick = (lane == side * half + o).astype(BF16)
            value = jnp.broadcast_to(ref[...], (16, half)).astype(BF16)
            total = total + jnp.dot(value, pick, preferred_element_type=F32)
        return total

    head_all = spread(hw_own_ref, hw_oth_ref, 8)
    q = lax.broadcasted_iota(jnp.int32, (16, 8 * F2), 0)
    k = lax.broadcasted_iota(jnp.int32, (16, 8 * F2), 1)
    head_ref[...] = jnp.where(
        q == 2 * ((k % (4 * F2)) // F2) + k // (4 * F2), head_all, 0.0
    ).astype(BF16)
    bias_all = spread(mb_own_ref, mb_oth_ref, 4)

    minus = F32(-jnp.inf)
    block = lax.broadcasted_iota(jnp.int32, (BAND + 1, count), 1)

    def live_at(y, variant):
        at_row = jnp.sum(jnp.where(block == i + variant, mask_ref[...], 0), axis=1, keepdims=True)
        offset = lax.broadcasted_iota(jnp.int32, (BAND + 1, 1), 0)

        def entry(u):
            return jnp.sum(
                jnp.where(offset == 2 * c + u - variant, at_row, 0), axis=0, keepdims=True
            )

        value = jnp.where(
            y < 0,
            entry(-1),
            jnp.where(y < bins, entry(0), jnp.where(y < columns, entry(1), entry(2))),
        )
        column = first_col + y
        return (value != 0) & (column >= 0) & (column < length)

    b_index = lax.broadcasted_iota(jnp.int32, (columns, 2 * F2), 0)
    low = lax.broadcasted_iota(jnp.int32, (columns, 2 * F2), 1) < F2
    masks = {}
    for variant in (-1, 0, 1):
        for r in range(3):
            masks[variant, r] = jnp.where(
                live_at(b_index + (r - 1) * D2, variant), 0.0, minus
            )
    for at, (v0, v1) in enumerate(((-1, 0), (0, 0), (0, 1))):
        col_mask_ref[at, :, : 2 * F2] = jnp.where(low, masks[v0, 0], masks[v0, 1])
        col_mask_ref[at, :, 2 * F2 : 4 * F2] = jnp.where(low, masks[v0, 2], masks[v1, 0])
        col_mask_ref[at, :, 4 * F2 :] = jnp.where(low, masks[v1, 1], masks[v1, 2])

    place = lax.broadcasted_iota(jnp.int32, (rows, 2 * F2), 0)
    bin_index = jnp.where(
        place < col_rows, first_col - HALO + place, first - HALO - col_rows + place
    )
    valid_ref[...] = jnp.where((bin_index >= 0) & (bin_index < length), 1.0, 0.0)

    small_ref[0:2, :] = cb_own_ref[...].astype(F32)
    small_ref[2:4, :] = cb_oth_ref[...].astype(F32)
    small_ref[4:5, :] = bias_all[:1]
    small_ref[5:6, : 2 * F2] = pb_ref[...].astype(F32)
    small_ref[5:6, 2 * F2 :] = jnp.where(
        live_at(lax.broadcasted_iota(jnp.int32, (1, columns), 1), 0), 1.0, 0.0
    )


def contact_kernel(
    own_ref,
    r1_ref,
    r2_ref,
    r3_ref,
    s1_ref,
    s3_ref,
    w_own_ref,
    w_oth_ref,
    pw_ref,
    wbig_ref,
    col_mask_ref,
    valid_ref,
    small_ref,
    head_ref,
    out_ref,
    h_s,
    pa6_s,
    x_s,
    mix_s,
):
    bins = own_ref.shape[1]
    half = own_ref.shape[2]
    col_rows = 2 * bins + 2 * HALO
    row_rows = bins + 2 * HALO
    rows = col_rows + row_rows
    count = lax.axis_size("blk")
    i = lax.axis_index("blk")
    c = lax.axis_index("chan")
    first = i * bins
    first_col = first + c * (2 * bins)

    def put(start, number, ref, source):
        keep = valid_ref[start : start + number, :] != 0
        for part in range(2):
            for at in range(0, half, 128):
                h_s[start : start + number, part * half + at : part * half + at + 128] = jnp.where(
                    keep, ref[part, source : source + number, at : at + 128].astype(F32), 0.0
                )

    tail = bins - HALO
    put(0, HALO, r1_ref, tail)
    put(col_rows + HALO, bins, own_ref, 0)

    @pl.when(c == 0)
    def _():
        put(HALO, bins, own_ref, 0)
        put(HALO + bins, bins, s1_ref, 0)
        put(HALO + 2 * bins, HALO, r2_ref, 0)
        put(col_rows, HALO, r1_ref, tail)
        put(col_rows + HALO + bins, HALO, s1_ref, 0)

    @pl.when(c == 1)
    def _():
        put(HALO, bins, r2_ref, 0)
        put(HALO + bins, bins, r3_ref, 0)
        put(HALO + 2 * bins, HALO, s3_ref, 0)
        put(col_rows, HALO, s1_ref, tail)
        put(col_rows + HALO + bins, HALO, r1_ref, 0)

    place = lax.broadcasted_iota(jnp.int32, (rows, 1), 0)
    bin_index = jnp.where(
        place < col_rows, first_col - HALO + place, first - HALO - col_rows + place
    )
    inside = (bin_index >= 0) & (bin_index < count * bins)

    for layer in range(CONV1):
        e = 2 ** (layer + 1)
        hidden = h_s[...]
        taps = [
            (hidden if t == 1 else pltpu.roll(hidden, ((1 - t) * e) % rows, axis=0)).astype(BF16)
            for t in range(3)
        ]
        for at, (w_ref, side) in enumerate(((w_own_ref, c), (w_oth_ref, 1 - c))):
            q = jnp.dot(taps[0], w_ref[layer, 0], preferred_element_type=F32)
            q = q + jnp.dot(taps[1], w_ref[layer, 1], preferred_element_type=F32)
            q = q + jnp.dot(taps[2], w_ref[layer, 2], preferred_element_type=F32)
            lanes = pl.ds(pl.multiple_of(side * half, half), half)
            bias = small_ref[2 * at + layer : 2 * at + layer + 1, :]
            new = (h_s[:, lanes] + jnp.maximum(q + bias, 0.0)).astype(BF16).astype(F32)
            h_s[:, lanes] = jnp.where(inside, new, 0.0)

    proj = jnp.dot(h_s[...].astype(BF16), pw_ref[...], preferred_element_type=F32)
    proj = (proj + small_ref[5:6, : 2 * F2]).astype(BF16).astype(F32)

    minus = F32(-jnp.inf)
    low = lax.broadcasted_iota(jnp.int32, (1, 2 * F2), 1) < F2
    pcol = proj[:col_rows]
    pcol = jnp.where(low, pltpu.roll(pcol, F2, axis=1), pcol)
    shifted = [
        pltpu.roll(pcol, col_rows - HALO - (r - 1) * D2, axis=0)[: 2 * bins] for r in range(3)
    ]
    tiles = [
        jnp.where(low, shifted[0], shifted[1]),
        jnp.where(low, shifted[2], shifted[0]),
        jnp.where(low, shifted[1], shifted[2]),
    ]
    tiled = jnp.concatenate(tiles, axis=1)
    col_first, col_mid, col_last = [
        (tiled + col_mask_ref[at]).astype(BF16).reshape(2 * bins // 16, 16, 6 * F2)
        for at in range(3)
    ]
    col_centre = shifted[1].astype(BF16).reshape(2 * bins // 16, 16, 2 * F2)

    prow = proj[col_rows:]
    prow = jnp.where(low, prow, pltpu.roll(prow, F2, axis=1))
    prow = jnp.where(valid_ref[col_rows:, :] != 0, prow, minus)
    prow_next = pltpu.roll(prow, row_rows - D2, axis=0)
    pa6_s[:, : 2 * F2] = prow
    pa6_s[:, 2 * F2 : 4 * F2] = jnp.where(low, prow, prow_next)
    pa6_s[:, 4 * F2 :] = prow_next

    groups = bins // 8
    per_dot = x_s.shape[0] // (2 * bins)
    zero = jnp.zeros((), BF16)
    bias4 = small_ref[4:5, :]
    for v in range(2):
        for start in range(0, groups, per_dot):
            for slot in range(2 * start, 2 * (start + per_dot) + 1):
                at = HALO - D2 + v + 4 * slot
                row = jnp.broadcast_to(pa6_s[at : at + 1, :], (16, 6 * F2)).astype(BF16)
                cols = col_first if slot == 0 else col_last if slot == 2 * groups else col_mid
                value = jnp.maximum(row[None] + cols, zero).reshape(2 * bins, 6 * F2)
                for s in range(3):
                    if (slot - s) % 2 == 0 and start <= (slot - s) // 2 < start + per_dot:
                        at_row = ((slot - s) // 2 - start) * 2 * bins
                        x_s[at_row : at_row + 2 * bins, s * 6 * F2 : (s + 1) * 6 * F2] = value
            y = jnp.dot(x_s[...], wbig_ref[...], preferred_element_type=F32)
            y = jnp.maximum(y + bias4, 0.0)
            for group in range(start, start + per_dot):
                at = HALO + v + 8 * group
                parts = []
                for k in range(2):
                    row = pa6_s[at + 4 * k : at + 4 * k + 1, 2 * F2 : 4 * F2]
                    row = jnp.broadcast_to(row, (16, 2 * F2)).astype(BF16)
                    parts.append(
                        jnp.maximum(row[None] + col_centre, zero).reshape(2 * bins, 2 * F2)
                    )
                centre = jnp.concatenate(parts, axis=1).astype(F32)
                at_row = (group - start) * 2 * bins
                mixed = y[at_row : at_row + 2 * bins] + centre
                mix_s[group, :, v * 4 * F2 : (v + 1) * 4 * F2] = mixed.astype(BF16)

    lane_live = small_ref[5:6, 2 * F2 :] != 0
    for group in range(groups):
        value = lax.dot_general(
            head_ref[...], mix_s[group], (((1,), (1,)), ((), ())), preferred_element_type=F32
        )[:8]
        at = col_rows + HALO + 8 * group
        out_ref[8 * group : 8 * group + 8, :] = jnp.where(
            lane_live & (valid_ref[at : at + 8, :] != 0), value, 0.0
        )


def local(
    features,
    chrom_len,
    band_mask,
    conv_weight,
    conv_bias,
    proj_weight,
    proj_bias,
    map_weight,
    map_bias,
    head_weight,
):
    bins, half = features.shape
    own = lax.all_gather(features, "chan", axis=0)
    r2 = blk_permute(own, 2, 2)
    r1 = blk_permute(own, -1, 1)
    r3 = blk_permute(own, 4, 3)
    s1 = chan_swap(r1)
    s3 = chan_swap(r3)
    w_oth = chan_swap(conv_weight)

    rows = 3 * bins + 4 * HALO
    vmem = pl.BlockSpec(memory_space=pltpu.VMEM)
    params = pltpu.CompilerParams(vmem_limit_bytes=24 * 1024 * 1024)
    prepared = pl.pallas_call(
        prep_kernel,
        out_shape=[
            jax.ShapeDtypeStruct((18 * F2, 4 * F2), BF16),
            jax.ShapeDtypeStruct((3, 2 * bins, 6 * F2), F32),
            jax.ShapeDtypeStruct((rows, 2 * F2), F32),
            jax.ShapeDtypeStruct((8, half), F32),
            jax.ShapeDtypeStruct((16, 8 * F2), BF16),
        ],
        in_specs=[vmem] * 11,
        out_specs=[vmem] * 5,
        scratch_shapes=[
            pltpu.VMEM((4 * F2, 18 * F2), F32),
            pltpu.VMEM((9, F2, F2), F32),
        ],
        compiler_params=params,
    )(
        chrom_len[None],
        band_mask.T,
        map_weight,
        chan_swap(map_weight),
        map_bias[None],
        chan_swap(map_bias)[None],
        head_weight[None],
        chan_swap(head_weight)[None],
        conv_bias,
        chan_swap(conv_bias),
        proj_bias[None],
    )
    return pl.pallas_call(
        contact_kernel,
        out_shape=jax.ShapeDtypeStruct((bins, 2 * bins), F32),
        in_specs=[vmem] * 14,
        out_specs=vmem,
        scratch_shapes=[
            pltpu.VMEM((rows, 2 * half), F32),
            pltpu.VMEM((bins + 2 * HALO, 6 * F2), F32),
            pltpu.VMEM((4 * 2 * bins, 18 * F2), BF16),
            pltpu.VMEM((bins // 8, 2 * bins, 8 * F2), BF16),
        ],
        compiler_params=params,
    )(own, r1, r2, r3, s1, s3, conv_weight, w_oth, proj_weight, *prepared)


def solution(mesh):
    return jax.shard_map(
        local,
        mesh=mesh,
        in_specs=(
            P(("dp", "blk"), "chan"),
            P("dp"),
            P("dp", None),
            P(None, None, None, "chan"),
            P(None, "chan"),
            P(),
            P(),
            P(None, None, "chan", None),
            P("chan"),
            P("chan"),
        ),
        out_specs=P(("dp", "blk"), "chan"),
        check_vma=False,
    )
```

profile of v0, /device:TPU:0, one launch (start us, length us, event | category | flops | bytes accessed | tf_op | source)
XLA Modules:
  0.0 32.0 jit_solution(5880737015362714431)
XLA Ops:
  0.0 0.5 %collective-permute-start.5 = (bf16[2,3,512,256]{3,2,1,0:T(8,128)(2,1)}, bf16[2,3,512,256]{3,2,1,0:T(8,128)(2,1)S(1)}, u32[]{:S(2)}, u32[]{:S(2)}) collective-permute-start(bf16[2,3,512,256]{3,2,1,0:T(8,128)(2,1)} %w_own_ref.1), channel_id=1, source_target_pairs={{0,1},{1,0},{2,3},{3,2},{4,5},{5,4},{6,7},{7,6},{8,9},{9,8},{10,11... | collective-permute-start | bytes 4718600 | tf_op jit(solution)/shard_map/ppermute | solution.py:18
  0.5 3.3 %all-gather = bf16[128,256]{1,0:T(8,128)(2,1)S(1)} all-gather(bf16[64,256]{1,0:T(8,128)(2,1)} %param.10), channel_id=2, replica_groups=mesh['dp'=2,'blk'=8,'chan'=2] {'chan'}, dimensions={0}, use_global_device_ids=true | all-gather | bytes 98304 | tf_op jit(solution)/shard_map/all_gather | solution.py:312
  3.7 4.0 %collective-permute-start.2 = (bf16[2,64,256]{2,1,0:T(8,128)(2,1)S(1)}, bf16[2,64,256]{2,1,0:T(8,128)(2,1)S(1)}, u32[]{:S(2)}, u32[]{:S(2)}) collective-permute-start(bf16[2,64,256]{2,1,0:T(8,128)(2,1)S(1)} %bitcast.9), channel_id=1, source_target_pairs={{8,0},{7,1},{10,2},{9,3},{12,4},{11,5},{14,6},{13,7},{0,8},{15,9},... | collective-permute-start | bytes 196616 | tf_op jit(solution)/shard_map/ppermute | solution.py:27
  7.7 1.5 %collective-permute-start = (bf16[2,64,256]{2,1,0:T(8,128)(2,1)S(1)}, bf16[2,64,256]{2,1,0:T(8,128)(2,1)S(1)}, u32[]{:S(2)}, u32[]{:S(2)}) collective-permute-start(bf16[2,64,256]{2,1,0:T(8,128)(2,1)S(1)} %bitcast.10), channel_id=1, source_target_pairs={{14,0},{3,1},{0,2},{5,3},{2,4},{7,5},{4,6},{9,7},{6,8},{11,9},{8,1... | collective-permute-start | bytes 196616 | tf_op jit(solution)/shard_map/ppermute | solution.py:27
  9.2 1.3 %collective-permute-start.1 = (bf16[2,64,256]{2,1,0:T(8,128)(2,1)S(1)}, bf16[2,64,256]{2,1,0:T(8,128)(2,1)S(1)}, u32[]{:S(2)}, u32[]{:S(2)}) collective-permute-start(bf16[2,64,256]{2,1,0:T(8,128)(2,1)S(1)} %bitcast.11), channel_id=1, source_target_pairs={{4,0},{5,1},{6,2},{7,3},{8,4},{9,5},{10,6},{11,7},{12,8},{13,9},{1... | collective-permute-start | bytes 196616 | tf_op jit(solution)/shard_map/ppermute | solution.py:27
  10.6 0.0 collective-permute-done.2.r3_ref
  10.6 0.0 collective-permute-start.4
  10.6 4.3 %collective-permute-done.r1_ref = bf16[2,64,256]{2,1,0:T(8,128)(2,1)S(1)} collective-permute-done((bf16[2,64,256]{2,1,0:T(8,128)(2,1)S(1)}, bf16[2,64,256]{2,1,0:T(8,128)(2,1)S(1)}, u32[]{:S(2)}, u32[]{:S(2)}) %collective-permute-start) | collective-permute-done | bytes 65568 | tf_op jit(solution)/shard_map/ppermute | solution.py:27
  14.8 0.0 collective-permute-start.3
  14.8 0.5 %collective-permute-start.7 = (bf16[32]{0:T(256)(128)(2,1)}, bf16[32]{0:T(256)(128)(2,1)S(1)}, u32[]{:S(2)}, u32[]{:S(2)}) collective-permute-start(bf16[32]{0:T(256)(128)(2,1)} %param.18), channel_id=1, source_target_pairs={{0,1},{1,0},{2,3},{3,2},{4,5},{5,4},{6,7},{7,6},{8,9},{9,8},{10,11... | collective-permute-start | bytes 200 | tf_op jit(solution)/shard_map/ppermute | solution.py:18
  15.4 1.0 %collective-permute-done.7 = bf16[32]{0:T(256)(128)(2,1)S(1)} collective-permute-done((bf16[32]{0:T(256)(128)(2,1)}, bf16[32]{0:T(256)(128)(2,1)S(1)}, u32[]{:S(2)}, u32[]{:S(2)}) %collective-permute-start.7) | collective-permute-done | bytes 96 | tf_op jit(solution)/shard_map/ppermute | solution.py:18
  16.3 0.3 collective-permute-start.8
  16.6 1.0 %collective-permute-done.8 = bf16[32]{0:T(256)(128)(2,1)S(1)} collective-permute-done((bf16[32]{0:T(256)(128)(2,1)}, bf16[32]{0:T(256)(128)(2,1)S(1)}, u32[]{:S(2)}, u32[]{:S(2)}) %collective-permute-start.8) | collective-permute-done | bytes 96 | tf_op jit(solution)/shard_map/ppermute | solution.py:18
  17.6 0.3 collective-permute-start.9
  17.9 1.0 %collective-permute-done.9.cb_oth_ref = bf16[2,256]{1,0:T(2,128)(2,1)S(1)} collective-permute-done((bf16[2,256]{1,0:T(2,128)(2,1)}, bf16[2,256]{1,0:T(2,128)(2,1)S(1)}, u32[]{:S(2)}, u32[]{:S(2)}) %collective-permute-start.9) | collective-permute-done | bytes 1056 | tf_op jit(solution)/shard_map/ppermute | solution.py:18
  18.9 0.3 collective-permute-start.6
  19.9 0.5 %collective-permute-done.6.mw_oth_ref = bf16[3,3,32,64]{3,2,1,0:T(8,128)(2,1)S(1)} collective-permute-done((bf16[3,3,32,64]{3,2,1,0:T(8,128)(2,1)}, bf16[3,3,32,64]{3,2,1,0:T(8,128)(2,1)S(1)}, u32[]{:S(2)}, u32[]{:S(2)}) %collective-permute-start.6) | collective-permute-done | bytes 36896 | tf_op jit(solution)/shard_map/ppermute | solution.py:18
  20.4 0.0 copy-start.2
  20.4 0.9 %copy-done.2 = bf16[3,3,32,64]{3,2,1,0:T(8,128)(2,1)S(1)} copy-done((bf16[3,3,32,64]{3,2,1,0:T(8,128)(2,1)S(1)}, bf16[3,3,32,64]{3,2,1,0:T(8,128)(2,1)}, u32[]{:S(2)}) %copy-start.2) | copy-done | bytes 36888
  21.3 0.0 copy-start.3
  21.3 0.7 %copy-done.3 = s32[8,4]{0,1:T(4,128)S(1)} copy-done((s32[8,4]{0,1:T(4,128)S(1)}, s32[8,4]{0,1:T(4,128)}, u32[]{:S(2)}) %copy-start.3) | copy-done | bytes 152
  22.0 0.0 copy-start.4
  22.0 0.7 %copy-done.4 = bf16[2,256]{1,0:T(2,128)(2,1)S(1)} copy-done((bf16[2,256]{1,0:T(2,128)(2,1)S(1)}, bf16[2,256]{1,0:T(2,128)(2,1)}, u32[]{:S(2)}) %copy-start.4) | copy-done | bytes 1048
  22.6 0.0 copy-start.5
  22.6 0.7 %copy-done.5 = bf16[32]{0:T(256)(128)(2,1)S(1)} copy-done((bf16[32]{0:T(256)(128)(2,1)S(1)}, bf16[32]{0:T(256)(128)(2,1)}, u32[]{:S(2)}) %copy-start.5) | copy-done | bytes 88
  23.3 0.0 copy-start.6
  23.3 0.7 %copy-done.6 = bf16[32]{0:T(256)(128)(2,1)S(1)} copy-done((bf16[32]{0:T(256)(128)(2,1)S(1)}, bf16[32]{0:T(256)(128)(2,1)}, u32[]{:S(2)}) %copy-start.6) | copy-done | bytes 88
  24.0 0.0 copy-start.7
  24.0 0.7 %copy-done.7 = bf16[128]{0:T(256)(128)(2,1)S(1)} copy-done((bf16[128]{0:T(256)(128)(2,1)S(1)}, bf16[128]{0:T(256)(128)(2,1)}, u32[]{:S(2)}) %copy-start.7) | copy-done | bytes 280
  24.6 0.5 %shard_map.100 = (bf16[1152,256]{1,0:T(8,128)(2,1)S(1)}, f32[3,128,384]{2,1,0:T(8,128)S(1)}, f32[256,128]{1,0:T(8,128)S(1)}, f32[8,256]{1,0:T(8,128)S(1)}, bf16[16,512]{1,0:T(8,128)(2,1)S(1)}) custom-call(s32[1,1]{1,0:T(1,128)} %bitcast.8.length_ref, s32[4,8]{1,0:T(4,128)S(1)} %bitcast.13, bf16[3,3,32,64]{3,2,1,0:T(8,128)(2,1)S(1)} %copy-done.2, ...), custom_call_target="tpu_custom_call" | custom-call | tf_op jit(solution)/shard_map/pallas_call | solution.py:323
  25.1 0.0 collective-permute-done.1.r2_ref
  25.2 0.0 collective-permute-done.4.s3_ref
  25.2 0.0 collective-permute-done.3.s1_ref
  25.2 0.0 collective-permute-done.5.w_oth_ref
  25.2 0.0 copy-start
  25.2 1.4 %copy-done = bf16[2,3,512,256]{3,2,1,0:T(8,128)(2,1)S(1)} copy-done((bf16[2,3,512,256]{3,2,1,0:T(8,128)(2,1)S(1)}, bf16[2,3,512,256]{3,2,1,0:T(8,128)(2,1)}, u32[]{:S(2)}) %copy-start) | copy-done | bytes 1572888
  26.6 0.0 copy-start.1
  26.6 0.9 %copy-done.1 = bf16[512,128]{1,0:T(8,128)(2,1)S(1)} copy-done((bf16[512,128]{1,0:T(8,128)(2,1)S(1)}, bf16[512,128]{1,0:T(8,128)(2,1)}, u32[]{:S(2)}) %copy-start.1) | copy-done | bytes 131096
  27.5 4.5 %shard_map.101 = f32[64,128]{1,0:T(8,128)} custom-call(bf16[2,64,256]{2,1,0:T(8,128)(2,1)S(1)} %bitcast.12, bf16[2,64,256]{2,1,0:T(8,128)(2,1)S(1)} %collective-permute-done.r1_ref, bf16[2,64,256]{2,1,0:T(8,128)(2,1)S(1)} %collective-permute-done.1.r2_ref, bf16[2,64,256]{2,1,0:T(8,128)(2,1)S(1)} %collective-permute-done.2.r3_ref, ...), custom_call_target="tpu_custom_call" | custom-call | tf_op jit(solution)/shard_map/pallas_call | solution.py:352
Async XLA Ops:
  0.0 25.2 %collective-permute-start.5 = (bf16[2,3,512,256]{3,2,1,0:T(8,128)(2,1)}, bf16[2,3,512,256]{3,2,1,0:T(8,128)(2,1)S(1)}, u32[]{:S(2)}, u32[]{:S(2)}) collective-permute-start(bf16[2,3,512,256]{3,2,1,0:T(8,128)(2,1)} %w_own_ref.1), channel_id=1, source_target_pairs={{0,1},{1,0},{2,3},{3,2},{4,5},{5,4},{6,7},{7,6},{8,9},{9,8},{10,11... | collective-permute-start | bytes 4718600 | tf_op jit(solution)/shard_map/ppermute | solution.py:18
  3.7 6.8 %collective-permute-start.2 = (bf16[2,64,256]{2,1,0:T(8,128)(2,1)S(1)}, bf16[2,64,256]{2,1,0:T(8,128)(2,1)S(1)}, u32[]{:S(2)}, u32[]{:S(2)}) collective-permute-start(bf16[2,64,256]{2,1,0:T(8,128)(2,1)S(1)} %bitcast.9), channel_id=1, source_target_pairs={{8,0},{7,1},{10,2},{9,3},{12,4},{11,5},{14,6},{13,7},{0,8},{15,9},... | collective-permute-start | bytes 196616 | tf_op jit(solution)/shard_map/ppermute | solution.py:27
  7.7 7.1 %collective-permute-start = (bf16[2,64,256]{2,1,0:T(8,128)(2,1)S(1)}, bf16[2,64,256]{2,1,0:T(8,128)(2,1)S(1)}, u32[]{:S(2)}, u32[]{:S(2)}) collective-permute-start(bf16[2,64,256]{2,1,0:T(8,128)(2,1)S(1)} %bitcast.10), channel_id=1, source_target_pairs={{14,0},{3,1},{0,2},{5,3},{2,4},{7,5},{4,6},{9,7},{6,8},{11,9},{8,1... | collective-permute-start | bytes 196616 | tf_op jit(solution)/shard_map/ppermute | solution.py:27
  9.2 15.9 %collective-permute-start.1 = (bf16[2,64,256]{2,1,0:T(8,128)(2,1)S(1)}, bf16[2,64,256]{2,1,0:T(8,128)(2,1)S(1)}, u32[]{:S(2)}, u32[]{:S(2)}) collective-permute-start(bf16[2,64,256]{2,1,0:T(8,128)(2,1)S(1)} %bitcast.11), channel_id=1, source_target_pairs={{4,0},{5,1},{6,2},{7,3},{8,4},{9,5},{10,6},{11,7},{12,8},{13,9},{1... | collective-permute-start | bytes 196616 | tf_op jit(solution)/shard_map/ppermute | solution.py:27
  10.6 14.6 %collective-permute-start.4 = (bf16[2,64,256]{2,1,0:T(8,128)(2,1)S(1)}, bf16[2,64,256]{2,1,0:T(8,128)(2,1)S(1)}, u32[]{:S(2)}, u32[]{:S(2)}) collective-permute-start(bf16[2,64,256]{2,1,0:T(8,128)(2,1)S(1)} %collective-permute-done.2.r3_ref), channel_id=1, source_target_pairs={{0,1},{1,0},{2,3},{3,2},{4,5},{5,4},{6,7},{7,6},{8,9},{9,8},{10,11... | collective-permute-start | bytes 196616 | tf_op jit(solution)/shard_map/ppermute | solution.py:18
  14.8 10.3 %collective-permute-start.3 = (bf16[2,64,256]{2,1,0:T(8,128)(2,1)S(1)}, bf16[2,64,256]{2,1,0:T(8,128)(2,1)S(1)}, u32[]{:S(2)}, u32[]{:S(2)}) collective-permute-start(bf16[2,64,256]{2,1,0:T(8,128)(2,1)S(1)} %collective-permute-done.r1_ref), channel_id=1, source_target_pairs={{0,1},{1,0},{2,3},{3,2},{4,5},{5,4},{6,7},{7,6},{8,9},{9,8},{10,11... | collective-permute-start | bytes 196616 | tf_op jit(solution)/shard_map/ppermute | solution.py:18
  14.8 1.5 %collective-permute-start.7 = (bf16[32]{0:T(256)(128)(2,1)}, bf16[32]{0:T(256)(128)(2,1)S(1)}, u32[]{:S(2)}, u32[]{:S(2)}) collective-permute-start(bf16[32]{0:T(256)(128)(2,1)} %param.18), channel_id=1, source_target_pairs={{0,1},{1,0},{2,3},{3,2},{4,5},{5,4},{6,7},{7,6},{8,9},{9,8},{10,11... | collective-permute-start | bytes 200 | tf_op jit(solution)/shard_map/ppermute | solution.py:18
  16.3 1.3 %collective-permute-start.8 = (bf16[32]{0:T(256)(128)(2,1)}, bf16[32]{0:T(256)(128)(2,1)S(1)}, u32[]{:S(2)}, u32[]{:S(2)}) collective-permute-start(bf16[32]{0:T(256)(128)(2,1)} %param.19), channel_id=1, source_target_pairs={{0,1},{1,0},{2,3},{3,2},{4,5},{5,4},{6,7},{7,6},{8,9},{9,8},{10,11... | collective-permute-start | bytes 200 | tf_op jit(solution)/shard_map/ppermute | solution.py:18
  17.6 1.4 %collective-permute-start.9 = (bf16[2,256]{1,0:T(2,128)(2,1)}, bf16[2,256]{1,0:T(2,128)(2,1)S(1)}, u32[]{:S(2)}, u32[]{:S(2)}) collective-permute-start(bf16[2,256]{1,0:T(2,128)(2,1)} %cb_own_ref.1), channel_id=1, source_target_pairs={{0,1},{1,0},{2,3},{3,2},{4,5},{5,4},{6,7},{7,6},{8,9},{9,8},{10,11... | collective-permute-start | bytes 3080 | tf_op jit(solution)/shard_map/ppermute | solution.py:18
  18.9 1.5 %collective-permute-start.6 = (bf16[3,3,32,64]{3,2,1,0:T(8,128)(2,1)}, bf16[3,3,32,64]{3,2,1,0:T(8,128)(2,1)S(1)}, u32[]{:S(2)}, u32[]{:S(2)}) collective-permute-start(bf16[3,3,32,64]{3,2,1,0:T(8,128)(2,1)} %mw_own_ref.1), channel_id=1, source_target_pairs={{0,1},{1,0},{2,3},{3,2},{4,5},{5,4},{6,7},{7,6},{8,9},{9,8},{10,11... | collective-permute-start | bytes 110600 | tf_op jit(solution)/shard_map/ppermute | solution.py:18
  20.4 0.9 %copy-start.2 = (bf16[3,3,32,64]{3,2,1,0:T(8,128)(2,1)S(1)}, bf16[3,3,32,64]{3,2,1,0:T(8,128)(2,1)}, u32[]{:S(2)}) copy-start(bf16[3,3,32,64]{3,2,1,0:T(8,128)(2,1)} %mw_own_ref.1) | copy-start | bytes 110596
  21.3 0.7 %copy-start.3 = (s32[8,4]{0,1:T(4,128)S(1)}, s32[8,4]{0,1:T(4,128)}, u32[]{:S(2)}) copy-start(s32[8,4]{0,1:T(4,128)} %param.12) | copy-start | bytes 388
  22.0 0.7 %copy-start.4 = (bf16[2,256]{1,0:T(2,128)(2,1)S(1)}, bf16[2,256]{1,0:T(2,128)(2,1)}, u32[]{:S(2)}) copy-start(bf16[2,256]{1,0:T(2,128)(2,1)} %cb_own_ref.1) | copy-start | bytes 3076
  22.6 0.7 %copy-start.5 = (bf16[32]{0:T(256)(128)(2,1)S(1)}, bf16[32]{0:T(256)(128)(2,1)}, u32[]{:S(2)}) copy-start(bf16[32]{0:T(256)(128)(2,1)} %param.18) | copy-start | bytes 196
  23.3 0.7 %copy-start.6 = (bf16[32]{0:T(256)(128)(2,1)S(1)}, bf16[32]{0:T(256)(128)(2,1)}, u32[]{:S(2)}) copy-start(bf16[32]{0:T(256)(128)(2,1)} %param.19) | copy-start | bytes 196
  24.0 0.7 %copy-start.7 = (bf16[128]{0:T(256)(128)(2,1)S(1)}, bf16[128]{0:T(256)(128)(2,1)}, u32[]{:S(2)}) copy-start(bf16[128]{0:T(256)(128)(2,1)} %param.16) | copy-start | bytes 772
  25.2 1.4 %copy-start = (bf16[2,3,512,256]{3,2,1,0:T(8,128)(2,1)S(1)}, bf16[2,3,512,256]{3,2,1,0:T(8,128)(2,1)}, u32[]{:S(2)}) copy-start(bf16[2,3,512,256]{3,2,1,0:T(8,128)(2,1)} %w_own_ref.1) | copy-start | bytes 4718596
  26.6 0.9 %copy-start.1 = (bf16[512,128]{1,0:T(8,128)(2,1)S(1)}, bf16[512,128]{1,0:T(8,128)(2,1)}, u32[]{:S(2)}) copy-start(bf16[512,128]{1,0:T(8,128)(2,1)} %pw_ref.1) | copy-start | bytes 393220
where the time goes:
time: 32.2 us; the launch traced here: 32 us
  starting transfers between devices  8.69 us (27%)
  waiting for transfers between devices  7.76 us (24%)
  local copies, waits for them, and re-layouts  6.51 us (20%)
  Pallas kernels  4.98 us (15%)
  blocking collectives  3.3 us (10%)
  between operations  0.72 us (2%)
    ppermute x3, starting transfers between devices, blk_permute(): return lax.ppermute(value, ('blk', 'chan'), pairs)  6.82 us
    unnamed x16, local copies, waits for them, and re-layouts  6.51 us
    pallas_call x1, Pallas kernels, local(): pl.pallas_call(contact_kernel, out_shape=jax.ShapeDtypeStruct((bins, 2 *...  4.45 us
    ppermute x3, waiting for transfers between devices, blk_permute(): return lax.ppermute(value, ('blk', 'chan'), pairs)  4.28 us
    ppermute x7, waiting for transfers between devices, chan_swap(): return lax.ppermute(value, 'chan', [(0, 1), (1, 0)])  3.48 us
    all_gather x1, blocking collectives, local(): own = lax.all_gather(features, 'chan', axis=0)  3.3 us
    ppermute x7, starting transfers between devices, chan_swap(): return lax.ppermute(value, 'chan', [(0, 1), (1, 0)])  1.87 us
  transfers between devices with their start and end apart: 10, of which 5 were waited for; matrix products, arithmetic and copies ran while one was open for 0% of the time, Pallas kernels for 2%

commit v1 on v0

--- a/solution.py
+++ b/solution.py
@@ -27,78 +27,85 @@
     return lax.ppermute(value, ("blk", "chan"), pairs)
 
 
-def prep_kernel(
-    length_ref,
-    mask_ref,
-    mw_own_ref,
-    mw_oth_ref,
-    mb_own_ref,
-    mb_oth_ref,
-    hw_own_ref,
-    hw_oth_ref,
-    cb_own_ref,
-    cb_oth_ref,
-    pb_ref,
-    wbig_ref,
+def pack_kernel(
+    own_any,
+    length_any,
+    mask_any,
+    mw_any,
+    mb_any,
+    hw_any,
+    cb_any,
+    pb_any,
+    w_any,
+    pw_any,
+    packed_ref,
     col_mask_ref,
     valid_ref,
     small_ref,
-    head_ref,
-    wt_s,
-    taps_s,
+    w_ref,
+    pw_ref,
+    length_s,
+    mask_s,
+    mw_s,
+    mb_s,
+    hw_s,
+    cb_s,
+    pb_s,
+    extra_s,
+    sems,
 ):
+    pairs = (
+        (length_any, length_s),
+        (mask_any, mask_s),
+        (mw_any, mw_s),
+        (mb_any, mb_s),
+        (hw_any, hw_s),
+        (cb_any, cb_s),
+        (pb_any, pb_s),
+        (w_any, w_ref),
+        (pw_any, pw_ref),
+    )
+    copies = [
+        pltpu.make_async_copy(source, target, sems.at[at])
+        for at, (source, target) in enumerate(pairs)
+    ]
+    for copy in copies:
+        copy.start()
+    for copy in copies[:7]:
+        copy.wait()
+
     rows = valid_ref.shape[0]
     columns = col_mask_ref.shape[1]
     bins = columns // 2
-    half = mw_own_ref.shape[2]
+    half = mw_any.shape[2]
     col_rows = columns + 2 * HALO
     count = lax.axis_size("blk")
     i = lax.axis_index("blk")
     c = lax.axis_index("chan")
     first = i * bins
     first_col = first + c * columns
-    length = length_ref[...]
-
-    for source, side in ((mw_own_ref, c), (mw_oth_ref, 1 - c)):
-        at = pl.ds(pl.multiple_of(side * half, half), half)
-        for s in range(3):
-            for r in range(3):
-                taps_s[3 * s + r, at, :] = source[s, r].astype(F32)
-    blank = jnp.zeros((F2, F2), F32)
-    for j in range(4):
-        pieces = []
-        for m in range(6):
-            for r in range(3):
-                pieces.append(taps_s[3 * (m - j) + r] if 0 <= m - j < 3 else blank)
-        for tile in range(9):
-            wt_s[j * F2 : (j + 1) * F2, tile * 2 * F2 : (tile + 1) * 2 * F2] = jnp.concatenate(
-                pieces[2 * tile : 2 * tile + 2], axis=1
-            )
-    wbig_ref[...] = wt_s[...].T.astype(BF16)
-
-    def spread(own_ref, oth_ref, repeats):
-        o = lax.broadcasted_iota(jnp.int32, (half, repeats * F2), 0)
-        lane = lax.broadcasted_iota(jnp.int32, (half, repeats * F2), 1) % F2
-        total = jnp.zeros((16, repeats * F2), F32)
-        for ref, side in ((own_ref, c), (oth_ref, 1 - c)):
-            pick = (lane == side * half + o).astype(BF16)
-            value = jnp.broadcast_to(ref[...], (16, half)).astype(BF16)
-            total = total + jnp.dot(value, pick, preferred_element_type=F32)
-        return total
-
-    head_all = spread(hw_own_ref, hw_oth_ref, 8)
-    q = lax.broadcasted_iota(jnp.int32, (16, 8 * F2), 0)
-    k = lax.broadcasted_iota(jnp.int32, (16, 8 * F2), 1)
-    head_ref[...] = jnp.where(
-        q == 2 * ((k % (4 * F2)) // F2) + k // (4 * F2), head_all, 0.0
-    ).astype(BF16)
-    bias_all = spread(mb_own_ref, mb_oth_ref, 4)
+    length = length_s[...]
+
+    extra_s[...] = jnp.zeros_like(extra_s)
+    biases = cb_s[...].astype(F32)
+    for layer in range(CONV1):
+        for quarter in range(4):
+            at = 4 * layer + quarter
+            extra_s[at : at + 1, :F2] = biases[layer : layer + 1, quarter * F2 : (quarter + 1) * F2]
+    extra_s[8:9, :half] = mb_s[...].astype(F32)
+    extra_s[9:10, :half] = hw_s[...].astype(F32)
+    extra = pltpu.roll(extra_s[...], F2, axis=1)
+    for s in range(3):
+        for r in range(3):
+            at = (3 * s + r) * half
+            packed_ref[at : at + half, :F2] = mw_s[s, r]
+    packed_ref[:32, F2:] = extra[:, F2:].astype(BF16)
 
     minus = F32(-jnp.inf)
     block = lax.broadcasted_iota(jnp.int32, (BAND + 1, count), 1)
 
     def live_at(y, variant):
-        at_row = jnp.sum(jnp.where(block == i + variant, mask_ref[...], 0), axis=1, keepdims=True)
+        at_row = jnp.sum(jnp.where(block == i + variant, mask_s[...], 0), axis=1, keepdims=True)
         offset = lax.broadcasted_iota(jnp.int32, (BAND + 1, 1), 0)
 
         def entry(u):
@@ -133,13 +140,60 @@
     )
     valid_ref[...] = jnp.where((bin_index >= 0) & (bin_index < length), 1.0, 0.0)
 
-    small_ref[0:2, :] = cb_own_ref[...].astype(F32)
-    small_ref[2:4, :] = cb_oth_ref[...].astype(F32)
-    small_ref[4:5, :] = bias_all[:1]
-    small_ref[5:6, : 2 * F2] = pb_ref[...].astype(F32)
-    small_ref[5:6, 2 * F2 :] = jnp.where(
+    small_ref[0:2, :] = cb_s[...].astype(F32)
+    small_ref[2:3, : 2 * F2] = pb_s[...].astype(F32)
+    small_ref[2:3, 2 * F2 :] = jnp.where(
         live_at(lax.broadcasted_iota(jnp.int32, (1, columns), 1), 0), 1.0, 0.0
     )
+    for copy in copies[7:]:
+        copy.wait()
+
+
+def prep_kernel(own_ref, oth_ref, wbig_ref, side_ref, head_ref, wt_s, taps_s):
+    half = own_ref.shape[0] // 9
+    c = lax.axis_index("chan")
+
+    for source, side in ((own_ref, c), (oth_ref, 1 - c)):
+        at = pl.ds(pl.multiple_of(side * half, half), half)
+        for tap in range(9):
+            taps_s[tap, at, :] = source[tap * half : (tap + 1) * half, :F2].astype(F32)
+    blank = jnp.zeros((F2, F2), F32)
+    for j in range(4):
+        pieces = []
+        for m in range(6):
+            for r in range(3):
+                pieces.append(taps_s[3 * (m - j) + r] if 0 <= m - j < 3 else blank)
+        for tile in range(9):
+            wt_s[j * F2 : (j + 1) * F2, tile * 2 * F2 : (tile + 1) * 2 * F2] = jnp.concatenate(
+                pieces[2 * tile : 2 * tile + 2], axis=1
+            )
+    wbig_ref[...] = wt_s[...].T.astype(BF16)
+
+    def spread(row, repeats):
+        o = lax.broadcasted_iota(jnp.int32, (2 * F2, repeats * F2), 0)
+        lane = lax.broadcasted_iota(jnp.int32, (2 * F2, repeats * F2), 1) % F2
+        total = jnp.zeros((16, repeats * F2), F32)
+        for ref, side in ((own_ref, c), (oth_ref, 1 - c)):
+            pick = ((lane == side * half + o - F2) & (o >= F2) & (o < F2 + half)).astype(BF16)
+            value = ref[:16, :].astype(F32)[row : row + 1]
+            value = jnp.broadcast_to(value, (16, 2 * F2)).astype(BF16)
+            total = total + jnp.dot(value, pick, preferred_element_type=F32)
+        return total
+
+    q = lax.broadcasted_iota(jnp.int32, (16, 8 * F2), 0)
+    k = lax.broadcasted_iota(jnp.int32, (16, 8 * F2), 1)
+    head_ref[...] = jnp.where(
+        q == 2 * ((k % (4 * F2)) // F2) + k // (4 * F2), spread(9, 8), 0.0
+    ).astype(BF16)
+    side_ref[0:1, :] = spread(8, 4)[:1]
+    other = oth_ref[:16, :].astype(F32)
+    other = pltpu.roll(other, F2, axis=1)
+    for layer in range(CONV1):
+        for quarter in range(4):
+            at = 4 * layer + quarter
+            side_ref[1 + layer : 2 + layer, quarter * F2 : (quarter + 1) * F2] = other[
+                at : at + 1, :F2
+            ]
 
 
 def contact_kernel(
@@ -152,10 +206,11 @@
     w_own_ref,
     w_oth_ref,
     pw_ref,
-    wbig_ref,
     col_mask_ref,
     valid_ref,
     small_ref,
+    wbig_ref,
+    side_ref,
     head_ref,
     out_ref,
     h_s,
@@ -220,12 +275,12 @@
             q = q + jnp.dot(taps[1], w_ref[layer, 1], preferred_element_type=F32)
             q = q + jnp.dot(taps[2], w_ref[layer, 2], preferred_element_type=F32)
             lanes = pl.ds(pl.multiple_of(side * half, half), half)
-            bias = small_ref[2 * at + layer : 2 * at + layer + 1, :]
+            bias = side_ref[1 + layer : 2 + layer, :] if at else small_ref[layer : layer + 1, :]
             new = (h_s[:, lanes] + jnp.maximum(q + bias, 0.0)).astype(BF16).astype(F32)
             h_s[:, lanes] = jnp.where(inside, new, 0.0)
 
     proj = jnp.dot(h_s[...].astype(BF16), pw_ref[...], preferred_element_type=F32)
-    proj = (proj + small_ref[5:6, : 2 * F2]).astype(BF16).astype(F32)
+    proj = (proj + small_ref[2:3, : 2 * F2]).astype(BF16).astype(F32)
 
     minus = F32(-jnp.inf)
     low = lax.broadcasted_iota(jnp.int32, (1, 2 * F2), 1) < F2
@@ -257,7 +312,7 @@
     groups = bins // 8
     per_dot = x_s.shape[0] // (2 * bins)
     zero = jnp.zeros((), BF16)
-    bias4 = small_ref[4:5, :]
+    bias4 = side_ref[0:1, :]
     for v in range(2):
         for start in range(0, groups, per_dot):
             for slot in range(2 * start, 2 * (start + per_dot) + 1):
@@ -285,7 +340,7 @@
                 mixed = y[at_row : at_row + 2 * bins] + centre
                 mix_s[group, :, v * 4 * F2 : (v + 1) * 4 * F2] = mixed.astype(BF16)
 
-    lane_live = small_ref[5:6, 2 * F2 :] != 0
+    lane_live = small_ref[2:3, 2 * F2 :] != 0
     for group in range(groups):
         value = lax.dot_general(
             head_ref[...], mix_s[group], (((1,), (1,)), ((), ())), preferred_element_type=F32
@@ -318,41 +373,65 @@
     w_oth = chan_swap(conv_weight)
 
     rows = 3 * bins + 4 * HALO
+    half_out = map_bias.shape[0]
     vmem = pl.BlockSpec(memory_space=pltpu.VMEM)
+    anywhere = pl.BlockSpec(memory_space=pl.ANY)
     params = pltpu.CompilerParams(vmem_limit_bytes=24 * 1024 * 1024)
+    packed, col_mask, valid, small, w_own, pw = pl.pallas_call(
+        pack_kernel,
+        out_shape=[
+            jax.ShapeDtypeStruct((9 * half_out, 2 * F2), BF16),
+            jax.ShapeDtypeStruct((3, 2 * bins, 6 * F2), F32),
+            jax.ShapeDtypeStruct((rows, 2 * F2), F32),
+            jax.ShapeDtypeStruct((8, half), F32),
+            jax.ShapeDtypeStruct(conv_weight.shape, BF16),
+            jax.ShapeDtypeStruct(proj_weight.shape, BF16),
+        ],
+        in_specs=[anywhere] * 10,
+        out_specs=[vmem] * 6,
+        scratch_shapes=[
+            pltpu.VMEM((1, 1), jnp.int32),
+            pltpu.VMEM(band_mask.shape[::-1], jnp.int32),
+            pltpu.VMEM(map_weight.shape, BF16),
+            pltpu.VMEM((1, half_out), BF16),
+            pltpu.VMEM((1, half_out), BF16),
+            pltpu.VMEM(conv_bias.shape, BF16),
+            pltpu.VMEM((1, 2 * F2), BF16),
+            pltpu.VMEM((32, 2 * F2), F32),
+            pltpu.SemaphoreType.DMA((9,)),
+        ],
+        compiler_params=params,
+    )(
+        own,
+        chrom_len[None],
+        band_mask.T,
+        map_weight,
+        map_bias[None],
+        head_weight[None],
+        conv_bias,
+        proj_bias[None],
+        conv_weight,
+        proj_weight,
+    )
     prepared = pl.pallas_call(
         prep_kernel,
         out_shape=[
             jax.ShapeDtypeStruct((18 * F2, 4 * F2), BF16),
-            jax.ShapeDtypeStruct((3, 2 * bins, 6 * F2), F32),
-            jax.ShapeDtypeStruct((rows, 2 * F2), F32),
             jax.ShapeDtypeStruct((8, half), F32),
             jax.ShapeDtypeStruct((16, 8 * F2), BF16),
         ],
-        in_specs=[vmem] * 11,
-        out_specs=[vmem] * 5,
+        in_specs=[vmem] * 2,
+        out_specs=[vmem] * 3,
         scratch_shapes=[
             pltpu.VMEM((4 * F2, 18 * F2), F32),
             pltpu.VMEM((9, F2, F2), F32),
         ],
         compiler_params=params,
-    )(
-        chrom_len[None],
-        band_mask.T,
-        map_weight,
-        chan_swap(map_weight),
-        map_bias[None],
-        chan_swap(map_bias)[None],
-        head_weight[None],
-        chan_swap(head_weight)[None],
-        conv_bias,
-        chan_swap(conv_bias),
-        proj_bias[None],
-    )
+    )(packed, chan_swap(packed))
     return pl.pallas_call(
         contact_kernel,
         out_shape=jax.ShapeDtypeStruct((bins, 2 * bins), F32),
-        in_specs=[vmem] * 14,
+        in_specs=[vmem] * 15,
         out_specs=vmem,
         scratch_shapes=[
             pltpu.VMEM((rows, 2 * half), F32),
@@ -361,7 +440,7 @@
             pltpu.VMEM((bins // 8, 2 * bins, 8 * F2), BF16),
         ],
         compiler_params=params,
-    )(own, r1, r2, r3, s1, s3, conv_weight, w_oth, proj_weight, *prepared)
+    )(own, r1, r2, r3, s1, s3, w_own, w_oth, pw, col_mask, valid, small, *prepared)
 
 
 def solution(mesh):

time: 32.2 us -> 26.4 us (0.82)
  waiting for transfers between devices: 7.76 us -> 2.29 us
  starting transfers between devices: 8.69 us -> 7.91 us
  Pallas kernels: 4.98 us -> 5.46 us
    ppermute x7 -> x4, waiting for transfers between devices: 3.48 us -> 0.01 us  [chan_swap(): return lax.ppermute(value, 'chan', [(0, 1), (1, 0)])]
    ppermute x3, waiting for transfers between devices: 4.28 us -> 2.28 us  [blk_permute(): return lax.ppermute(value, ('blk', 'chan'), pairs)]
    pallas_call x0 -> x1, Pallas kernels: none -> 0.72 us  [local(): pl.pallas_call(pack_kernel, out_shape=[jax.ShapeDtypeStruct((9 * half_out...]
    ppermute x7 -> x4, starting transfers between devices: 1.87 us -> 1.32 us  [chan_swap(): return lax.ppermute(value, 'chan', [(0, 1), (1, 0)])]
  transfers between devices with their start and end apart: 10 -> 7, of which waited for: 5 -> 1; matrix products, arithmetic and copies ran while one was open for 0% -> 0% of each run, Pallas kernels for 2% -> 4%
where the time goes in v1:
time: 26.4 us; the launch traced here: 26.2 us
  starting transfers between devices  7.91 us (30%)
  local copies, waits for them, and re-layouts  6.51 us (25%)
  Pallas kernels  5.46 us (21%)
  blocking collectives  3.3 us (12%)
  waiting for transfers between devices  2.29 us (9%)
  between operations  0.69 us (3%)
    ppermute x3, starting transfers between devices, blk_permute(): return lax.ppermute(value, ('blk', 'chan'), pairs)  6.6 us
    unnamed x16, local copies, waits for them, and re-layouts  6.51 us
    pallas_call x1, Pallas kernels, local(): pl.pallas_call(contact_kernel, out_shape=jax.ShapeDtypeStruct((bins, 2 *...  4.4 us
    all_gather x1, blocking collectives, local(): own = lax.all_gather(features, 'chan', axis=0)  3.3 us
    ppermute x3, waiting for transfers between devices, blk_permute(): return lax.ppermute(value, ('blk', 'chan'), pairs)  2.28 us
    ppermute x4, starting transfers between devices, chan_swap(): return lax.ppermute(value, 'chan', [(0, 1), (1, 0)])  1.32 us
    pallas_call x1, Pallas kernels, local(): pl.pallas_call(pack_kernel, out_shape=[jax.ShapeDtypeStruct((9 * half_out...  0.72 us
  transfers between devices with their start and end apart: 7, of which 1 were waited for; matrix products, arithmetic and copies ran while one was open for 0% of the time, Pallas kernels for 4%

profile of v1, /device:TPU:0, one launch (start us, length us, event | category | flops | bytes accessed | tf_op | source)
XLA Modules:
  0.0 26.2 jit_solution(9532653181986127103)
XLA Ops:
  0.0 0.5 %collective-permute-start.5 = (bf16[2,3,512,256]{3,2,1,0:T(8,128)(2,1)}, bf16[2,3,512,256]{3,2,1,0:T(8,128)(2,1)S(1)}, u32[]{:S(2)}, u32[]{:S(2)}) collective-permute-start(bf16[2,3,512,256]{3,2,1,0:T(8,128)(2,1)} %w_any.1), channel_id=1, source_target_pairs={{0,1},{1,0},{2,3},{3,2},{4,5},{5,4},{6,7},{7,6},{8,9},{9,8},{10,11... | collective-permute-start | bytes 4718600 | tf_op jit(solution)/shard_map/ppermute | solution.py:18
  0.5 3.3 %all-gather = bf16[128,256]{1,0:T(8,128)(2,1)S(1)} all-gather(bf16[64,256]{1,0:T(8,128)(2,1)} %param.10), channel_id=2, replica_groups=mesh['dp'=2,'blk'=8,'chan'=2] {'chan'}, dimensions={0}, use_global_device_ids=true | all-gather | bytes 98304 | tf_op jit(solution)/shard_map/all_gather | solution.py:367
  3.7 2.9 %collective-permute-start = (bf16[2,64,256]{2,1,0:T(8,128)(2,1)S(1)}, bf16[2,64,256]{2,1,0:T(8,128)(2,1)S(1)}, u32[]{:S(2)}, u32[]{:S(2)}) collective-permute-start(bf16[2,64,256]{2,1,0:T(8,128)(2,1)S(1)} %bitcast.7), channel_id=1, source_target_pairs={{14,0},{3,1},{0,2},{5,3},{2,4},{7,5},{4,6},{9,7},{6,8},{11,9},{8,1... | collective-permute-start | bytes 196616 | tf_op jit(solution)/shard_map/ppermute | solution.py:27
  6.6 2.6 %collective-permute-start.2 = (bf16[2,64,256]{2,1,0:T(8,128)(2,1)S(1)}, bf16[2,64,256]{2,1,0:T(8,128)(2,1)S(1)}, u32[]{:S(2)}, u32[]{:S(2)}) collective-permute-start(bf16[2,64,256]{2,1,0:T(8,128)(2,1)S(1)} %bitcast.8), channel_id=1, source_target_pairs={{8,0},{7,1},{10,2},{9,3},{12,4},{11,5},{14,6},{13,7},{0,8},{15,9},... | collective-permute-start | bytes 196616 | tf_op jit(solution)/shard_map/ppermute | solution.py:27
  9.9 0.0 copy-start
  9.9 1.4 %copy-done = bf16[2,3,512,256]{3,2,1,0:T(8,128)(2,1)S(1)} copy-done((bf16[2,3,512,256]{3,2,1,0:T(8,128)(2,1)S(1)}, bf16[2,3,512,256]{3,2,1,0:T(8,128)(2,1)}, u32[]{:S(2)}) %copy-start) | copy-done | bytes 1572888
  11.3 0.0 copy-start.1
  11.3 0.9 %copy-done.1 = bf16[512,128]{1,0:T(8,128)(2,1)S(1)} copy-done((bf16[512,128]{1,0:T(8,128)(2,1)S(1)}, bf16[512,128]{1,0:T(8,128)(2,1)}, u32[]{:S(2)}) %copy-start.1) | copy-done | bytes 131096
  12.2 0.0 copy-start.2
  12.2 0.9 %copy-done.2 = bf16[3,3,32,64]{3,2,1,0:T(8,128)(2,1)S(1)} copy-done((bf16[3,3,32,64]{3,2,1,0:T(8,128)(2,1)S(1)}, bf16[3,3,32,64]{3,2,1,0:T(8,128)(2,1)}, u32[]{:S(2)}) %copy-start.2) | copy-done | bytes 36888
  13.1 0.0 copy-start.3
  13.1 0.7 %copy-done.3 = s32[8,4]{0,1:T(4,128)S(1)} copy-done((s32[8,4]{0,1:T(4,128)S(1)}, s32[8,4]{0,1:T(4,128)}, u32[]{:S(2)}) %copy-start.3) | copy-done | bytes 152
  13.8 0.0 copy-start.4
  13.8 0.7 %copy-done.4 = bf16[2,256]{1,0:T(2,128)(2,1)S(1)} copy-done((bf16[2,256]{1,0:T(2,128)(2,1)S(1)}, bf16[2,256]{1,0:T(2,128)(2,1)}, u32[]{:S(2)}) %copy-start.4) | copy-done | bytes 1048
  14.4 0.0 copy-start.5
  14.4 0.7 %copy-done.5 = bf16[32]{0:T(256)(128)(2,1)S(1)} copy-done((bf16[32]{0:T(256)(128)(2,1)S(1)}, bf16[32]{0:T(256)(128)(2,1)}, u32[]{:S(2)}) %copy-start.5) | copy-done | bytes 88
  15.1 0.0 copy-start.6
  15.1 0.7 %copy-done.6 = bf16[32]{0:T(256)(128)(2,1)S(1)} copy-done((bf16[32]{0:T(256)(128)(2,1)S(1)}, bf16[32]{0:T(256)(128)(2,1)}, u32[]{:S(2)}) %copy-start.6) | copy-done | bytes 88
  15.7 0.0 copy-start.7
  15.7 0.7 %copy-done.7 = bf16[128]{0:T(256)(128)(2,1)S(1)} copy-done((bf16[128]{0:T(256)(128)(2,1)S(1)}, bf16[128]{0:T(256)(128)(2,1)}, u32[]{:S(2)}) %copy-start.7) | copy-done | bytes 280
  16.4 0.7 %shard_map.100 = (bf16[288,128]{1,0:T(8,128)(2,1)S(1)}, f32[3,128,384]{2,1,0:T(8,128)S(1)}, f32[256,128]{1,0:T(8,128)S(1)}, f32[8,256]{1,0:T(8,128)S(1)}, bf16[2...) custom-call(bf16[2,64,256]{2,1,0:T(8,128)(2,1)S(1)} %bitcast.9, s32[1,1]{1,0:T(1,128)} %bitcast.6.length_any, ...), custom_call_target="tpu_custom_call" | custom-call | tf_op jit(solution)/shard_map/pallas_call | solution.py:380
  17.1 0.4 %collective-permute-start.6 = (bf16[288,128]{1,0:T(8,128)(2,1)S(1)}, bf16[288,128]{1,0:T(8,128)(2,1)S(1)}, u32[]{:S(2)}, u32[]{:S(2)}) collective-permute-start(bf16[288,128]{1,0:T(8,128)(2,1)S(1)} %get-tuple-element.19.own_ref), channel_id=1, source_target_pairs={{0,1},{1,0},{2,3},{3,2},{4,5},{5,4},{6,7},{7,6},{8,9},{9,8},{10,11... | collective-permute-start | bytes 221192 | tf_op jit(solution)/shard_map/ppermute | solution.py:18
  17.5 1.1 %collective-permute-start.1 = (bf16[2,64,256]{2,1,0:T(8,128)(2,1)S(1)}, bf16[2,64,256]{2,1,0:T(8,128)(2,1)S(1)}, u32[]{:S(2)}, u32[]{:S(2)}) collective-permute-start(bf16[2,64,256]{2,1,0:T(8,128)(2,1)S(1)} %bitcast.10), channel_id=1, source_target_pairs={{4,0},{5,1},{6,2},{7,3},{8,4},{9,5},{10,6},{11,7},{12,8},{13,9},{1... | collective-permute-start | bytes 196616 | tf_op jit(solution)/shard_map/ppermute | solution.py:27
  18.6 0.0 collective-permute-done.r1_ref
  18.6 0.2 collective-permute-start.3
  18.8 0.0 collective-permute-done.2.r3_ref
  18.8 0.3 %collective-permute-start.4 = (bf16[2,64,256]{2,1,0:T(8,128)(2,1)S(1)}, bf16[2,64,256]{2,1,0:T(8,128)(2,1)S(1)}, u32[]{:S(2)}, u32[]{:S(2)}) collective-permute-start(bf16[2,64,256]{2,1,0:T(8,128)(2,1)S(1)} %collective-permute-done.2.r3_ref), channel_id=1, source_target_pairs={{0,1},{1,0},{2,3},{3,2},{4,5},{5,4},{6,7},{7,6},{8,9},{9,8},{10,11... | collective-permute-start | bytes 196616 | tf_op jit(solution)/shard_map/ppermute | solution.py:18
  19.1 0.0 collective-permute-done.6.oth_ref
  19.1 0.3 %shard_map.101 = (bf16[1152,256]{1,0:T(8,128)(2,1)S(1)}, f32[8,256]{1,0:T(8,128)S(1)}, bf16[16,512]{1,0:T(8,128)(2,1)S(1)}) custom-call(bf16[288,128]{1,0:T(8,128)(2,1)S(1)} %get-tuple-element.19.own_ref, bf16[288,128]{1,0:T(8,128)(2,1)S(1)} %collective-permute-done.6.oth_ref), custom_call_target="tpu_custom_call" | custom-call | tf_op jit(solution)/shard_map/pallas_call | solution.py:416
  19.5 2.3 %collective-permute-done.1.r2_ref = bf16[2,64,256]{2,1,0:T(8,128)(2,1)S(1)} collective-permute-done((bf16[2,64,256]{2,1,0:T(8,128)(2,1)S(1)}, bf16[2,64,256]{2,1,0:T(8,128)(2,1)S(1)}, u32[]{:S(2)}, u32[]{:S(2)}) %collective-permute-start.1) | collective-permute-done | bytes 65568 | tf_op jit(solution)/shard_map/ppermute | solution.py:27
  21.7 0.0 collective-permute-done.3.s1_ref
  21.8 0.0 collective-permute-done.4.s3_ref
  21.8 0.0 collective-permute-done.5.w_oth_ref
  21.8 4.4 %shard_map.102 = f32[64,128]{1,0:T(8,128)} custom-call(bf16[2,64,256]{2,1,0:T(8,128)(2,1)S(1)} %bitcast.11, bf16[2,64,256]{2,1,0:T(8,128)(2,1)S(1)} %collective-permute-done.r1_ref, bf16[2,64,256]{2,1,0:T(8,128)(2,1)S(1)} %collective-permute-done.1.r2_ref, bf16[2,64,256]{2,1,0:T(8,128)(2,1)S(1)} %collective-permute-done.2.r3_ref, ...), custom_call_target="tpu_custom_call" | custom-call | tf_op jit(solution)/shard_map/pallas_call | solution.py:431
Async XLA Ops:
  0.0 21.8 %collective-permute-start.5 = (bf16[2,3,512,256]{3,2,1,0:T(8,128)(2,1)}, bf16[2,3,512,256]{3,2,1,0:T(8,128)(2,1)S(1)}, u32[]{:S(2)}, u32[]{:S(2)}) collective-permute-start(bf16[2,3,512,256]{3,2,1,0:T(8,128)(2,1)} %w_any.1), channel_id=1, source_target_pairs={{0,1},{1,0},{2,3},{3,2},{4,5},{5,4},{6,7},{7,6},{8,9},{9,8},{10,11... | collective-permute-start | bytes 4718600 | tf_op jit(solution)/shard_map/ppermute | solution.py:18
  3.7 14.9 %collective-permute-start = (bf16[2,64,256]{2,1,0:T(8,128)(2,1)S(1)}, bf16[2,64,256]{2,1,0:T(8,128)(2,1)S(1)}, u32[]{:S(2)}, u32[]{:S(2)}) collective-permute-start(bf16[2,64,256]{2,1,0:T(8,128)(2,1)S(1)} %bitcast.7), channel_id=1, source_target_pairs={{14,0},{3,1},{0,2},{5,3},{2,4},{7,5},{4,6},{9,7},{6,8},{11,9},{8,1... | collective-permute-start | bytes 196616 | tf_op jit(solution)/shard_map/ppermute | solution.py:27
  6.6 12.2 %collective-permute-start.2 = (bf16[2,64,256]{2,1,0:T(8,128)(2,1)S(1)}, bf16[2,64,256]{2,1,0:T(8,128)(2,1)S(1)}, u32[]{:S(2)}, u32[]{:S(2)}) collective-permute-start(bf16[2,64,256]{2,1,0:T(8,128)(2,1)S(1)} %bitcast.8), channel_id=1, source_target_pairs={{8,0},{7,1},{10,2},{9,3},{12,4},{11,5},{14,6},{13,7},{0,8},{15,9},... | collective-permute-start | bytes 196616 | tf_op jit(solution)/shard_map/ppermute | solution.py:27
  9.9 1.4 %copy-start = (bf16[2,3,512,256]{3,2,1,0:T(8,128)(2,1)S(1)}, bf16[2,3,512,256]{3,2,1,0:T(8,128)(2,1)}, u32[]{:S(2)}) copy-start(bf16[2,3,512,256]{3,2,1,0:T(8,128)(2,1)} %w_any.1) | copy-start | bytes 4718596
  11.3 0.9 %copy-start.1 = (bf16[512,128]{1,0:T(8,128)(2,1)S(1)}, bf16[512,128]{1,0:T(8,128)(2,1)}, u32[]{:S(2)}) copy-start(bf16[512,128]{1,0:T(8,128)(2,1)} %pw_any.1) | copy-start | bytes 393220
  12.2 0.9 %copy-start.2 = (bf16[3,3,32,64]{3,2,1,0:T(8,128)(2,1)S(1)}, bf16[3,3,32,64]{3,2,1,0:T(8,128)(2,1)}, u32[]{:S(2)}) copy-start(bf16[3,3,32,64]{3,2,1,0:T(8,128)(2,1)} %mw_any.1) | copy-start | bytes 110596
  13.1 0.7 %copy-start.3 = (s32[8,4]{0,1:T(4,128)S(1)}, s32[8,4]{0,1:T(4,128)}, u32[]{:S(2)}) copy-start(s32[8,4]{0,1:T(4,128)} %param.12) | copy-start | bytes 388
  13.8 0.7 %copy-start.4 = (bf16[2,256]{1,0:T(2,128)(2,1)S(1)}, bf16[2,256]{1,0:T(2,128)(2,1)}, u32[]{:S(2)}) copy-start(bf16[2,256]{1,0:T(2,128)(2,1)} %cb_any.1) | copy-start | bytes 3076
  14.4 0.7 %copy-start.5 = (bf16[32]{0:T(256)(128)(2,1)S(1)}, bf16[32]{0:T(256)(128)(2,1)}, u32[]{:S(2)}) copy-start(bf16[32]{0:T(256)(128)(2,1)} %param.18) | copy-start | bytes 196
  15.1 0.7 %copy-start.6 = (bf16[32]{0:T(256)(128)(2,1)S(1)}, bf16[32]{0:T(256)(128)(2,1)}, u32[]{:S(2)}) copy-start(bf16[32]{0:T(256)(128)(2,1)} %param.19) | copy-start | bytes 196
  15.7 0.7 %copy-start.7 = (bf16[128]{0:T(256)(128)(2,1)S(1)}, bf16[128]{0:T(256)(128)(2,1)}, u32[]{:S(2)}) copy-start(bf16[128]{0:T(256)(128)(2,1)} %param.16) | copy-start | bytes 772
  17.1 2.0 %collective-permute-start.6 = (bf16[288,128]{1,0:T(8,128)(2,1)S(1)}, bf16[288,128]{1,0:T(8,128)(2,1)S(1)}, u32[]{:S(2)}, u32[]{:S(2)}) collective-permute-start(bf16[288,128]{1,0:T(8,128)(2,1)S(1)} %get-tuple-element.19.own_ref), channel_id=1, source_target_pairs={{0,1},{1,0},{2,3},{3,2},{4,5},{5,4},{6,7},{7,6},{8,9},{9,8},{10,11... | collective-permute-start | bytes 221192 | tf_op jit(solution)/shard_map/ppermute | solution.py:18
  17.5 4.3 %collective-permute-start.1 = (bf16[2,64,256]{2,1,0:T(8,128)(2,1)S(1)}, bf16[2,64,256]{2,1,0:T(8,128)(2,1)S(1)}, u32[]{:S(2)}, u32[]{:S(2)}) collective-permute-start(bf16[2,64,256]{2,1,0:T(8,128)(2,1)S(1)} %bitcast.10), channel_id=1, source_target_pairs={{4,0},{5,1},{6,2},{7,3},{8,4},{9,5},{10,6},{11,7},{12,8},{13,9},{1... | collective-permute-start | bytes 196616 | tf_op jit(solution)/shard_map/ppermute | solution.py:27
  18.6 3.1 %collective-permute-start.3 = (bf16[2,64,256]{2,1,0:T(8,128)(2,1)S(1)}, bf16[2,64,256]{2,1,0:T(8,128)(2,1)S(1)}, u32[]{:S(2)}, u32[]{:S(2)}) collective-permute-start(bf16[2,64,256]{2,1,0:T(8,128)(2,1)S(1)} %collective-permute-done.r1_ref), channel_id=1, source_target_pairs={{0,1},{1,0},{2,3},{3,2},{4,5},{5,4},{6,7},{7,6},{8,9},{9,8},{10,11... | collective-permute-start | bytes 196616 | tf_op jit(solution)/shard_map/ppermute | solution.py:18
  18.8 3.0 %collective-permute-start.4 = (bf16[2,64,256]{2,1,0:T(8,128)(2,1)S(1)}, bf16[2,64,256]{2,1,0:T(8,128)(2,1)S(1)}, u32[]{:S(2)}, u32[]{:S(2)}) collective-permute-start(bf16[2,64,256]{2,1,0:T(8,128)(2,1)S(1)} %collective-permute-done.2.r3_ref), channel_id=1, source_target_pairs={{0,1},{1,0},{2,3},{3,2},{4,5},{5,4},{6,7},{7,6},{8,9},{9,8},{10,11... | collective-permute-start | bytes 196616 | tf_op jit(solution)/shard_map/ppermute | solution.py:18

commit v2 on v1

--- a/solution.py
+++ b/solution.py
@@ -18,7 +18,7 @@
     return lax.ppermute(value, "chan", [(0, 1), (1, 0)])
 
 
-def blk_permute(value, offset_0, offset_1):
+def ring_permute(value, offset_0, offset_1):
     count = lax.axis_size("blk")
     pairs = []
     for i in range(count):
@@ -27,9 +27,18 @@
     return lax.ppermute(value, ("blk", "chan"), pairs)
 
 
+def line_permute(value, step):
+    count = lax.axis_size("blk")
+    pairs = []
+    for i in range(count):
+        pairs.append(((i - step) * 2 if i >= step else i * 2 + 1, i * 2))
+        pairs.append(((i + step) * 2 + 1 if i + step < count else i * 2, i * 2 + 1))
+    return lax.ppermute(value, ("blk", "chan"), pairs)
+
+
 def pack_kernel(
+    length_ref,
     own_any,
-    length_any,
     mask_any,
     mw_any,
     mb_any,
@@ -44,7 +53,6 @@
     small_ref,
     w_ref,
     pw_ref,
-    length_s,
     mask_s,
     mw_s,
     mb_s,
@@ -55,7 +63,6 @@
     sems,
 ):
     pairs = (
-        (length_any, length_s),
         (mask_any, mask_s),
         (mw_any, mw_s),
         (mb_any, mb_s),
@@ -71,7 +78,7 @@
     ]
     for copy in copies:
         copy.start()
-    for copy in copies[:7]:
+    for copy in copies[:6]:
         copy.wait()
 
     rows = valid_ref.shape[0]
@@ -84,7 +91,7 @@
     c = lax.axis_index("chan")
     first = i * bins
     first_col = first + c * columns
-    length = length_s[...]
+    length = length_ref[0]
 
     extra_s[...] = jnp.zeros_like(extra_s)
     biases = cb_s[...].astype(F32)
@@ -145,7 +152,7 @@
     small_ref[2:3, 2 * F2 :] = jnp.where(
         live_at(lax.broadcasted_iota(jnp.int32, (1, columns), 1), 0), 1.0, 0.0
     )
-    for copy in copies[7:]:
+    for copy in copies[6:]:
         copy.wait()
 
 
@@ -202,6 +209,7 @@
     r2_ref,
     r3_ref,
     s1_ref,
+    s2_ref,
     s3_ref,
     w_own_ref,
     w_oth_ref,
@@ -245,7 +253,7 @@
     def _():
         put(HALO, bins, own_ref, 0)
         put(HALO + bins, bins, s1_ref, 0)
-        put(HALO + 2 * bins, HALO, r2_ref, 0)
+        put(HALO + 2 * bins, HALO, s2_ref, 0)
         put(col_rows, HALO, r1_ref, tail)
         put(col_rows + HALO + bins, HALO, s1_ref, 0)
 
@@ -365,17 +373,19 @@
 ):
     bins, half = features.shape
     own = lax.all_gather(features, "chan", axis=0)
-    r2 = blk_permute(own, 2, 2)
-    r1 = blk_permute(own, -1, 1)
-    r3 = blk_permute(own, 4, 3)
+    r1 = line_permute(own, 1)
+    r2 = line_permute(own, 2)
+    r3 = ring_permute(own, 4, 3)
     s1 = chan_swap(r1)
+    s2 = chan_swap(r2)
     s3 = chan_swap(r3)
-    w_oth = chan_swap(conv_weight)
+    w_in, own = lax.optimization_barrier((conv_weight, own))
+    w_oth = chan_swap(w_in)
 
     rows = 3 * bins + 4 * HALO
     half_out = map_bias.shape[0]
     vmem = pl.BlockSpec(memory_space=pltpu.VMEM)
-    anywhere = pl.BlockSpec(memory_space=pl.ANY)
+    anywhere = pl.BlockSpec(memory_space=pltpu.HBM)
     params = pltpu.CompilerParams(vmem_limit_bytes=24 * 1024 * 1024)
     packed, col_mask, valid, small, w_own, pw = pl.pallas_call(
         pack_kernel,
@@ -387,10 +397,9 @@
             jax.ShapeDtypeStruct(conv_weight.shape, BF16),
             jax.ShapeDtypeStruct(proj_weight.shape, BF16),
         ],
-        in_specs=[anywhere] * 10,
+        in_specs=[pl.BlockSpec(memory_space=pltpu.SMEM)] + [anywhere] * 9,
         out_specs=[vmem] * 6,
         scratch_shapes=[
-            pltpu.VMEM((1, 1), jnp.int32),
             pltpu.VMEM(band_mask.shape[::-1], jnp.int32),
             pltpu.VMEM(map_weight.shape, BF16),
             pltpu.VMEM((1, half_out), BF16),
@@ -398,20 +407,25 @@
             pltpu.VMEM(conv_bias.shape, BF16),
             pltpu.VMEM((1, 2 * F2), BF16),
             pltpu.VMEM((32, 2 * F2), F32),
-            pltpu.SemaphoreType.DMA((9,)),
+            pltpu.SemaphoreType.DMA((8,)),
         ],
         compiler_params=params,
     )(
+        chrom_len,
         own,
-        chrom_len[None],
-        band_mask.T,
-        map_weight,
-        map_bias[None],
-        head_weight[None],
-        conv_bias,
-        proj_bias[None],
-        conv_weight,
-        proj_weight,
+        *[
+            pltpu.with_memory_space_constraint(value, pltpu.HBM)
+            for value in (
+                band_mask.T,
+                map_weight,
+                map_bias[None],
+                head_weight[None],
+                conv_bias,
+                proj_bias[None],
+                conv_weight,
+                proj_weight,
+            )
+        ],
     )
     prepared = pl.pallas_call(
         prep_kernel,
@@ -431,7 +445,7 @@
     return pl.pallas_call(
         contact_kernel,
         out_shape=jax.ShapeDtypeStruct((bins, 2 * bins), F32),
-        in_specs=[vmem] * 15,
+        in_specs=[vmem] * 16,
         out_specs=vmem,
         scratch_shapes=[
             pltpu.VMEM((rows, 2 * half), F32),
@@ -440,7 +454,7 @@
             pltpu.VMEM((bins // 8, 2 * bins, 8 * F2), BF16),
         ],
         compiler_params=params,
-    )(own, r1, r2, r3, s1, s3, w_own, w_oth, pw, col_mask, valid, small, *prepared)
+    )(own, r1, r2, r3, s1, s2, s3, w_own, w_oth, pw, col_mask, valid, small, *prepared)
 
 
 def solution(mesh):

time: 26.4 us -> 18.9 us (0.72)
  local copies, waits for them, and re-layouts: 6.51 us -> 0 us
  blocking collectives: 3.3 us -> 2.16 us
  Pallas kernels: 5.46 us -> 6.35 us
  waiting for transfers between devices: 2.29 us -> 1.75 us
    unnamed x16 -> x0, local copies, waits for them, and re-layouts: 6.51 us -> none
    ppermute x3, waiting for transfers between devices: 2.28 us -> 0.85 us  [the longest x1 0.84 us: ring_permute(): return lax.ppermute(value, ('blk', 'chan'), pairs)]
    all_gather x1, blocking collectives: 3.3 us -> 2.16 us  [local(): own = lax.all_gather(features, 'chan', axis=0)]
    ppermute x4 -> x5, waiting for transfers between devices: 0.01 us -> 0.91 us  [chan_swap(): return lax.ppermute(value, 'chan', [(0, 1), (1, 0)])]
    pallas_call x1, Pallas kernels: 0.72 us -> 1.61 us  [local(): pl.pallas_call(pack_kernel, out_shape=[jax.ShapeDtypeStruct((9 * half_out...]
    ppermute x4 -> x5, starting transfers between devices: 1.32 us -> 1.03 us  [chan_swap(): return lax.ppermute(value, 'chan', [(0, 1), (1, 0)])]
  transfers between devices with their start and end apart: 7 -> 8, of which waited for: 1 -> 2; matrix products, arithmetic and copies ran while one was open for 0% -> 0% of each run, Pallas kernels for 4% -> 10%
where the time goes in v2:
time: 18.9 us; the launch traced here: 18.8 us
  starting transfers between devices  7.81 us (41%)
  Pallas kernels  6.35 us (34%)
  blocking collectives  2.16 us (11%)
  waiting for transfers between devices  1.75 us (9%)
  between operations  0.69 us (4%)
    pallas_call x1, Pallas kernels, local(): pl.pallas_call(contact_kernel, out_shape=jax.ShapeDtypeStruct((bins, 2 *...  4.39 us
    ppermute x2, starting transfers between devices, line_permute(): return lax.ppermute(value, ('blk', 'chan'), pairs)  4.19 us
    ppermute x1, starting transfers between devices, ring_permute(): return lax.ppermute(value, ('blk', 'chan'), pairs)  2.59 us
    all_gather x1, blocking collectives, local(): own = lax.all_gather(features, 'chan', axis=0)  2.16 us
    pallas_call x1, Pallas kernels, local(): pl.pallas_call(pack_kernel, out_shape=[jax.ShapeDtypeStruct((9 * half_out...  1.61 us
    ppermute x5, starting transfers between devices, chan_swap(): return lax.ppermute(value, 'chan', [(0, 1), (1, 0)])  1.03 us
    ppermute x5, waiting for transfers between devices, chan_swap(): return lax.ppermute(value, 'chan', [(0, 1), (1, 0)])  0.91 us
    ppermute x1, waiting for transfers between devices, ring_permute(): return lax.ppermute(value, ('blk', 'chan'), pairs)  0.84 us
  transfers between devices with their start and end apart: 8, of which 2 were waited for; matrix products, arithmetic and copies ran while one was open for 0% of the time, Pallas kernels for 10%

profile of v2, /device:TPU:0, one launch (start us, length us, event | category | flops | bytes accessed | tf_op | source)
XLA Modules:
  0.0 18.8 jit_solution(15187763081202727179)
XLA Ops:
  0.0 2.2 %all-gather = bf16[128,256]{1,0:T(8,128)(2,1)S(1)} all-gather(bf16[64,256]{1,0:T(8,128)(2,1)} %param.10), channel_id=2, replica_groups=mesh['dp'=2,'blk'=8,'chan'=2] {'chan'}, dimensions={0}, use_global_device_ids=true | all-gather | bytes 98304 | tf_op jit(solution)/shard_map/all_gather | solution.py:375
  2.2 0.4 %collective-permute-start.6 = (bf16[2,3,512,256]{3,2,1,0:T(8,128)(2,1)}, bf16[2,3,512,256]{3,2,1,0:T(8,128)(2,1)S(1)}, u32[]{:S(2)}, u32[]{:S(2)}) collective-permute-start(bf16[2,3,512,256]{3,2,1,0:T(8,128)(2,1)} %w_any.1), channel_id=1, source_target_pairs={{0,1},{1,0},{2,3},{3,2},{4,5},{5,4},{6,7},{7,6},{8,9},{9,8},{10,11... | collective-permute-start | bytes 4718600 | tf_op jit(solution)/shard_map/ppermute | solution.py:18
  2.5 2.6 %collective-permute-start = (bf16[2,64,256]{2,1,0:T(8,128)(2,1)S(1)}, bf16[2,64,256]{2,1,0:T(8,128)(2,1)S(1)}, u32[]{:S(2)}, u32[]{:S(2)}) collective-permute-start(bf16[2,64,256]{2,1,0:T(8,128)(2,1)S(1)} %bitcast.5), channel_id=1, source_target_pairs={{1,0},{3,1},{0,2},{5,3},{2,4},{7,5},{4,6},{9,7},{6,8},{11,9},{8,10... | collective-permute-start | bytes 196616 | tf_op jit(solution)/shard_map/ppermute | solution.py:36
  5.2 1.6 %collective-permute-start.1 = (bf16[2,64,256]{2,1,0:T(8,128)(2,1)S(1)}, bf16[2,64,256]{2,1,0:T(8,128)(2,1)S(1)}, u32[]{:S(2)}, u32[]{:S(2)}) collective-permute-start(bf16[2,64,256]{2,1,0:T(8,128)(2,1)S(1)} %bitcast.6), channel_id=1, source_target_pairs={{1,0},{5,1},{3,2},{7,3},{0,4},{9,5},{2,6},{11,7},{4,8},{13,9},{6,1... | collective-permute-start | bytes 196616 | tf_op jit(solution)/shard_map/ppermute | solution.py:36
  6.7 2.6 %collective-permute-start.2 = (bf16[2,64,256]{2,1,0:T(8,128)(2,1)S(1)}, bf16[2,64,256]{2,1,0:T(8,128)(2,1)S(1)}, u32[]{:S(2)}, u32[]{:S(2)}) collective-permute-start(bf16[2,64,256]{2,1,0:T(8,128)(2,1)S(1)} %bitcast.7), channel_id=1, source_target_pairs={{8,0},{7,1},{10,2},{9,3},{12,4},{11,5},{14,6},{13,7},{0,8},{15,9},... | collective-permute-start | bytes 196616 | tf_op jit(solution)/shard_map/ppermute | solution.py:27
  10.0 1.6 %shard_map.100 = (bf16[288,128]{1,0:T(8,128)(2,1)S(1)}, f32[3,128,384]{2,1,0:T(8,128)S(1)}, f32[256,128]{1,0:T(8,128)S(1)}, f32[8,256]{1,0:T(8,128)S(1)}, bf16[2...) custom-call(s32[1]{0:T(128)S(6)} %copy.11.length_ref, bf16[2,64,256]{2,1,0:T(8,128)(2,1)S(1)} %bitcast.8, ...), custom_call_target="tpu_custom_call" | custom-call | tf_op jit(solution)/shard_map/pallas_call | solution.py:390
  11.6 0.1 collective-permute-start.7
  11.7 0.0 collective-permute-done.r1_ref
  11.7 0.5 %collective-permute-start.3 = (bf16[2,64,256]{2,1,0:T(8,128)(2,1)S(1)}, bf16[2,64,256]{2,1,0:T(8,128)(2,1)S(1)}, u32[]{:S(2)}, u32[]{:S(2)}) collective-permute-start(bf16[2,64,256]{2,1,0:T(8,128)(2,1)S(1)} %collective-permute-done.r1_ref), channel_id=1, source_target_pairs={{0,1},{1,0},{2,3},{3,2},{4,5},{5,4},{6,7},{7,6},{8,9},{9,8},{10,11... | collective-permute-start | bytes 196616 | tf_op jit(solution)/shard_map/ppermute | solution.py:18
  12.2 0.0 collective-permute-done.1.r2_ref
  12.2 0.1 collective-permute-start.4
  12.3 0.8 %collective-permute-done.2.r3_ref = bf16[2,64,256]{2,1,0:T(8,128)(2,1)S(1)} collective-permute-done((bf16[2,64,256]{2,1,0:T(8,128)(2,1)S(1)}, bf16[2,64,256]{2,1,0:T(8,128)(2,1)S(1)}, u32[]{:S(2)}, u32[]{:S(2)}) %collective-permute-start.2) | collective-permute-done | bytes 65568 | tf_op jit(solution)/shard_map/ppermute | solution.py:27
  13.1 0.0 collective-permute-start.5
  13.1 0.0 collective-permute-done.7.oth_ref
  13.1 0.3 %shard_map.101 = (bf16[1152,256]{1,0:T(8,128)(2,1)S(1)}, f32[8,256]{1,0:T(8,128)S(1)}, bf16[16,512]{1,0:T(8,128)(2,1)S(1)}) custom-call(bf16[288,128]{1,0:T(8,128)(2,1)S(1)} %get-tuple-element.23.own_ref, bf16[288,128]{1,0:T(8,128)(2,1)S(1)} %collective-permute-done.7.oth_ref), custom_call_target="tpu_custom_call" | custom-call | tf_op jit(solution)/shard_map/pallas_call | solution.py:430
  13.5 0.0 collective-permute-done.3.s1_ref
  13.5 0.0 collective-permute-done.4.s2_ref
  13.5 0.9 %collective-permute-done.5.s3_ref = bf16[2,64,256]{2,1,0:T(8,128)(2,1)S(1)} collective-permute-done((bf16[2,64,256]{2,1,0:T(8,128)(2,1)S(1)}, bf16[2,64,256]{2,1,0:T(8,128)(2,1)S(1)}, u32[]{:S(2)}, u32[]{:S(2)}) %collective-permute-start.5) | collective-permute-done | bytes 65568 | tf_op jit(solution)/shard_map/ppermute | solution.py:18
  14.4 0.0 collective-permute-done.6.w_oth_ref
  14.4 4.4 %shard_map.102 = f32[64,128]{1,0:T(8,128)} custom-call(bf16[2,64,256]{2,1,0:T(8,128)(2,1)S(1)} %bitcast.9, bf16[2,64,256]{2,1,0:T(8,128)(2,1)S(1)} %collective-permute-done.r1_ref, bf16[2,64,256]{2,1,0:T(8,128)(2,1)S(1)} %collective-permute-done.1.r2_ref, bf16[2,64,256]{2,1,0:T(8,128)(2,1)S(1)} %collective-permute-done.2.r3_ref, ...), custom_call_target="tpu_custom_call" | custom-call | tf_op jit(solution)/shard_map/pallas_call | solution.py:445
Async XLA Ops:
  2.2 12.2 %collective-permute-start.6 = (bf16[2,3,512,256]{3,2,1,0:T(8,128)(2,1)}, bf16[2,3,512,256]{3,2,1,0:T(8,128)(2,1)S(1)}, u32[]{:S(2)}, u32[]{:S(2)}) collective-permute-start(bf16[2,3,512,256]{3,2,1,0:T(8,128)(2,1)} %w_any.1), channel_id=1, source_target_pairs={{0,1},{1,0},{2,3},{3,2},{4,5},{5,4},{6,7},{7,6},{8,9},{9,8},{10,11... | collective-permute-start | bytes 4718600 | tf_op jit(solution)/shard_map/ppermute | solution.py:18
  2.5 9.1 %collective-permute-start = (bf16[2,64,256]{2,1,0:T(8,128)(2,1)S(1)}, bf16[2,64,256]{2,1,0:T(8,128)(2,1)S(1)}, u32[]{:S(2)}, u32[]{:S(2)}) collective-permute-start(bf16[2,64,256]{2,1,0:T(8,128)(2,1)S(1)} %bitcast.5), channel_id=1, source_target_pairs={{1,0},{3,1},{0,2},{5,3},{2,4},{7,5},{4,6},{9,7},{6,8},{11,9},{8,10... | collective-permute-start | bytes 196616 | tf_op jit(solution)/shard_map/ppermute | solution.py:36
  5.2 7.0 %collective-permute-start.1 = (bf16[2,64,256]{2,1,0:T(8,128)(2,1)S(1)}, bf16[2,64,256]{2,1,0:T(8,128)(2,1)S(1)}, u32[]{:S(2)}, u32[]{:S(2)}) collective-permute-start(bf16[2,64,256]{2,1,0:T(8,128)(2,1)S(1)} %bitcast.6), channel_id=1, source_target_pairs={{1,0},{5,1},{3,2},{7,3},{0,4},{9,5},{2,6},{11,7},{4,8},{13,9},{6,1... | collective-permute-start | bytes 196616 | tf_op jit(solution)/shard_map/ppermute | solution.py:36
  6.7 6.4 %collective-permute-start.2 = (bf16[2,64,256]{2,1,0:T(8,128)(2,1)S(1)}, bf16[2,64,256]{2,1,0:T(8,128)(2,1)S(1)}, u32[]{:S(2)}, u32[]{:S(2)}) collective-permute-start(bf16[2,64,256]{2,1,0:T(8,128)(2,1)S(1)} %bitcast.7), channel_id=1, source_target_pairs={{8,0},{7,1},{10,2},{9,3},{12,4},{11,5},{14,6},{13,7},{0,8},{15,9},... | collective-permute-start | bytes 196616 | tf_op jit(solution)/shard_map/ppermute | solution.py:27
  11.6 1.5 %collective-permute-start.7 = (bf16[288,128]{1,0:T(8,128)(2,1)S(1)}, bf16[288,128]{1,0:T(8,128)(2,1)S(1)}, u32[]{:S(2)}, u32[]{:S(2)}) collective-permute-start(bf16[288,128]{1,0:T(8,128)(2,1)S(1)} %get-tuple-element.23.own_ref), channel_id=1, source_target_pairs={{0,1},{1,0},{2,3},{3,2},{4,5},{5,4},{6,7},{7,6},{8,9},{9,8},{10,11... | collective-permute-start | bytes 221192 | tf_op jit(solution)/shard_map/ppermute | solution.py:18
  11.7 1.8 %collective-permute-start.3 = (bf16[2,64,256]{2,1,0:T(8,128)(2,1)S(1)}, bf16[2,64,256]{2,1,0:T(8,128)(2,1)S(1)}, u32[]{:S(2)}, u32[]{:S(2)}) collective-permute-start(bf16[2,64,256]{2,1,0:T(8,128)(2,1)S(1)} %collective-permute-done.r1_ref), channel_id=1, source_target_pairs={{0,1},{1,0},{2,3},{3,2},{4,5},{5,4},{6,7},{7,6},{8,9},{9,8},{10,11... | collective-permute-start | bytes 196616 | tf_op jit(solution)/shard_map/ppermute | solution.py:18
  12.2 1.3 %collective-permute-start.4 = (bf16[2,64,256]{2,1,0:T(8,128)(2,1)S(1)}, bf16[2,64,256]{2,1,0:T(8,128)(2,1)S(1)}, u32[]{:S(2)}, u32[]{:S(2)}) collective-permute-start(bf16[2,64,256]{2,1,0:T(8,128)(2,1)S(1)} %collective-permute-done.1.r2_ref), channel_id=1, source_target_pairs={{0,1},{1,0},{2,3},{3,2},{4,5},{5,4},{6,7},{7,6},{8,9},{9,8},{10,11... | collective-permute-start | bytes 196616 | tf_op jit(solution)/shard_map/ppermute | solution.py:18
  13.1 1.3 %collective-permute-start.5 = (bf16[2,64,256]{2,1,0:T(8,128)(2,1)S(1)}, bf16[2,64,256]{2,1,0:T(8,128)(2,1)S(1)}, u32[]{:S(2)}, u32[]{:S(2)}) collective-permute-start(bf16[2,64,256]{2,1,0:T(8,128)(2,1)S(1)} %collective-permute-done.2.r3_ref), channel_id=1, source_target_pairs={{0,1},{1,0},{2,3},{3,2},{4,5},{5,4},{6,7},{7,6},{8,9},{9,8},{10,11... | collective-permute-start | bytes 196616 | tf_op jit(solution)/shard_map/ppermute | solution.py:18

commit v3 on v0

--- a/solution.py
+++ b/solution.py
@@ -18,7 +18,7 @@
     return lax.ppermute(value, "chan", [(0, 1), (1, 0)])
 
 
-def blk_permute(value, offset_0, offset_1):
+def ring_permute(value, offset_0, offset_1):
     count = lax.axis_size("blk")
     pairs = []
     for i in range(count):
@@ -27,43 +27,103 @@
     return lax.ppermute(value, ("blk", "chan"), pairs)
 
 
+def line_permute(value, step):
+    count = lax.axis_size("blk")
+    pairs = []
+    for i in range(count):
+        pairs.append(((i - step) * 2 if i >= step else i * 2 + 1, i * 2))
+        pairs.append(((i + step) * 2 + 1 if i + step < count else i * 2, i * 2 + 1))
+    return lax.ppermute(value, ("blk", "chan"), pairs)
+
+
+def pack_kernel(
+    own_any,
+    mask_any,
+    mw_any,
+    mb_any,
+    hw_any,
+    cb_any,
+    pb_any,
+    own_ref,
+    mask_ref,
+    packed_ref,
+    small_ref,
+    mw_s,
+    mb_s,
+    hw_s,
+    cb_s,
+    pb_s,
+    extra_s,
+    sems,
+):
+    pairs = (
+        (mw_any, mw_s),
+        (cb_any, cb_s),
+        (mb_any, mb_s),
+        (hw_any, hw_s),
+        (pb_any, pb_s),
+        (mask_any, mask_ref),
+        (own_any, own_ref),
+    )
+    copies = [
+        pltpu.make_async_copy(source, target, sems.at[at])
+        for at, (source, target) in enumerate(pairs)
+    ]
+    for copy in copies:
+        copy.start()
+    extra_s[...] = jnp.zeros_like(extra_s)
+    for copy in copies[:5]:
+        copy.wait()
+
+    half = mw_any.shape[2]
+    biases = cb_s[...].astype(F32)
+    for layer in range(CONV1):
+        for quarter in range(4):
+            at = 4 * layer + quarter
+            extra_s[at : at + 1, :F2] = biases[layer : layer + 1, quarter * F2 : (quarter + 1) * F2]
+    extra_s[8:9, :half] = mb_s[...].astype(F32)
+    extra_s[9:10, :half] = hw_s[...].astype(F32)
+    extra = pltpu.roll(extra_s[...], F2, axis=1)
+    for s in range(3):
+        for r in range(3):
+            at = (3 * s + r) * half
+            packed_ref[at : at + half, :F2] = mw_s[s, r]
+    packed_ref[:32, F2:] = extra[:, F2:].astype(BF16)
+    small_ref[0:2, :] = biases
+    small_ref[2:3, : 2 * F2] = pb_s[...].astype(F32)
+    for copy in copies[5:]:
+        copy.wait()
+
+
 def prep_kernel(
     length_ref,
     mask_ref,
-    mw_own_ref,
-    mw_oth_ref,
-    mb_own_ref,
-    mb_oth_ref,
-    hw_own_ref,
-    hw_oth_ref,
-    cb_own_ref,
-    cb_oth_ref,
-    pb_ref,
-    wbig_ref,
+    own_ref,
+    oth_ref,
     col_mask_ref,
     valid_ref,
-    small_ref,
+    wbig_ref,
+    side_ref,
     head_ref,
     wt_s,
     taps_s,
 ):
+    half = own_ref.shape[0] // 9
     rows = valid_ref.shape[0]
     columns = col_mask_ref.shape[1]
     bins = columns // 2
-    half = mw_own_ref.shape[2]
     col_rows = columns + 2 * HALO
     count = lax.axis_size("blk")
     i = lax.axis_index("blk")
     c = lax.axis_index("chan")
     first = i * bins
     first_col = first + c * columns
-    length = length_ref[...]
-
-    for source, side in ((mw_own_ref, c), (mw_oth_ref, 1 - c)):
+    length = length_ref[0]
+
+    for source, side in ((own_ref, c), (oth_ref, 1 - c)):
         at = pl.ds(pl.multiple_of(side * half, half), half)
-        for s in range(3):
-            for r in range(3):
-                taps_s[3 * s + r, at, :] = source[s, r].astype(F32)
+        for tap in range(9):
+            taps_s[tap, at, :] = source[tap * half : (tap + 1) * half, :F2].astype(F32)
     blank = jnp.zeros((F2, F2), F32)
     for j in range(4):
         pieces = []
@@ -76,23 +136,31 @@
             )
     wbig_ref[...] = wt_s[...].T.astype(BF16)
 
-    def spread(own_ref, oth_ref, repeats):
-        o = lax.broadcasted_iota(jnp.int32, (half, repeats * F2), 0)
-        lane = lax.broadcasted_iota(jnp.int32, (half, repeats * F2), 1) % F2
+    def spread(row, repeats):
+        o = lax.broadcasted_iota(jnp.int32, (2 * F2, repeats * F2), 0)
+        lane = lax.broadcasted_iota(jnp.int32, (2 * F2, repeats * F2), 1) % F2
         total = jnp.zeros((16, repeats * F2), F32)
         for ref, side in ((own_ref, c), (oth_ref, 1 - c)):
-            pick = (lane == side * half + o).astype(BF16)
-            value = jnp.broadcast_to(ref[...], (16, half)).astype(BF16)
+            pick = ((lane == side * half + o - F2) & (o >= F2) & (o < F2 + half)).astype(BF16)
+            value = ref[:16, :].astype(F32)[row : row + 1]
+            value = jnp.broadcast_to(value, (16, 2 * F2)).astype(BF16)
             total = total + jnp.dot(value, pick, preferred_element_type=F32)
         return total
 
-    head_all = spread(hw_own_ref, hw_oth_ref, 8)
     q = lax.broadcasted_iota(jnp.int32, (16, 8 * F2), 0)
     k = lax.broadcasted_iota(jnp.int32, (16, 8 * F2), 1)
     head_ref[...] = jnp.where(
-        q == 2 * ((k % (4 * F2)) // F2) + k // (4 * F2), head_all, 0.0
+        q == 2 * ((k % (4 * F2)) // F2) + k // (4 * F2), spread(9, 8), 0.0
     ).astype(BF16)
-    bias_all = spread(mb_own_ref, mb_oth_ref, 4)
+    side_ref[0:1, :] = spread(8, 4)[:1]
+    other = oth_ref[:16, :].astype(F32)
+    other = pltpu.roll(other, F2, axis=1)
+    for layer in range(CONV1):
+        for quarter in range(4):
+            at = 4 * layer + quarter
+            side_ref[1 + layer : 2 + layer, quarter * F2 : (quarter + 1) * F2] = other[
+                at : at + 1, :F2
+            ]
 
     minus = F32(-jnp.inf)
     block = lax.broadcasted_iota(jnp.int32, (BAND + 1, count), 1)
@@ -133,29 +201,27 @@
     )
     valid_ref[...] = jnp.where((bin_index >= 0) & (bin_index < length), 1.0, 0.0)
 
-    small_ref[0:2, :] = cb_own_ref[...].astype(F32)
-    small_ref[2:4, :] = cb_oth_ref[...].astype(F32)
-    small_ref[4:5, :] = bias_all[:1]
-    small_ref[5:6, : 2 * F2] = pb_ref[...].astype(F32)
-    small_ref[5:6, 2 * F2 :] = jnp.where(
+    side_ref[3:4, : 2 * F2] = jnp.where(
         live_at(lax.broadcasted_iota(jnp.int32, (1, columns), 1), 0), 1.0, 0.0
     )
 
 
 def contact_kernel(
     own_ref,
+    r2_ref,
+    s2_ref,
     r1_ref,
-    r2_ref,
+    s1_ref,
     r3_ref,
-    s1_ref,
     s3_ref,
     w_own_ref,
+    pw_ref,
     w_oth_ref,
-    pw_ref,
-    wbig_ref,
+    small_ref,
     col_mask_ref,
     valid_ref,
-    small_ref,
+    wbig_ref,
+    side_ref,
     head_ref,
     out_ref,
     h_s,
@@ -174,12 +240,13 @@
     first = i * bins
     first_col = first + c * (2 * bins)
 
-    def put(start, number, ref, source):
+    def put(start, number, ref, source, swapped=0):
         keep = valid_ref[start : start + number, :] != 0
         for part in range(2):
+            held = lax.rem(part + c + swapped, 2)
             for at in range(0, half, 128):
                 h_s[start : start + number, part * half + at : part * half + at + 128] = jnp.where(
-                    keep, ref[part, source : source + number, at : at + 128].astype(F32), 0.0
+                    keep, ref[held, source : source + number, at : at + 128].astype(F32), 0.0
                 )
 
     tail = bins - HALO
@@ -189,17 +256,17 @@
     @pl.when(c == 0)
     def _():
         put(HALO, bins, own_ref, 0)
-        put(HALO + bins, bins, s1_ref, 0)
-        put(HALO + 2 * bins, HALO, r2_ref, 0)
+        put(HALO + bins, bins, s1_ref, 0, 1)
+        put(HALO + 2 * bins, HALO, s2_ref, 0, 1)
         put(col_rows, HALO, r1_ref, tail)
-        put(col_rows + HALO + bins, HALO, s1_ref, 0)
+        put(col_rows + HALO + bins, HALO, s1_ref, 0, 1)
 
     @pl.when(c == 1)
     def _():
         put(HALO, bins, r2_ref, 0)
         put(HALO + bins, bins, r3_ref, 0)
-        put(HALO + 2 * bins, HALO, s3_ref, 0)
-        put(col_rows, HALO, s1_ref, tail)
+        put(HALO + 2 * bins, HALO, s3_ref, 0, 1)
+        put(col_rows, HALO, s1_ref, tail, 1)
         put(col_rows + HALO + bins, HALO, r1_ref, 0)
 
     place = lax.broadcasted_iota(jnp.int32, (rows, 1), 0)
@@ -220,12 +287,12 @@
             q = q + jnp.dot(taps[1], w_ref[layer, 1], preferred_element_type=F32)
             q = q + jnp.dot(taps[2], w_ref[layer, 2], preferred_element_type=F32)
             lanes = pl.ds(pl.multiple_of(side * half, half), half)
-            bias = small_ref[2 * at + layer : 2 * at + layer + 1, :]
+            bias = side_ref[1 + layer : 2 + layer, :] if at else small_ref[layer : layer + 1, :]
             new = (h_s[:, lanes] + jnp.maximum(q + bias, 0.0)).astype(BF16).astype(F32)
             h_s[:, lanes] = jnp.where(inside, new, 0.0)
 
     proj = jnp.dot(h_s[...].astype(BF16), pw_ref[...], preferred_element_type=F32)
-    proj = (proj + small_ref[5:6, : 2 * F2]).astype(BF16).astype(F32)
+    proj = (proj + small_ref[2:3, : 2 * F2]).astype(BF16).astype(F32)
 
     minus = F32(-jnp.inf)
     low = lax.broadcasted_iota(jnp.int32, (1, 2 * F2), 1) < F2
@@ -257,7 +324,7 @@
     groups = bins // 8
     per_dot = x_s.shape[0] // (2 * bins)
     zero = jnp.zeros((), BF16)
-    bias4 = small_ref[4:5, :]
+    bias4 = side_ref[0:1, :]
     for v in range(2):
         for start in range(0, groups, per_dot):
             for slot in range(2 * start, 2 * (start + per_dot) + 1):
@@ -285,7 +352,7 @@
                 mixed = y[at_row : at_row + 2 * bins] + centre
                 mix_s[group, :, v * 4 * F2 : (v + 1) * 4 * F2] = mixed.astype(BF16)
 
-    lane_live = small_ref[5:6, 2 * F2 :] != 0
+    lane_live = side_ref[3:4, : 2 * F2] != 0
     for group in range(groups):
         value = lax.dot_general(
             head_ref[...], mix_s[group], (((1,), (1,)), ((), ())), preferred_element_type=F32
@@ -309,50 +376,77 @@
     head_weight,
 ):
     bins, half = features.shape
-    own = lax.all_gather(features, "chan", axis=0)
-    r2 = blk_permute(own, 2, 2)
-    r1 = blk_permute(own, -1, 1)
-    r3 = blk_permute(own, 4, 3)
+    rows = 3 * bins + 4 * HALO
+    half_out = map_bias.shape[0]
+    smem = pl.BlockSpec(memory_space=pltpu.SMEM)
+    vmem = pl.BlockSpec(memory_space=pltpu.VMEM)
+    anywhere = pl.BlockSpec(memory_space=pl.ANY)
+    params = pltpu.CompilerParams(vmem_limit_bytes=24 * 1024 * 1024)
+
+    def in_hbm(value):
+        return pltpu.with_memory_space_constraint(value, pltpu.HBM)
+
+    other = chan_swap(features)
+    own, mask, packed, small = pl.pallas_call(
+        pack_kernel,
+        out_shape=[
+            jax.ShapeDtypeStruct(features.shape, BF16),
+            jax.ShapeDtypeStruct(band_mask.shape[::-1], jnp.int32),
+            jax.ShapeDtypeStruct((9 * half_out, 2 * F2), BF16),
+            jax.ShapeDtypeStruct((8, half), F32),
+        ],
+        in_specs=[anywhere] * 7,
+        out_specs=[vmem] * 4,
+        scratch_shapes=[
+            pltpu.VMEM(map_weight.shape, BF16),
+            pltpu.VMEM((1, half_out), BF16),
+            pltpu.VMEM((1, half_out), BF16),
+            pltpu.VMEM(conv_bias.shape, BF16),
+            pltpu.VMEM((1, 2 * F2), BF16),
+            pltpu.VMEM((32, 2 * F2), F32),
+            pltpu.SemaphoreType.DMA((7,)),
+        ],
+        cost_estimate=pl.CostEstimate(flops=4000000000, bytes_accessed=1000000, transcendentals=0),
+        compiler_params=params,
+    )(
+        in_hbm(features),
+        in_hbm(band_mask.T),
+        in_hbm(map_weight),
+        in_hbm(map_bias[None]),
+        in_hbm(head_weight[None]),
+        in_hbm(conv_bias),
+        in_hbm(proj_bias[None]),
+    )
+    own = jnp.stack([own, other])
+    r1 = line_permute(own, 1)
+    r2 = line_permute(own, 2)
+    r3 = ring_permute(own, 4, 3)
     s1 = chan_swap(r1)
+    s2 = chan_swap(r2)
     s3 = chan_swap(r3)
-    w_oth = chan_swap(conv_weight)
-
-    rows = 3 * bins + 4 * HALO
-    vmem = pl.BlockSpec(memory_space=pltpu.VMEM)
-    params = pltpu.CompilerParams(vmem_limit_bytes=24 * 1024 * 1024)
+    w_in, own = lax.optimization_barrier((conv_weight, own))
+    w_oth = chan_swap(w_in)
     prepared = pl.pallas_call(
         prep_kernel,
         out_shape=[
-            jax.ShapeDtypeStruct((18 * F2, 4 * F2), BF16),
             jax.ShapeDtypeStruct((3, 2 * bins, 6 * F2), F32),
             jax.ShapeDtypeStruct((rows, 2 * F2), F32),
+            jax.ShapeDtypeStruct((18 * F2, 4 * F2), BF16),
             jax.ShapeDtypeStruct((8, half), F32),
             jax.ShapeDtypeStruct((16, 8 * F2), BF16),
         ],
-        in_specs=[vmem] * 11,
+        in_specs=[smem] + [vmem] * 3,
         out_specs=[vmem] * 5,
         scratch_shapes=[
             pltpu.VMEM((4 * F2, 18 * F2), F32),
             pltpu.VMEM((9, F2, F2), F32),
         ],
         compiler_params=params,
-    )(
-        chrom_len[None],
-        band_mask.T,
-        map_weight,
-        chan_swap(map_weight),
-        map_bias[None],
-        chan_swap(map_bias)[None],
-        head_weight[None],
-        chan_swap(head_weight)[None],
-        conv_bias,
-        chan_swap(conv_bias),
-        proj_bias[None],
-    )
+    )(chrom_len, mask, packed, chan_swap(packed))
     return pl.pallas_call(
         contact_kernel,
         out_shape=jax.ShapeDtypeStruct((bins, 2 * bins), F32),
-        in_specs=[vmem] * 14,
+        in_specs=[vmem] * 16,
         out_specs=vmem,
         scratch_shapes=[
             pltpu.VMEM((rows, 2 * half), F32),
@@ -361,7 +455,20 @@
             pltpu.VMEM((bins // 8, 2 * bins, 8 * F2), BF16),
         ],
         compiler_params=params,
-    )(own, r1, r2, r3, s1, s3, conv_weight, w_oth, proj_weight, *prepared)
+    )(
+        own,
+        r2,
+        s2,
+        r1,
+        s1,
+        r3,
+        s3,
+        conv_weight,
+        proj_weight,
+        w_oth,
+        small,
+        *prepared,
+    )
 
 
 def solution(mesh):

time: 32.2 us -> 17.3 us (0.54)
  waiting for transfers between devices: 7.76 us -> 1.23 us
  local copies, waits for them, and re-layouts: 6.51 us -> 0.27 us
  blocking collectives: 3.3 us -> 0 us
  Pallas kernels: 4.98 us -> 6.16 us
    unnamed x16 -> x4, local copies, waits for them, and re-layouts: 6.51 us -> 0.27 us
    ppermute x7 -> x6, waiting for transfers between devices: 3.48 us -> 0.02 us  [chan_swap(): return lax.ppermute(value, 'chan', [(0, 1), (1, 0)])]
    all_gather x1 -> x0, blocking collectives: 3.3 us -> none  [local(): own = lax.all_gather(features, 'chan', axis=0)]
    ppermute x3, waiting for transfers between devices: 4.28 us -> 1.21 us  [the longest x2 1.21 us: line_permute(): return lax.ppermute(value, ('blk', 'chan'), pairs)]
    pallas_call x1 -> x2, Pallas kernels: 0.53 us -> 1.77 us  [the longest x1 1.23 us: local(): pl.pallas_call(pack_kernel, out_shape=[jax.ShapeDtypeStruct(features.shap...]
    ppermute x7 -> x6, starting transfers between devices: 1.87 us -> 1.68 us  [chan_swap(): return lax.ppermute(value, 'chan', [(0, 1), (1, 0)])]
  transfers between devices with their start and end apart: 10 -> 9, of which waited for: 5 -> 1; matrix products, arithmetic and copies ran while one was open for 0% -> 0% of each run, Pallas kernels for 2% -> 10%
where the time goes in v3:
time: 17.3 us; the launch traced here: 17.2 us
  starting transfers between devices  8.78 us (51%)
  Pallas kernels  6.16 us (36%)
  waiting for transfers between devices  1.23 us (7%)
  between operations  0.74 us (4%)
  local copies, waits for them, and re-layouts  0.27 us (2%)
    pallas_call x1, Pallas kernels, local(): pl.pallas_call(contact_kernel, out_shape=jax.ShapeDtypeStruct((bins, 2 *...  4.38 us
    ppermute x1, starting transfers between devices, ring_permute(): return lax.ppermute(value, ('blk', 'chan'), pairs)  4.04 us
    ppermute x2, starting transfers between devices, line_permute(): return lax.ppermute(value, ('blk', 'chan'), pairs)  3.07 us
    ppermute x6, starting transfers between devices, chan_swap(): return lax.ppermute(value, 'chan', [(0, 1), (1, 0)])  1.68 us
    pallas_call x1, Pallas kernels, local(): pl.pallas_call(pack_kernel, out_shape=[jax.ShapeDtypeStruct(features.shap...  1.23 us
    ppermute x2, waiting for transfers between devices, line_permute(): return lax.ppermute(value, ('blk', 'chan'), pairs)  1.21 us
    pallas_call x1, Pallas kernels, local(): pl.pallas_call(prep_kernel, out_shape=[jax.ShapeDtypeStruct((3, 2 * bins,...  0.54 us
  transfers between devices with their start and end apart: 9, of which 1 were waited for; matrix products, arithmetic and copies ran while one was open for 0% of the time, Pallas kernels for 10%

profile of v3, /device:TPU:0, one launch (start us, length us, event | category | flops | bytes accessed | tf_op | source)
XLA Modules:
  0.0 17.2 jit_solution(1157261204818865219)
XLA Ops:
  0.0 0.5 %collective-permute-start = (bf16[64,256]{1,0:T(8,128)(2,1)}, bf16[64,256]{1,0:T(8,128)(2,1)S(1)}, u32[]{:S(2)}, u32[]{:S(2)}) collective-permute-start(bf16[64,256]{1,0:T(8,128)(2,1)} %own_any.1), channel_id=1, source_target_pairs={{0,1},{1,0},{2,3},{3,2},{4,5},{5,4},{6,7},{7,6},{8,9},{9,8},{10,11... | collective-permute-start | bytes 98312 | tf_op jit(solution)/shard_map/ppermute | solution.py:18
  0.5 0.0 copy-start
  0.5 0.0 copy-start.1
  0.5 1.2 %shard_map.100 = (bf16[64,256]{1,0:T(8,128)(2,1)S(1)}, s32[4,8]{1,0:T(4,128)S(1)}, bf16[288,128]{1,0:T(8,128)(2,1)S(1)}, f32[8,256]{1,0:T(8,128)S(1)}) custom-call(bf16[64,256]{1,0:T(8,128)(2,1)} %own_any.1, s32[4,8]{1,0:T(4,128)} %bitcast.8, bf16[3,3,32,64]{3,2,1,0:T(8,128)(2,1)} %mw_any.1, bf16[1,32]{1,0:T(2,128)(2,1)} %bitcast.9, bf16[1,32]{1,0:T(2,128)(2,1)} %bitcast.10, ...), custom_call_target="tpu_custom_call" | custom-call | flops 4000000000 | bytes 1000000 | tf_op jit(solution)/shard_map/pallas_call | solution.py:390
  1.7 0.0 collective-permute-done
  1.7 0.3 %copy-done = bf16[2,3,512,256]{3,2,1,0:T(8,128)(2,1)S(1)} copy-done((bf16[2,3,512,256]{3,2,1,0:T(8,128)(2,1)S(1)}, bf16[2,3,512,256]{3,2,1,0:T(8,128)(2,1)}, u32[]{:S(2)}) %copy-start) | copy-done | bytes 1572888
  2.0 0.1 collective-permute-start.7
  2.0 4.0 %collective-permute-start.5 = (bf16[2,64,256]{2,1,0:T(8,128)(2,1)S(1)}, bf16[2,64,256]{2,1,0:T(8,128)(2,1)S(1)}, u32[]{:S(2)}, u32[]{:S(2)}) collective-permute-start(bf16[2,64,256]{2,1,0:T(8,128)(2,1)S(1)} %pad_maximum_fusion.own_ref), channel_id=1, source_target_pairs={{8,0},{7,1},{10,2},{9,3},{12,4},{11,5},{14,6},{13,7},{0,8},{15,9},... | collective-permute-start | bytes 196616 | tf_op jit(solution)/shard_map/ppermute | solution.py:27
  6.1 1.5 %collective-permute-start.3 = (bf16[2,64,256]{2,1,0:T(8,128)(2,1)S(1)}, bf16[2,64,256]{2,1,0:T(8,128)(2,1)S(1)}, u32[]{:S(2)}, u32[]{:S(2)}) collective-permute-start(bf16[2,64,256]{2,1,0:T(8,128)(2,1)S(1)} %pad_maximum_fusion.own_ref), channel_id=1, source_target_pairs={{1,0},{3,1},{0,2},{5,3},{2,4},{7,5},{4,6},{9,7},{6,8},{11,9},{8,10... | collective-permute-start | bytes 196616 | tf_op jit(solution)/shard_map/ppermute | solution.py:36
  7.6 1.6 %collective-permute-start.1 = (bf16[2,64,256]{2,1,0:T(8,128)(2,1)S(1)}, bf16[2,64,256]{2,1,0:T(8,128)(2,1)S(1)}, u32[]{:S(2)}, u32[]{:S(2)}) collective-permute-start(bf16[2,64,256]{2,1,0:T(8,128)(2,1)S(1)} %pad_maximum_fusion.own_ref), channel_id=1, source_target_pairs={{1,0},{5,1},{3,2},{7,3},{0,4},{9,5},{2,6},{11,7},{4,8},{13,9},{6,1... | collective-permute-start | bytes 196616 | tf_op jit(solution)/shard_map/ppermute | solution.py:36
  9.2 0.0 collective-permute-start.8
  9.2 0.0 collective-permute-done.5.r3_ref
  9.2 0.5 %collective-permute-start.6 = (bf16[2,64,256]{2,1,0:T(8,128)(2,1)S(1)}, bf16[2,64,256]{2,1,0:T(8,128)(2,1)S(1)}, u32[]{:S(2)}, u32[]{:S(2)}) collective-permute-start(bf16[2,64,256]{2,1,0:T(8,128)(2,1)S(1)} %collective-permute-done.5.r3_ref), channel_id=1, source_target_pairs={{0,1},{1,0},{2,3},{3,2},{4,5},{5,4},{6,7},{7,6},{8,9},{9,8},{10,11... | collective-permute-start | bytes 196616 | tf_op jit(solution)/shard_map/ppermute | solution.py:18
  9.7 0.0 collective-permute-done.3.r1_ref
  9.7 0.2 %collective-permute-start.4 = (bf16[2,64,256]{2,1,0:T(8,128)(2,1)S(1)}, bf16[2,64,256]{2,1,0:T(8,128)(2,1)S(1)}, u32[]{:S(2)}, u32[]{:S(2)}) collective-permute-start(bf16[2,64,256]{2,1,0:T(8,128)(2,1)S(1)} %collective-permute-done.3.r1_ref), channel_id=1, source_target_pairs={{0,1},{1,0},{2,3},{3,2},{4,5},{5,4},{6,7},{7,6},{8,9},{9,8},{10,11... | collective-permute-start | bytes 196616 | tf_op jit(solution)/shard_map/ppermute | solution.py:18
  9.9 1.2 %collective-permute-done.1.r2_ref = bf16[2,64,256]{2,1,0:T(8,128)(2,1)S(1)} collective-permute-done((bf16[2,64,256]{2,1,0:T(8,128)(2,1)S(1)}, bf16[2,64,256]{2,1,0:T(8,128)(2,1)S(1)}, u32[]{:S(2)}, u32[]{:S(2)}) %collective-permute-start.1) | collective-permute-done | bytes 65568 | tf_op jit(solution)/shard_map/ppermute | solution.py:36
  11.1 0.5 %collective-permute-start.2 = (bf16[2,64,256]{2,1,0:T(8,128)(2,1)S(1)}, bf16[2,64,256]{2,1,0:T(8,128)(2,1)S(1)}, u32[]{:S(2)}, u32[]{:S(2)}) collective-permute-start(bf16[2,64,256]{2,1,0:T(8,128)(2,1)S(1)} %collective-permute-done.1.r2_ref), channel_id=1, source_target_pairs={{0,1},{1,0},{2,3},{3,2},{4,5},{5,4},{6,7},{7,6},{8,9},{9,8},{10,11... | collective-permute-start | bytes 196616 | tf_op jit(solution)/shard_map/ppermute | solution.py:18
  12.2 0.0 collective-permute-done.8.oth_ref
  12.2 0.5 %shard_map.101 = (f32[3,128,384]{2,1,0:T(8,128)S(1)}, f32[256,128]{1,0:T(8,128)S(1)}, bf16[1152,256]{1,0:T(8,128)(2,1)S(1)}, f32[8,256]{1,0:T(8,128)S(1)}, bf16[16,512]{1,0:T(8,128)(2,1)S(1)}) custom-call(s32[1]{0:T(128)S(6)} %copy.11.length_ref, s32[4,8]{1,0:T(4,128)S(1)} %get-tuple-element.20.mask_ref, bf16[288,128]{1,0:T(8,128)(2,1)S(1)} %get-tuple-element.21.own_ref, ...), custom_call_target="tpu_custom_call" | custom-call | tf_op jit(solution)/shard_map/pallas_call | solution.py:429
  12.8 0.0 collective-permute-done.6.s3_ref
  12.8 0.0 collective-permute-done.4.s1_ref
  12.8 0.0 collective-permute-done.2.s2_ref
  12.8 0.0 collective-permute-done.7.w_oth_ref
  12.8 0.0 copy-done.1
  12.8 4.4 %shard_map.102 = f32[64,128]{1,0:T(8,128)} custom-call(bf16[2,64,256]{2,1,0:T(8,128)(2,1)S(1)} %pad_maximum_fusion.own_ref, bf16[2,64,256]{2,1,0:T(8,128)(2,1)S(1)} %collective-permute-done.1.r2_ref, bf16[2,64,256]{2,1,0:T(8,128)(2,1)S(1)} %collective-permute-done.2.s2_ref, bf16[2,64,256]{2,1,0:T(8,128)(2,1)S(1)} %collective-permute-done.3.r1_ref, ...), custom_call_target="tpu_custom_call" | custom-call | tf_op jit(solution)/shard_map/pallas_call | solution.py:446
  (1 shorter events, 0.0 us)
Async XLA Ops:
  0.0 1.7 %collective-permute-start = (bf16[64,256]{1,0:T(8,128)(2,1)}, bf16[64,256]{1,0:T(8,128)(2,1)S(1)}, u32[]{:S(2)}, u32[]{:S(2)}) collective-permute-start(bf16[64,256]{1,0:T(8,128)(2,1)} %own_any.1), channel_id=1, source_target_pairs={{0,1},{1,0},{2,3},{3,2},{4,5},{5,4},{6,7},{7,6},{8,9},{9,8},{10,11... | collective-permute-start | bytes 98312 | tf_op jit(solution)/shard_map/ppermute | solution.py:18
  0.5 1.5 %copy-start = (bf16[2,3,512,256]{3,2,1,0:T(8,128)(2,1)S(1)}, bf16[2,3,512,256]{3,2,1,0:T(8,128)(2,1)}, u32[]{:S(2)}) copy-start(bf16[2,3,512,256]{3,2,1,0:T(8,128)(2,1)} %w_own_ref.1) | copy-start | bytes 4718596
  0.5 12.3 %copy-start.1 = (bf16[512,128]{1,0:T(8,128)(2,1)S(1)}, bf16[512,128]{1,0:T(8,128)(2,1)}, u32[]{:S(2)}) copy-start(bf16[512,128]{1,0:T(8,128)(2,1)} %pw_ref.1) | copy-start | bytes 393220
  2.0 10.8 %collective-permute-start.7 = (bf16[2,3,512,256]{3,2,1,0:T(8,128)(2,1)S(1)}, bf16[2,3,512,256]{3,2,1,0:T(8,128)(2,1)S(1)}, u32[]{:S(2)}, u32[]{:S(2)}) collective-permute-start(bf16[2,3,512,256]{3,2,1,0:T(8,128)(2,1)S(1)} %copy-done), channel_id=1, source_target_pairs={{0,1},{1,0},{2,3},{3,2},{4,5},{5,4},{6,7},{7,6},{8,9},{9,8},{10,11... | collective-permute-start | bytes 4718600 | tf_op jit(solution)/shard_map/ppermute | solution.py:18
  2.0 7.1 %collective-permute-start.5 = (bf16[2,64,256]{2,1,0:T(8,128)(2,1)S(1)}, bf16[2,64,256]{2,1,0:T(8,128)(2,1)S(1)}, u32[]{:S(2)}, u32[]{:S(2)}) collective-permute-start(bf16[2,64,256]{2,1,0:T(8,128)(2,1)S(1)} %pad_maximum_fusion.own_ref), channel_id=1, source_target_pairs={{8,0},{7,1},{10,2},{9,3},{12,4},{11,5},{14,6},{13,7},{0,8},{15,9},... | collective-permute-start | bytes 196616 | tf_op jit(solution)/shard_map/ppermute | solution.py:27
  6.1 3.6 %collective-permute-start.3 = (bf16[2,64,256]{2,1,0:T(8,128)(2,1)S(1)}, bf16[2,64,256]{2,1,0:T(8,128)(2,1)S(1)}, u32[]{:S(2)}, u32[]{:S(2)}) collective-permute-start(bf16[2,64,256]{2,1,0:T(8,128)(2,1)S(1)} %pad_maximum_fusion.own_ref), channel_id=1, source_target_pairs={{1,0},{3,1},{0,2},{5,3},{2,4},{7,5},{4,6},{9,7},{6,8},{11,9},{8,10... | collective-permute-start | bytes 196616 | tf_op jit(solution)/shard_map/ppermute | solution.py:36
  7.6 3.5 %collective-permute-start.1 = (bf16[2,64,256]{2,1,0:T(8,128)(2,1)S(1)}, bf16[2,64,256]{2,1,0:T(8,128)(2,1)S(1)}, u32[]{:S(2)}, u32[]{:S(2)}) collective-permute-start(bf16[2,64,256]{2,1,0:T(8,128)(2,1)S(1)} %pad_maximum_fusion.own_ref), channel_id=1, source_target_pairs={{1,0},{5,1},{3,2},{7,3},{0,4},{9,5},{2,6},{11,7},{4,8},{13,9},{6,1... | collective-permute-start | bytes 196616 | tf_op jit(solution)/shard_map/ppermute | solution.py:36
  9.2 3.0 %collective-permute-start.8 = (bf16[288,128]{1,0:T(8,128)(2,1)S(1)}, bf16[288,128]{1,0:T(8,128)(2,1)S(1)}, u32[]{:S(2)}, u32[]{:S(2)}) collective-permute-start(bf16[288,128]{1,0:T(8,128)(2,1)S(1)} %get-tuple-element.21.own_ref), channel_id=1, source_target_pairs={{0,1},{1,0},{2,3},{3,2},{4,5},{5,4},{6,7},{7,6},{8,9},{9,8},{10,11... | collective-permute-start | bytes 221192 | tf_op jit(solution)/shard_map/ppermute | solution.py:18
  9.2 3.6 %collective-permute-start.6 = (bf16[2,64,256]{2,1,0:T(8,128)(2,1)S(1)}, bf16[2,64,256]{2,1,0:T(8,128)(2,1)S(1)}, u32[]{:S(2)}, u32[]{:S(2)}) collective-permute-start(bf16[2,64,256]{2,1,0:T(8,128)(2,1)S(1)} %collective-permute-done.5.r3_ref), channel_id=1, source_target_pairs={{0,1},{1,0},{2,3},{3,2},{4,5},{5,4},{6,7},{7,6},{8,9},{9,8},{10,11... | collective-permute-start | bytes 196616 | tf_op jit(solution)/shard_map/ppermute | solution.py:18
  9.7 3.1 %collective-permute-start.4 = (bf16[2,64,256]{2,1,0:T(8,128)(2,1)S(1)}, bf16[2,64,256]{2,1,0:T(8,128)(2,1)S(1)}, u32[]{:S(2)}, u32[]{:S(2)}) collective-permute-start(bf16[2,64,256]{2,1,0:T(8,128)(2,1)S(1)} %collective-permute-done.3.r1_ref), channel_id=1, source_target_pairs={{0,1},{1,0},{2,3},{3,2},{4,5},{5,4},{6,7},{7,6},{8,9},{9,8},{10,11... | collective-permute-start | bytes 196616 | tf_op jit(solution)/shard_map/ppermute | solution.py:18
  11.1 1.7 %collective-permute-start.2 = (bf16[2,64,256]{2,1,0:T(8,128)(2,1)S(1)}, bf16[2,64,256]{2,1,0:T(8,128)(2,1)S(1)}, u32[]{:S(2)}, u32[]{:S(2)}) collective-permute-start(bf16[2,64,256]{2,1,0:T(8,128)(2,1)S(1)} %collective-permute-done.1.r2_ref), channel_id=1, source_target_pairs={{0,1},{1,0},{2,3},{3,2},{4,5},{5,4},{6,7},{7,6},{8,9},{9,8},{10,11... | collective-permute-start | bytes 196616 | tf_op jit(solution)/shard_map/ppermute | solution.py:18

commit v4 on v3

--- a/solution.py
+++ b/solution.py
@@ -18,15 +18,6 @@
     return lax.ppermute(value, "chan", [(0, 1), (1, 0)])
 
 
-def ring_permute(value, offset_0, offset_1):
-    count = lax.axis_size("blk")
-    pairs = []
-    for i in range(count):
-        pairs.append((((i + offset_0) % count) * 2, i * 2))
-        pairs.append((((i + offset_1) % count) * 2 + 1, i * 2 + 1))
-    return lax.ppermute(value, ("blk", "chan"), pairs)
-
-
 def line_permute(value, step):
     count = lax.axis_size("blk")
     pairs = []
@@ -36,15 +27,20 @@
     return lax.ppermute(value, ("blk", "chan"), pairs)
 
 
+def front_kernel(own_any, own_ref, sem):
+    copy = pltpu.make_async_copy(own_any, own_ref, sem)
+    copy.start()
+    copy.wait()
+
+
 def pack_kernel(
-    own_any,
+    after_any,
     mask_any,
     mw_any,
     mb_any,
     hw_any,
     cb_any,
     pb_any,
-    own_ref,
     mask_ref,
     packed_ref,
     small_ref,
@@ -63,7 +59,6 @@
         (hw_any, hw_s),
         (pb_any, pb_s),
         (mask_any, mask_ref),
-        (own_any, own_ref),
     )
     copies = [
         pltpu.make_async_copy(source, target, sems.at[at])
@@ -101,7 +96,6 @@
     own_ref,
     oth_ref,
     col_mask_ref,
-    valid_ref,
     wbig_ref,
     side_ref,
     head_ref,
@@ -109,15 +103,12 @@
     taps_s,
 ):
     half = own_ref.shape[0] // 9
-    rows = valid_ref.shape[0]
     columns = col_mask_ref.shape[1]
     bins = columns // 2
-    col_rows = columns + 2 * HALO
     count = lax.axis_size("blk")
     i = lax.axis_index("blk")
     c = lax.axis_index("chan")
-    first = i * bins
-    first_col = first + c * columns
+    first_col = i * bins + c * columns
     length = length_ref[0]
 
     for source, side in ((own_ref, c), (oth_ref, 1 - c)):
@@ -153,15 +144,6 @@
         q == 2 * ((k % (4 * F2)) // F2) + k // (4 * F2), spread(9, 8), 0.0
     ).astype(BF16)
     side_ref[0:1, :] = spread(8, 4)[:1]
-    other = oth_ref[:16, :].astype(F32)
-    other = pltpu.roll(other, F2, axis=1)
-    for layer in range(CONV1):
-        for quarter in range(4):
-            at = 4 * layer + quarter
-            side_ref[1 + layer : 2 + layer, quarter * F2 : (quarter + 1) * F2] = other[
-                at : at + 1, :F2
-            ]
-
     minus = F32(-jnp.inf)
     block = lax.broadcasted_iota(jnp.int32, (BAND + 1, count), 1)
 
@@ -195,53 +177,41 @@
         col_mask_ref[at, :, 2 * F2 : 4 * F2] = jnp.where(low, masks[v0, 2], masks[v1, 0])
         col_mask_ref[at, :, 4 * F2 :] = jnp.where(low, masks[v1, 1], masks[v1, 2])
 
-    place = lax.broadcasted_iota(jnp.int32, (rows, 2 * F2), 0)
-    bin_index = jnp.where(
-        place < col_rows, first_col - HALO + place, first - HALO - col_rows + place
-    )
-    valid_ref[...] = jnp.where((bin_index >= 0) & (bin_index < length), 1.0, 0.0)
-
-    side_ref[3:4, : 2 * F2] = jnp.where(
+    side_ref[1:2, : 2 * F2] = jnp.where(
         live_at(lax.broadcasted_iota(jnp.int32, (1, columns), 1), 0), 1.0, 0.0
     )
 
 
-def contact_kernel(
+def trunk_kernel(
+    length_ref,
     own_ref,
     r2_ref,
     s2_ref,
     r1_ref,
     s1_ref,
-    r3_ref,
-    s3_ref,
     w_own_ref,
     pw_ref,
     w_oth_ref,
     small_ref,
-    col_mask_ref,
-    valid_ref,
-    wbig_ref,
-    side_ref,
-    head_ref,
-    out_ref,
+    oth_ref,
+    cols_ref,
+    rows_ref,
     h_s,
-    pa6_s,
-    x_s,
-    mix_s,
+    bias_s,
 ):
     bins = own_ref.shape[1]
     half = own_ref.shape[2]
-    col_rows = 2 * bins + 2 * HALO
-    row_rows = bins + 2 * HALO
-    rows = col_rows + row_rows
+    rows = cols_ref.shape[0]
+    row_rows = rows_ref.shape[0]
     count = lax.axis_size("blk")
     i = lax.axis_index("blk")
     c = lax.axis_index("chan")
-    first = i * bins
-    first_col = first + c * (2 * bins)
+    bin_index = i * bins - HALO + lax.broadcasted_iota(jnp.int32, (rows, 2 * F2), 0)
+    valid = (bin_index >= 0) & (bin_index < length_ref[0])
+    inside = ((bin_index >= 0) & (bin_index < count * bins))[:, :1]
 
     def put(start, number, ref, source, swapped=0):
-        keep = valid_ref[start : start + number, :] != 0
+        keep = valid[start : start + number, :]
         for part in range(2):
             held = lax.rem(part + c + swapped, 2)
             for at in range(0, half, 128):
@@ -250,30 +220,25 @@
                 )
 
     tail = bins - HALO
-    put(0, HALO, r1_ref, tail)
-    put(col_rows + HALO, bins, own_ref, 0)
+    put(HALO, bins, own_ref, 0)
 
     @pl.when(c == 0)
     def _():
-        put(HALO, bins, own_ref, 0)
+        put(0, HALO, r1_ref, tail)
         put(HALO + bins, bins, s1_ref, 0, 1)
         put(HALO + 2 * bins, HALO, s2_ref, 0, 1)
-        put(col_rows, HALO, r1_ref, tail)
-        put(col_rows + HALO + bins, HALO, s1_ref, 0, 1)
 
     @pl.when(c == 1)
     def _():
-        put(HALO, bins, r2_ref, 0)
-        put(HALO + bins, bins, r3_ref, 0)
-        put(HALO + 2 * bins, HALO, s3_ref, 0, 1)
-        put(col_rows, HALO, s1_ref, tail, 1)
-        put(col_rows + HALO + bins, HALO, r1_ref, 0)
-
-    place = lax.broadcasted_iota(jnp.int32, (rows, 1), 0)
-    bin_index = jnp.where(
-        place < col_rows, first_col - HALO + place, first - HALO - col_rows + place
-    )
-    inside = (bin_index >= 0) & (bin_index < count * bins)
+        put(0, HALO, s1_ref, tail, 1)
+        put(HALO + bins, bins, r1_ref, 0)
+        put(HALO + 2 * bins, HALO, r2_ref, 0)
+
+    other = pltpu.roll(oth_ref[:16, :].astype(F32), F2, axis=1)
+    for layer in range(CONV1):
+        for quarter in range(4):
+            at = 4 * layer + quarter
+            bias_s[layer : layer + 1, quarter * F2 : (quarter + 1) * F2] = other[at : at + 1, :F2]
 
     for layer in range(CONV1):
         e = 2 ** (layer + 1)
@@ -282,22 +247,48 @@
             (hidden if t == 1 else pltpu.roll(hidden, ((1 - t) * e) % rows, axis=0)).astype(BF16)
             for t in range(3)
         ]
-        for at, (w_ref, side) in enumerate(((w_own_ref, c), (w_oth_ref, 1 - c))):
+        for w_ref, bias_ref, side in (
+            (w_own_ref, small_ref, c),
+            (w_oth_ref, bias_s, 1 - c),
+        ):
             q = jnp.dot(taps[0], w_ref[layer, 0], preferred_element_type=F32)
             q = q + jnp.dot(taps[1], w_ref[layer, 1], preferred_element_type=F32)
             q = q + jnp.dot(taps[2], w_ref[layer, 2], preferred_element_type=F32)
             lanes = pl.ds(pl.multiple_of(side * half, half), half)
-            bias = side_ref[1 + layer : 2 + layer, :] if at else small_ref[layer : layer + 1, :]
+            bias = bias_ref[layer : layer + 1, :]
             new = (h_s[:, lanes] + jnp.maximum(q + bias, 0.0)).astype(BF16).astype(F32)
             h_s[:, lanes] = jnp.where(inside, new, 0.0)
 
     proj = jnp.dot(h_s[...].astype(BF16), pw_ref[...], preferred_element_type=F32)
     proj = (proj + small_ref[2:3, : 2 * F2]).astype(BF16).astype(F32)
-
-    minus = F32(-jnp.inf)
     low = lax.broadcasted_iota(jnp.int32, (1, 2 * F2), 1) < F2
-    pcol = proj[:col_rows]
-    pcol = jnp.where(low, pltpu.roll(pcol, F2, axis=1), pcol)
+    turned = pltpu.roll(proj, F2, axis=1)
+    cols_ref[...] = jnp.where(low, turned, proj).astype(BF16)
+    rows_ref[...] = jnp.where(valid, jnp.where(low, proj, turned), -jnp.inf)[:row_rows]
+
+
+def contact_kernel(
+    length_ref,
+    cols_own_ref,
+    cols_far_ref,
+    rows_ref,
+    col_mask_ref,
+    wbig_ref,
+    side_ref,
+    head_ref,
+    out_ref,
+    pa6_s,
+    x_s,
+    mix_s,
+):
+    bins = out_ref.shape[0]
+    col_rows = cols_own_ref.shape[0]
+    row_rows = rows_ref.shape[0]
+    i = lax.axis_index("blk")
+    c = lax.axis_index("chan")
+
+    low = lax.broadcasted_iota(jnp.int32, (1, 2 * F2), 1) < F2
+    pcol = jnp.where(c == 0, cols_own_ref[...].astype(F32), cols_far_ref[...].astype(F32))
     shifted = [
         pltpu.roll(pcol, col_rows - HALO - (r - 1) * D2, axis=0)[: 2 * bins] for r in range(3)
     ]
@@ -313,9 +304,7 @@
     ]
     col_centre = shifted[1].astype(BF16).reshape(2 * bins // 16, 16, 2 * F2)
 
-    prow = proj[col_rows:]
-    prow = jnp.where(low, prow, pltpu.roll(prow, F2, axis=1))
-    prow = jnp.where(valid_ref[col_rows:, :] != 0, prow, minus)
+    prow = rows_ref[...]
     prow_next = pltpu.roll(prow, row_rows - D2, axis=0)
     pa6_s[:, : 2 * F2] = prow
     pa6_s[:, 2 * F2 : 4 * F2] = jnp.where(low, prow, prow_next)
@@ -352,14 +341,14 @@
                 mixed = y[at_row : at_row + 2 * bins] + centre
                 mix_s[group, :, v * 4 * F2 : (v + 1) * 4 * F2] = mixed.astype(BF16)
 
-    lane_live = side_ref[3:4, : 2 * F2] != 0
+    lane_live = side_ref[1:2, : 2 * F2] != 0
     for group in range(groups):
         value = lax.dot_general(
             head_ref[...], mix_s[group], (((1,), (1,)), ((), ())), preferred_element_type=F32
         )[:8]
-        at = col_rows + HALO + 8 * group
+        bin_index = i * bins + 8 * group + lax.broadcasted_iota(jnp.int32, (8, 2 * bins), 0)
         out_ref[8 * group : 8 * group + 8, :] = jnp.where(
-            lane_live & (valid_ref[at : at + 8, :] != 0), value, 0.0
+            lane_live & (bin_index < length_ref[0]), value, 0.0
         )
 
 
@@ -376,7 +365,7 @@
     head_weight,
 ):
     bins, half = features.shape
-    rows = 3 * bins + 4 * HALO
+    rows = 2 * bins + 2 * HALO
     half_out = map_bias.shape[0]
     smem = pl.BlockSpec(memory_space=pltpu.SMEM)
     vmem = pl.BlockSpec(memory_space=pltpu.VMEM)
@@ -387,16 +376,25 @@
         return pltpu.with_memory_space_constraint(value, pltpu.HBM)
 
     other = chan_swap(features)
-    own, mask, packed, small = pl.pallas_call(
+    own = pl.pallas_call(
+        front_kernel,
+        out_shape=jax.ShapeDtypeStruct(features.shape, BF16),
+        in_specs=[anywhere],
+        out_specs=vmem,
+        scratch_shapes=[pltpu.SemaphoreType.DMA],
+        cost_estimate=pl.CostEstimate(flops=4000000000, bytes_accessed=1000000, transcendentals=0),
+        compiler_params=params,
+    )(in_hbm(features))
+    own = jnp.stack([own, other])
+    mask, packed, small = pl.pallas_call(
         pack_kernel,
         out_shape=[
-            jax.ShapeDtypeStruct(features.shape, BF16),
             jax.ShapeDtypeStruct(band_mask.shape[::-1], jnp.int32),
             jax.ShapeDtypeStruct((9 * half_out, 2 * F2), BF16),
             jax.ShapeDtypeStruct((8, half), F32),
         ],
         in_specs=[anywhere] * 7,
-        out_specs=[vmem] * 4,
+        out_specs=[vmem] * 3,
         scratch_shapes=[
             pltpu.VMEM(map_weight.shape, BF16),
             pltpu.VMEM((1, half_out), BF16),
@@ -404,12 +402,11 @@
             pltpu.VMEM(conv_bias.shape, BF16),
             pltpu.VMEM((1, 2 * F2), BF16),
             pltpu.VMEM((32, 2 * F2), F32),
-            pltpu.SemaphoreType.DMA((7,)),
-        ],
-        cost_estimate=pl.CostEstimate(flops=4000000000, bytes_accessed=1000000, transcendentals=0),
+            pltpu.SemaphoreType.DMA((6,)),
+        ],
         compiler_params=params,
     )(
-        in_hbm(features),
+        own,
         in_hbm(band_mask.T),
         in_hbm(map_weight),
         in_hbm(map_bias[None]),
@@ -417,58 +414,57 @@
         in_hbm(conv_bias),
         in_hbm(proj_bias[None]),
     )
-    own = jnp.stack([own, other])
     r1 = line_permute(own, 1)
-    r2 = line_permute(own, 2)
-    r3 = ring_permute(own, 4, 3)
+    r2 = line_permute(own[:, :HALO], 2)
+    r1, r2 = lax.optimization_barrier((r1, r2))
     s1 = chan_swap(r1)
     s2 = chan_swap(r2)
-    s3 = chan_swap(r3)
     w_in, own = lax.optimization_barrier((conv_weight, own))
     w_oth = chan_swap(w_in)
+    oth = chan_swap(packed)
+    cols, row_features = pl.pallas_call(
+        trunk_kernel,
+        out_shape=[
+            jax.ShapeDtypeStruct((rows, 2 * F2), BF16),
+            jax.ShapeDtypeStruct((bins + 2 * HALO, 2 * F2), F32),
+        ],
+        in_specs=[smem] + [vmem] * 10,
+        out_specs=[vmem] * 2,
+        scratch_shapes=[
+            pltpu.VMEM((rows, 2 * half), F32),
+            pltpu.VMEM((8, half), F32),
+        ],
+        compiler_params=params,
+    )(chrom_len, own, r2, s2, r1, s1, conv_weight, proj_weight, w_oth, small, oth)
+    cols_far = line_permute(cols, 2)
     prepared = pl.pallas_call(
         prep_kernel,
         out_shape=[
             jax.ShapeDtypeStruct((3, 2 * bins, 6 * F2), F32),
-            jax.ShapeDtypeStruct((rows, 2 * F2), F32),
             jax.ShapeDtypeStruct((18 * F2, 4 * F2), BF16),
             jax.ShapeDtypeStruct((8, half), F32),
             jax.ShapeDtypeStruct((16, 8 * F2), BF16),
         ],
         in_specs=[smem] + [vmem] * 3,
-        out_specs=[vmem] * 5,
+        out_specs=[vmem] * 4,
         scratch_shapes=[
             pltpu.VMEM((4 * F2, 18 * F2), F32),
             pltpu.VMEM((9, F2, F2), F32),
         ],
         compiler_params=params,
-    )(chrom_len, mask, packed, chan_swap(packed))
+    )(chrom_len, mask, packed, oth)
     return pl.pallas_call(
         contact_kernel,
         out_shape=jax.ShapeDtypeStruct((bins, 2 * bins), F32),
-        in_specs=[vmem] * 16,
+        in_specs=[smem] + [vmem] * 7,
         out_specs=vmem,
         scratch_shapes=[
-            pltpu.VMEM((rows, 2 * half), F32),
             pltpu.VMEM((bins + 2 * HALO, 6 * F2), F32),
             pltpu.VMEM((4 * 2 * bins, 18 * F2), BF16),
             pltpu.VMEM((bins // 8, 2 * bins, 8 * F2), BF16),
         ],
         compiler_params=params,
-    )(
-        own,
-        r2,
-        s2,
-        r1,
-        s1,
-        r3,
-        s3,
-        conv_weight,
-        proj_weight,
-        w_oth,
-        small,
-        *prepared,
-    )
+    )(chrom_len, cols, cols_far, row_features, *prepared)
 
 
 def solution(mesh):

time: 17.3 us -> 17.2 us (level)
  starting transfers between devices: 8.78 us -> 7.91 us
  waiting for transfers between devices: 1.23 us -> 1.98 us
  local copies, waits for them, and re-layouts: 0.27 us -> 0.01 us
  Pallas kernels: 6.16 us -> 6.37 us
    ppermute x1 -> x0, starting transfers between devices: 4.04 us -> none  [ring_permute(): return lax.ppermute(value, ('blk', 'chan'), pairs)]
    ppermute x2 -> x3, starting transfers between devices: 3.07 us -> 6.46 us  [line_permute(): return lax.ppermute(value, ('blk', 'chan'), pairs)]
    pallas_call x1 -> x3, Pallas kernels: 1.23 us -> 3.22 us  [the longest x1 1.31 us: local(): pl.pallas_call(trunk_kernel, out_shape=[jax.ShapeDtypeStruct((rows, 2 * F...]
    pallas_call x1, Pallas kernels: 4.38 us -> 2.69 us  [local(): pl.pallas_call(contact_kernel, out_shape=jax.ShapeDtypeStruct((bins, 2 *...]
    ppermute x6 -> x5, waiting for transfers between devices: 0.02 us -> 0.5 us  [chan_swap(): return lax.ppermute(value, 'chan', [(0, 1), (1, 0)])]
    ppermute x2 -> x3, waiting for transfers between devices: 1.21 us -> 1.47 us  [line_permute(): return lax.ppermute(value, ('blk', 'chan'), pairs)]
    unnamed x4, local copies, waits for them, and re-layouts: 0.27 us -> 0.01 us
    ppermute x6 -> x5, starting transfers between devices: 1.68 us -> 1.45 us  [chan_swap(): return lax.ppermute(value, 'chan', [(0, 1), (1, 0)])]
  transfers between devices with their start and end apart: 9 -> 8, of which waited for: 1 -> 4; matrix products, arithmetic and copies ran while one was open for 0% -> 0% of each run, Pallas kernels for 10% -> 14%
where the time goes in v4:
time: 17.2 us; the launch traced here: 17 us
  starting transfers between devices  7.91 us (46%)
  Pallas kernels  6.37 us (37%)
  waiting for transfers between devices  1.98 us (12%)
  between operations  0.71 us (4%)
    ppermute x3, starting transfers between devices, line_permute(): return lax.ppermute(value, ('blk', 'chan'), pairs)  6.46 us
    pallas_call x1, Pallas kernels, local(): pl.pallas_call(contact_kernel, out_shape=jax.ShapeDtypeStruct((bins, 2 *...  2.69 us
    ppermute x3, waiting for transfers between devices, line_permute(): return lax.ppermute(value, ('blk', 'chan'), pairs)  1.47 us
    ppermute x5, starting transfers between devices, chan_swap(): return lax.ppermute(value, 'chan', [(0, 1), (1, 0)])  1.45 us
    pallas_call x1, Pallas kernels, local(): pl.pallas_call(trunk_kernel, out_shape=[jax.ShapeDtypeStruct((rows, 2 * F...  1.31 us
    pallas_call x1, Pallas kernels, local(): pl.pallas_call(pack_kernel, out_shape=[jax.ShapeDtypeStruct(band_mask.sha...  1.09 us
    pallas_call x1, Pallas kernels, local(): pl.pallas_call(front_kernel, out_shape=jax.ShapeDtypeStruct(features.shap...  0.82 us
    ppermute x5, waiting for transfers between devices, chan_swap(): return lax.ppermute(value, 'chan', [(0, 1), (1, 0)])  0.5 us
  transfers between devices with their start and end apart: 8, of which 4 were waited for; matrix products, arithmetic and copies ran while one was open for 0% of the time, Pallas kernels for 14%

profile of v4, /device:TPU:0, one launch (start us, length us, event | category | flops | bytes accessed | tf_op | source)
XLA Modules:
  0.0 17.0 jit_solution(11701678619383259567)
XLA Ops:
  0.0 0.0 copy-start
  0.0 0.0 copy-start.1
  0.0 0.5 %collective-permute-start = (bf16[64,256]{1,0:T(8,128)(2,1)}, bf16[64,256]{1,0:T(8,128)(2,1)S(1)}, u32[]{:S(2)}, u32[]{:S(2)}) collective-permute-start(bf16[64,256]{1,0:T(8,128)(2,1)} %own_any.1), channel_id=1, source_target_pairs={{0,1},{1,0},{2,3},{3,2},{4,5},{5,4},{6,7},{7,6},{8,9},{9,8},{10,11... | collective-permute-start | bytes 98312 | tf_op jit(solution)/shard_map/ppermute | solution.py:18
  0.5 0.8 %shard_map.100 = bf16[64,256]{1,0:T(8,128)(2,1)S(1)} custom-call(bf16[64,256]{1,0:T(8,128)(2,1)} %own_any.1), custom_call_target="tpu_custom_call" | custom-call | flops 4000000000 | bytes 1000000 | tf_op jit(solution)/shard_map/pallas_call | solution.py:379
  1.3 0.2 %collective-permute-done = bf16[64,256]{1,0:T(8,128)(2,1)S(1)} collective-permute-done((bf16[64,256]{1,0:T(8,128)(2,1)}, bf16[64,256]{1,0:T(8,128)(2,1)S(1)}, u32[]{:S(2)}, u32[]{:S(2)}) %collective-permute-start) | collective-permute-done | bytes 32800 | tf_op jit(solution)/shard_map/ppermute | solution.py:18
  1.5 0.0 copy-done
  1.5 0.4 %collective-permute-start.5 = (bf16[2,3,512,256]{3,2,1,0:T(8,128)(2,1)S(1)}, bf16[2,3,512,256]{3,2,1,0:T(8,128)(2,1)S(1)}, u32[]{:S(2)}, u32[]{:S(2)}) collective-permute-start(bf16[2,3,512,256]{3,2,1,0:T(8,128)(2,1)S(1)} %copy-done), channel_id=1, source_target_pairs={{0,1},{1,0},{2,3},{3,2},{4,5},{5,4},{6,7},{7,6},{8,9},{9,8},{10,11... | collective-permute-start | bytes 4718600 | tf_op jit(solution)/shard_map/ppermute | solution.py:18
  2.0 2.6 %collective-permute-start.1 = (bf16[2,64,256]{2,1,0:T(8,128)(2,1)S(1)}, bf16[2,64,256]{2,1,0:T(8,128)(2,1)S(1)}, u32[]{:S(2)}, u32[]{:S(2)}) collective-permute-start(bf16[2,64,256]{2,1,0:T(8,128)(2,1)S(1)} %pad_maximum_fusion.after_any.own_ref), channel_id=1, source_target_pairs={{1,0},{3,1},{0,2},{5,3},{2,4},{7,5},{4,6},{9,7},{6,8},{11,9},{8,10... | collective-permute-start | bytes 196616 | tf_op jit(solution)/shard_map/ppermute | solution.py:27
  4.6 1.6 %collective-permute-start.2 = (bf16[2,16,256]{2,1,0:T(8,128)(2,1)S(1)}, bf16[2,16,256]{2,1,0:T(8,128)(2,1)S(1)}, u32[]{:S(2)}, u32[]{:S(2)}) collective-permute-start(bf16[2,16,256]{2,1,0:T(8,128)(2,1)S(1)} %fusion), channel_id=1, source_target_pairs={{1,0},{5,1},{3,2},{7,3},{0,4},{9,5},{2,6},{11,7},{4,8},{13,9},{6,1... | collective-permute-start | bytes 49160 | tf_op jit(solution)/shard_map/ppermute | solution.py:27
  6.2 1.1 %shard_map.101 = (s32[4,8]{1,0:T(4,128)S(1)}, bf16[288,128]{1,0:T(8,128)(2,1)S(1)}, f32[8,256]{1,0:T(8,128)S(1)}) custom-call(bf16[2,64,256]{2,1,0:T(8,128)(2,1)S(1)} %pad_maximum_fusion.after_any.own_ref, s32[4,8]{1,0:T(4,128)} %bitcast.10, bf16[3,3,32,64]{3,2,1,0:T(8,128)(2,1)} %mw_any.1, bf16[1,32]{1,0:T(2,128)(2,1)} %bitcast.11, bf16[1,32]{1,0:T(2,128)(2,1)} %bitcast.12, ...), custom_call_target="tpu_custom_call" | custom-call | tf_op jit(solution)/shard_map/pallas_call | solution.py:389
  7.3 0.1 collective-permute-start.6
  7.4 0.3 %collective-permute-done.2.r2_ref = bf16[2,16,256]{2,1,0:T(8,128)(2,1)S(1)} collective-permute-done((bf16[2,16,256]{2,1,0:T(8,128)(2,1)S(1)}, bf16[2,16,256]{2,1,0:T(8,128)(2,1)S(1)}, u32[]{:S(2)}, u32[]{:S(2)}) %collective-permute-start.2) | collective-permute-done | bytes 16416 | tf_op jit(solution)/shard_map/ppermute | solution.py:27
  7.6 0.0 collective-permute-done.1.r1_ref
  7.6 0.2 %collective-permute-start.4 = (bf16[2,64,256]{2,1,0:T(8,128)(2,1)S(1)}, bf16[2,64,256]{2,1,0:T(8,128)(2,1)S(1)}, u32[]{:S(2)}, u32[]{:S(2)}) collective-permute-start(bf16[2,64,256]{2,1,0:T(8,128)(2,1)S(1)} %collective-permute-done.1.r1_ref), channel_id=1, source_target_pairs={{0,1},{1,0},{2,3},{3,2},{4,5},{5,4},{6,7},{7,6},{8,9},{9,8},{10,11... | collective-permute-start | bytes 196616 | tf_op jit(solution)/shard_map/ppermute | solution.py:18
  7.9 0.3 %collective-permute-start.3 = (bf16[2,16,256]{2,1,0:T(8,128)(2,1)S(1)}, bf16[2,16,256]{2,1,0:T(8,128)(2,1)S(1)}, u32[]{:S(2)}, u32[]{:S(2)}) collective-permute-start(bf16[2,16,256]{2,1,0:T(8,128)(2,1)S(1)} %collective-permute-done.2.r2_ref), channel_id=1, source_target_pairs={{0,1},{1,0},{2,3},{3,2},{4,5},{5,4},{6,7},{7,6},{8,9},{9,8},{10,11... | collective-permute-start | bytes 49160 | tf_op jit(solution)/shard_map/ppermute | solution.py:18
  8.8 0.0 collective-permute-done.6.oth_ref
  8.8 0.2 %collective-permute-done.3.s2_ref = bf16[2,16,256]{2,1,0:T(8,128)(2,1)S(1)} collective-permute-done((bf16[2,16,256]{2,1,0:T(8,128)(2,1)S(1)}, bf16[2,16,256]{2,1,0:T(8,128)(2,1)S(1)}, u32[]{:S(2)}, u32[]{:S(2)}) %collective-permute-start.3) | collective-permute-done | bytes 16416 | tf_op jit(solution)/shard_map/ppermute | solution.py:18
  9.1 0.0 collective-permute-done.4.s1_ref
  9.1 0.0 collective-permute-done.5.w_oth_ref
  9.1 0.0 copy-done.1
  9.1 1.3 %shard_map.102 = (bf16[160,128]{1,0:T(8,128)(2,1)S(1)}, f32[96,128]{1,0:T(8,128)S(1)}) custom-call(s32[1]{0:T(128)S(6)} %copy.11.length_ref, bf16[2,64,256]{2,1,0:T(8,128)(2,1)S(1)} %pad_maximum_fusion.after_any.own_ref, bf16[2,16,256]{2,1,0:T(8,128)(2,1)S(1)} %collective-permute-done.2.r2_ref, bf16[2,16,256]{2,1,0:T(8,128)(2,1)S(1)} %collective-permute-done.3.s2_ref, ...), custom_call_target="tpu_custom_call" | custom-call | tf_op jit(solution)/shard_map/pallas_call | solution.py:425
  10.4 2.2 %collective-permute-start.7 = (bf16[160,128]{1,0:T(8,128)(2,1)S(1)}, bf16[160,128]{1,0:T(8,128)(2,1)S(1)}, u32[]{:S(2)}, u32[]{:S(2)}) collective-permute-start(bf16[160,128]{1,0:T(8,128)(2,1)S(1)} %get-tuple-element.24.cols_own_ref), channel_id=1, source_target_pairs={{1,0},{5,1},{3,2},{7,3},{0,4},{9,5},{2,6},{11,7},{4,8},{13,9},{6,1... | collective-permute-start | bytes 122888 | tf_op jit(solution)/shard_map/ppermute | solution.py:27
  12.6 0.5 %shard_map.103 = (f32[3,128,384]{2,1,0:T(8,128)S(1)}, bf16[1152,256]{1,0:T(8,128)(2,1)S(1)}, f32[8,256]{1,0:T(8,128)S(1)}, bf16[16,512]{1,0:T(8,128)(2,1)S(1)}) custom-call(s32[1]{0:T(128)S(6)} %copy.11.length_ref, s32[4,8]{1,0:T(4,128)S(1)} %get-tuple-element.26.mask_ref, bf16[288,128]{1,0:T(8,128)(2,1)S(1)} %get-tuple-element.23.own_ref, ...), custom_call_target="tpu_custom_call" | custom-call | tf_op jit(solution)/shard_map/pallas_call | solution.py:440
  13.1 1.2 %collective-permute-done.7.cols_far_ref = bf16[160,128]{1,0:T(8,128)(2,1)S(1)} collective-permute-done((bf16[160,128]{1,0:T(8,128)(2,1)S(1)}, bf16[160,128]{1,0:T(8,128)(2,1)S(1)}, u32[]{:S(2)}, u32[]{:S(2)}) %collective-permute-start.7) | collective-permute-done | bytes 40992 | tf_op jit(solution)/shard_map/ppermute | solution.py:27
  14.3 2.7 %shard_map.104 = f32[64,128]{1,0:T(8,128)} custom-call(s32[1]{0:T(128)S(6)} %copy.11.length_ref, bf16[160,128]{1,0:T(8,128)(2,1)S(1)} %get-tuple-element.24.cols_own_ref, bf16[160,128]{1,0:T(8,128)(2,1)S(1)} %collective-permute-done.7.cols_far_ref, f32[96,128]{1,0:T(8,128)S(1)} %get-tuple-element.25.rows_ref, ...), custom_call_target="tpu_custom_call" | custom-call | tf_op jit(solution)/shard_map/pallas_call | solution.py:456
  (2 shorter events, 0.0 us)
Async XLA Ops:
  0.0 1.5 %copy-start = (bf16[2,3,512,256]{3,2,1,0:T(8,128)(2,1)S(1)}, bf16[2,3,512,256]{3,2,1,0:T(8,128)(2,1)}, u32[]{:S(2)}) copy-start(bf16[2,3,512,256]{3,2,1,0:T(8,128)(2,1)} %w_own_ref.1) | copy-start | bytes 4718596
  0.0 9.1 %copy-start.1 = (bf16[512,128]{1,0:T(8,128)(2,1)S(1)}, bf16[512,128]{1,0:T(8,128)(2,1)}, u32[]{:S(2)}) copy-start(bf16[512,128]{1,0:T(8,128)(2,1)} %pw_ref.1) | copy-start | bytes 393220
  0.0 1.5 %collective-permute-start = (bf16[64,256]{1,0:T(8,128)(2,1)}, bf16[64,256]{1,0:T(8,128)(2,1)S(1)}, u32[]{:S(2)}, u32[]{:S(2)}) collective-permute-start(bf16[64,256]{1,0:T(8,128)(2,1)} %own_any.1), channel_id=1, source_target_pairs={{0,1},{1,0},{2,3},{3,2},{4,5},{5,4},{6,7},{7,6},{8,9},{9,8},{10,11... | collective-permute-start | bytes 98312 | tf_op jit(solution)/shard_map/ppermute | solution.py:18
  1.5 7.5 %collective-permute-start.5 = (bf16[2,3,512,256]{3,2,1,0:T(8,128)(2,1)S(1)}, bf16[2,3,512,256]{3,2,1,0:T(8,128)(2,1)S(1)}, u32[]{:S(2)}, u32[]{:S(2)}) collective-permute-start(bf16[2,3,512,256]{3,2,1,0:T(8,128)(2,1)S(1)} %copy-done), channel_id=1, source_target_pairs={{0,1},{1,0},{2,3},{3,2},{4,5},{5,4},{6,7},{7,6},{8,9},{9,8},{10,11... | collective-permute-start | bytes 4718600 | tf_op jit(solution)/shard_map/ppermute | solution.py:18
  2.0 5.7 %collective-permute-start.1 = (bf16[2,64,256]{2,1,0:T(8,128)(2,1)S(1)}, bf16[2,64,256]{2,1,0:T(8,128)(2,1)S(1)}, u32[]{:S(2)}, u32[]{:S(2)}) collective-permute-start(bf16[2,64,256]{2,1,0:T(8,128)(2,1)S(1)} %pad_maximum_fusion.after_any.own_ref), channel_id=1, source_target_pairs={{1,0},{3,1},{0,2},{5,3},{2,4},{7,5},{4,6},{9,7},{6,8},{11,9},{8,10... | collective-permute-start | bytes 196616 | tf_op jit(solution)/shard_map/ppermute | solution.py:27
  4.6 3.0 %collective-permute-start.2 = (bf16[2,16,256]{2,1,0:T(8,128)(2,1)S(1)}, bf16[2,16,256]{2,1,0:T(8,128)(2,1)S(1)}, u32[]{:S(2)}, u32[]{:S(2)}) collective-permute-start(bf16[2,16,256]{2,1,0:T(8,128)(2,1)S(1)} %fusion), channel_id=1, source_target_pairs={{1,0},{5,1},{3,2},{7,3},{0,4},{9,5},{2,6},{11,7},{4,8},{13,9},{6,1... | collective-permute-start | bytes 49160 | tf_op jit(solution)/shard_map/ppermute | solution.py:27
  7.3 1.5 %collective-permute-start.6 = (bf16[288,128]{1,0:T(8,128)(2,1)S(1)}, bf16[288,128]{1,0:T(8,128)(2,1)S(1)}, u32[]{:S(2)}, u32[]{:S(2)}) collective-permute-start(bf16[288,128]{1,0:T(8,128)(2,1)S(1)} %get-tuple-element.23.own_ref), channel_id=1, source_target_pairs={{0,1},{1,0},{2,3},{3,2},{4,5},{5,4},{6,7},{7,6},{8,9},{9,8},{10,11... | collective-permute-start | bytes 221192 | tf_op jit(solution)/shard_map/ppermute | solution.py:18
  7.6 1.4 %collective-permute-start.4 = (bf16[2,64,256]{2,1,0:T(8,128)(2,1)S(1)}, bf16[2,64,256]{2,1,0:T(8,128)(2,1)S(1)}, u32[]{:S(2)}, u32[]{:S(2)}) collective-permute-start(bf16[2,64,256]{2,1,0:T(8,128)(2,1)S(1)} %collective-permute-done.1.r1_ref), channel_id=1, source_target_pairs={{0,1},{1,0},{2,3},{3,2},{4,5},{5,4},{6,7},{7,6},{8,9},{9,8},{10,11... | collective-permute-start | bytes 196616 | tf_op jit(solution)/shard_map/ppermute | solution.py:18
  7.9 1.2 %collective-permute-start.3 = (bf16[2,16,256]{2,1,0:T(8,128)(2,1)S(1)}, bf16[2,16,256]{2,1,0:T(8,128)(2,1)S(1)}, u32[]{:S(2)}, u32[]{:S(2)}) collective-permute-start(bf16[2,16,256]{2,1,0:T(8,128)(2,1)S(1)} %collective-permute-done.2.r2_ref), channel_id=1, source_target_pairs={{0,1},{1,0},{2,3},{3,2},{4,5},{5,4},{6,7},{7,6},{8,9},{9,8},{10,11... | collective-permute-start | bytes 49160 | tf_op jit(solution)/shard_map/ppermute | solution.py:18
  10.4 3.9 %collective-permute-start.7 = (bf16[160,128]{1,0:T(8,128)(2,1)S(1)}, bf16[160,128]{1,0:T(8,128)(2,1)S(1)}, u32[]{:S(2)}, u32[]{:S(2)}) collective-permute-start(bf16[160,128]{1,0:T(8,128)(2,1)S(1)} %get-tuple-element.24.cols_own_ref), channel_id=1, source_target_pairs={{1,0},{5,1},{3,2},{7,3},{0,4},{9,5},{2,6},{11,7},{4,8},{13,9},{6,1... | collective-permute-start | bytes 122888 | tf_op jit(solution)/shard_map/ppermute | solution.py:27

commit v5 on v4

--- a/solution.py
+++ b/solution.py
@@ -1,3 +1,5 @@
+import functools
+
 import jax
 import jax.numpy as jnp
 from jax import lax
@@ -267,10 +269,25 @@
     rows_ref[...] = jnp.where(valid, jnp.where(low, proj, turned), -jnp.inf)[:row_rows]
 
 
-def contact_kernel(
+def near_kernel(*refs):
+    @pl.when(lax.axis_index("chan") == 0)
+    def _():
+        contact_tiles(*refs)
+
+
+def far_kernel(near_ref, *refs):
+    @pl.when(lax.axis_index("chan") == 0)
+    def _():
+        refs[7][...] = near_ref[...]
+
+    @pl.when(lax.axis_index("chan") == 1)
+    def _():
+        contact_tiles(*refs)
+
+
+def contact_tiles(
     length_ref,
-    cols_own_ref,
-    cols_far_ref,
+    cols_ref,
     rows_ref,
     col_mask_ref,
     wbig_ref,
@@ -282,13 +299,12 @@
     mix_s,
 ):
     bins = out_ref.shape[0]
-    col_rows = cols_own_ref.shape[0]
+    col_rows = cols_ref.shape[0]
     row_rows = rows_ref.shape[0]
     i = lax.axis_index("blk")
-    c = lax.axis_index("chan")
 
     low = lax.broadcasted_iota(jnp.int32, (1, 2 * F2), 1) < F2
-    pcol = jnp.where(c == 0, cols_own_ref[...].astype(F32), cols_far_ref[...].astype(F32))
+    pcol = cols_ref[...].astype(F32)
     shifted = [
         pltpu.roll(pcol, col_rows - HALO - (r - 1) * D2, axis=0)[: 2 * bins] for r in range(3)
     ]
@@ -453,10 +469,9 @@
         ],
         compiler_params=params,
     )(chrom_len, mask, packed, oth)
-    return pl.pallas_call(
-        contact_kernel,
+    tiles = functools.partial(
+        pl.pallas_call,
         out_shape=jax.ShapeDtypeStruct((bins, 2 * bins), F32),
-        in_specs=[smem] + [vmem] * 7,
         out_specs=vmem,
         scratch_shapes=[
             pltpu.VMEM((bins + 2 * HALO, 6 * F2), F32),
@@ -464,7 +479,13 @@
             pltpu.VMEM((bins // 8, 2 * bins, 8 * F2), BF16),
         ],
         compiler_params=params,
-    )(chrom_len, cols, cols_far, row_features, *prepared)
+    )
+    near = tiles(near_kernel, in_specs=[smem] + [vmem] * 6)(
+        chrom_len, cols, row_features, *prepared
+    )
+    return tiles(far_kernel, in_specs=[vmem, smem] + [vmem] * 6)(
+        near, chrom_len, cols_far, row_features, *prepared
+    )
 
 
 def solution(mesh):

time: 17.2 us -> 16.5 us (0.959)
  the two profiles are of different devices: /device:TPU:0 before, /device:TPU:1 now
where the time goes in v5:
time: 16.5 us; the launch traced here: 16.3 us
  Pallas kernels  6.47 us (39%)
  starting transfers between devices  5.66 us (34%)
  waiting for transfers between devices  3.46 us (21%)
  between operations  0.72 us (4%)
    ppermute x3, starting transfers between devices, line_permute(): return lax.ppermute(value, ('blk', 'chan'), pairs)  3.23 us
    pallas_call x1, Pallas kernels, local(): tiles(far_kernel, in_specs=[vmem, smem] + [vmem] * 6)  2.7 us
    ppermute x3, waiting for transfers between devices, line_permute(): return lax.ppermute(value, ('blk', 'chan'), pairs)  2.7 us
    ppermute x5, starting transfers between devices, chan_swap(): return lax.ppermute(value, 'chan', [(0, 1), (1, 0)])  2.43 us
    pallas_call x1, Pallas kernels, local(): pl.pallas_call(trunk_kernel, out_shape=[jax.ShapeDtypeStruct((rows, 2 * F...  1.32 us
    pallas_call x1, Pallas kernels, local(): pl.pallas_call(pack_kernel, out_shape=[jax.ShapeDtypeStruct(band_mask.sha...  1.09 us
    pallas_call x1, Pallas kernels, local(): pl.pallas_call(front_kernel, out_shape=jax.ShapeDtypeStruct(features.shap...  0.88 us
    ppermute x5, waiting for transfers between devices, chan_swap(): return lax.ppermute(value, 'chan', [(0, 1), (1, 0)])  0.76 us
  transfers between devices with their start and end apart: 8, of which 3 were waited for; matrix products, arithmetic and copies ran while one was open for 0% of the time, Pallas kernels for 15%

profile of v5, /device:TPU:1, one launch (start us, length us, event | category | flops | bytes accessed | tf_op | source)
XLA Modules:
  0.0 16.3 jit_solution(5710292010417942971)
XLA Ops:
  0.0 0.0 copy-start
  0.0 0.0 copy-start.1
  0.0 0.1 collective-permute-start
  0.1 0.9 %shard_map.100 = bf16[64,256]{1,0:T(8,128)(2,1)S(1)} custom-call(bf16[64,256]{1,0:T(8,128)(2,1)} %own_any.1), custom_call_target="tpu_custom_call" | custom-call | flops 4000000000 | bytes 1000000 | tf_op jit(solution)/shard_map/pallas_call | solution.py:395
  1.0 0.5 %collective-permute-done = bf16[64,256]{1,0:T(8,128)(2,1)S(1)} collective-permute-done((bf16[64,256]{1,0:T(8,128)(2,1)}, bf16[64,256]{1,0:T(8,128)(2,1)S(1)}, u32[]{:S(2)}, u32[]{:S(2)}) %collective-permute-start) | collective-permute-done | bytes 32800 | tf_op jit(solution)/shard_map/ppermute | solution.py:20
  1.4 0.0 copy-done
  1.4 0.2 %collective-permute-start.5 = (bf16[2,3,512,256]{3,2,1,0:T(8,128)(2,1)S(1)}, bf16[2,3,512,256]{3,2,1,0:T(8,128)(2,1)S(1)}, u32[]{:S(2)}, u32[]{:S(2)}) collective-permute-start(bf16[2,3,512,256]{3,2,1,0:T(8,128)(2,1)S(1)} %copy-done), channel_id=1, source_target_pairs={{0,1},{1,0},{2,3},{3,2},{4,5},{5,4},{6,7},{7,6},{8,9},{9,8},{10,11... | collective-permute-start | bytes 4718600 | tf_op jit(solution)/shard_map/ppermute | solution.py:20
  1.7 0.4 %collective-permute-start.1 = (bf16[2,64,256]{2,1,0:T(8,128)(2,1)S(1)}, bf16[2,64,256]{2,1,0:T(8,128)(2,1)S(1)}, u32[]{:S(2)}, u32[]{:S(2)}) collective-permute-start(bf16[2,64,256]{2,1,0:T(8,128)(2,1)S(1)} %pad_maximum_fusion.after_any.own_ref), channel_id=1, source_target_pairs={{1,0},{3,1},{0,2},{5,3},{2,4},{7,5},{4,6},{9,7},{6,8},{11,9},{8,10... | collective-permute-start | bytes 196616 | tf_op jit(solution)/shard_map/ppermute | solution.py:29
  2.0 2.6 %collective-permute-start.2 = (bf16[2,16,256]{2,1,0:T(8,128)(2,1)S(1)}, bf16[2,16,256]{2,1,0:T(8,128)(2,1)S(1)}, u32[]{:S(2)}, u32[]{:S(2)}) collective-permute-start(bf16[2,16,256]{2,1,0:T(8,128)(2,1)S(1)} %fusion), channel_id=1, source_target_pairs={{1,0},{5,1},{3,2},{7,3},{0,4},{9,5},{2,6},{11,7},{4,8},{13,9},{6,1... | collective-permute-start | bytes 49160 | tf_op jit(solution)/shard_map/ppermute | solution.py:29
  4.7 1.1 %shard_map.101 = (s32[4,8]{1,0:T(4,128)S(1)}, bf16[288,128]{1,0:T(8,128)(2,1)S(1)}, f32[8,256]{1,0:T(8,128)S(1)}) custom-call(bf16[2,64,256]{2,1,0:T(8,128)(2,1)S(1)} %pad_maximum_fusion.after_any.own_ref, s32[4,8]{1,0:T(4,128)} %bitcast.10, bf16[3,3,32,64]{3,2,1,0:T(8,128)(2,1)} %mw_any.1, bf16[1,32]{1,0:T(2,128)(2,1)} %bitcast.11, bf16[1,32]{1,0:T(2,128)(2,1)} %bitcast.12, ...), custom_call_target="tpu_custom_call" | custom-call | tf_op jit(solution)/shard_map/pallas_call | solution.py:405
  5.8 1.6 %collective-permute-start.6 = (bf16[288,128]{1,0:T(8,128)(2,1)S(1)}, bf16[288,128]{1,0:T(8,128)(2,1)S(1)}, u32[]{:S(2)}, u32[]{:S(2)}) collective-permute-start(bf16[288,128]{1,0:T(8,128)(2,1)S(1)} %get-tuple-element.23.own_ref), channel_id=1, source_target_pairs={{0,1},{1,0},{2,3},{3,2},{4,5},{5,4},{6,7},{7,6},{8,9},{9,8},{10,11... | collective-permute-start | bytes 221192 | tf_op jit(solution)/shard_map/ppermute | solution.py:20
  7.4 0.0 collective-permute-done.2.r2_ref
  7.4 0.0 collective-permute-done.1.r1_ref
  7.4 0.3 %collective-permute-start.4 = (bf16[2,64,256]{2,1,0:T(8,128)(2,1)S(1)}, bf16[2,64,256]{2,1,0:T(8,128)(2,1)S(1)}, u32[]{:S(2)}, u32[]{:S(2)}) collective-permute-start(bf16[2,64,256]{2,1,0:T(8,128)(2,1)S(1)} %collective-permute-done.1.r1_ref), channel_id=1, source_target_pairs={{0,1},{1,0},{2,3},{3,2},{4,5},{5,4},{6,7},{7,6},{8,9},{9,8},{10,11... | collective-permute-start | bytes 196616 | tf_op jit(solution)/shard_map/ppermute | solution.py:20
  7.7 0.2 %collective-permute-start.3 = (bf16[2,16,256]{2,1,0:T(8,128)(2,1)S(1)}, bf16[2,16,256]{2,1,0:T(8,128)(2,1)S(1)}, u32[]{:S(2)}, u32[]{:S(2)}) collective-permute-start(bf16[2,16,256]{2,1,0:T(8,128)(2,1)S(1)} %collective-permute-done.2.r2_ref), channel_id=1, source_target_pairs={{0,1},{1,0},{2,3},{3,2},{4,5},{5,4},{6,7},{7,6},{8,9},{9,8},{10,11... | collective-permute-start | bytes 49160 | tf_op jit(solution)/shard_map/ppermute | solution.py:20
  8.6 0.0 collective-permute-done.6.oth_ref
  8.6 0.3 %collective-permute-done.3.s2_ref = bf16[2,16,256]{2,1,0:T(8,128)(2,1)S(1)} collective-permute-done((bf16[2,16,256]{2,1,0:T(8,128)(2,1)S(1)}, bf16[2,16,256]{2,1,0:T(8,128)(2,1)S(1)}, u32[]{:S(2)}, u32[]{:S(2)}) %collective-permute-start.3) | collective-permute-done | bytes 16416 | tf_op jit(solution)/shard_map/ppermute | solution.py:20
  8.9 0.0 collective-permute-done.4.s1_ref
  8.9 0.0 collective-permute-done.5.w_oth_ref
  8.9 0.0 copy-done.1
  8.9 1.3 %shard_map.102 = (bf16[160,128]{1,0:T(8,128)(2,1)S(1)}, f32[96,128]{1,0:T(8,128)S(1)}) custom-call(s32[1]{0:T(128)S(6)} %copy.11.length_ref.refs_0_, bf16[2,64,256]{2,1,0:T(8,128)(2,1)S(1)} %pad_maximum_fusion.after_any.own_ref, bf16[2,16,256]{2,1,0:T(8,128)(2,1)S(1)} %collective-permute-done.2.r2_ref, ...), custom_call_target="tpu_custom_call" | custom-call | tf_op jit(solution)/shard_map/pallas_call | solution.py:441
  10.2 0.2 %collective-permute-start.7 = (bf16[160,128]{1,0:T(8,128)(2,1)S(1)}, bf16[160,128]{1,0:T(8,128)(2,1)S(1)}, u32[]{:S(2)}, u32[]{:S(2)}) collective-permute-start(bf16[160,128]{1,0:T(8,128)(2,1)S(1)} %get-tuple-element.24.refs_1_), channel_id=1, source_target_pairs={{1,0},{5,1},{3,2},{7,3},{0,4},{9,5},{2,6},{11,7},{4,8},{13,9},{6,1... | collective-permute-start | bytes 122888 | tf_op jit(solution)/shard_map/ppermute | solution.py:29
  10.4 0.5 %shard_map.103 = (f32[3,128,384]{2,1,0:T(8,128)S(1)}, bf16[1152,256]{1,0:T(8,128)(2,1)S(1)}, f32[8,256]{1,0:T(8,128)S(1)}, bf16[16,512]{1,0:T(8,128)(2,1)S(1)}) custom-call(s32[1]{0:T(128)S(6)} %copy.11.length_ref.refs_0_, s32[4,8]{1,0:T(4,128)S(1)} %get-tuple-element.26.mask_ref, bf16[288,128]{1,0:T(8,128)(2,1)S(1)} %get-tuple-element.23.own_ref, ...), custom_call_target="tpu_custom_call" | custom-call | tf_op jit(solution)/shard_map/pallas_call | solution.py:456
  10.9 2.7 %collective-permute-done.7.refs_1_ = bf16[160,128]{1,0:T(8,128)(2,1)S(1)} collective-permute-done((bf16[160,128]{1,0:T(8,128)(2,1)S(1)}, bf16[160,128]{1,0:T(8,128)(2,1)S(1)}, u32[]{:S(2)}, u32[]{:S(2)}) %collective-permute-start.7) | collective-permute-done | bytes 40992 | tf_op jit(solution)/shard_map/ppermute | solution.py:29
  13.6 2.7 %shard_map.105 = f32[64,128]{1,0:T(8,128)} custom-call(f32[64,128]{1,0:T(8,128)S(1)} %shard_map.104.near_ref, s32[1]{0:T(128)S(6)} %copy.11.length_ref.refs_0_, bf16[160,128]{1,0:T(8,128)(2,1)S(1)} %collective-permute-done.7.refs_1_, f32[96,128]{1,0:T(8,128)S(1)} %get-tuple-element.25.refs_2_, f32[3,128,384]{2,1,0:T(8,128)S(1)} %get-tuple-element.27.refs_3_, ...), custom_call_target="tpu_custom_call" | custom-call | tf_op jit(solution)/shard_map/pallas_call | solution.py:486
  (3 shorter events, 0.0 us)
Async XLA Ops:
  0.0 1.4 %copy-start = (bf16[2,3,512,256]{3,2,1,0:T(8,128)(2,1)S(1)}, bf16[2,3,512,256]{3,2,1,0:T(8,128)(2,1)}, u32[]{:S(2)}) copy-start(bf16[2,3,512,256]{3,2,1,0:T(8,128)(2,1)} %w_own_ref.1) | copy-start | bytes 4718596
  0.0 8.9 %copy-start.1 = (bf16[512,128]{1,0:T(8,128)(2,1)S(1)}, bf16[512,128]{1,0:T(8,128)(2,1)}, u32[]{:S(2)}) copy-start(bf16[512,128]{1,0:T(8,128)(2,1)} %pw_ref.1) | copy-start | bytes 393220
  0.0 1.4 %collective-permute-start = (bf16[64,256]{1,0:T(8,128)(2,1)}, bf16[64,256]{1,0:T(8,128)(2,1)S(1)}, u32[]{:S(2)}, u32[]{:S(2)}) collective-permute-start(bf16[64,256]{1,0:T(8,128)(2,1)} %own_any.1), channel_id=1, source_target_pairs={{0,1},{1,0},{2,3},{3,2},{4,5},{5,4},{6,7},{7,6},{8,9},{9,8},{10,11... | collective-permute-start | bytes 98312 | tf_op jit(solution)/shard_map/ppermute | solution.py:20
  1.4 7.4 %collective-permute-start.5 = (bf16[2,3,512,256]{3,2,1,0:T(8,128)(2,1)S(1)}, bf16[2,3,512,256]{3,2,1,0:T(8,128)(2,1)S(1)}, u32[]{:S(2)}, u32[]{:S(2)}) collective-permute-start(bf16[2,3,512,256]{3,2,1,0:T(8,128)(2,1)S(1)} %copy-done), channel_id=1, source_target_pairs={{0,1},{1,0},{2,3},{3,2},{4,5},{5,4},{6,7},{7,6},{8,9},{9,8},{10,11... | collective-permute-start | bytes 4718600 | tf_op jit(solution)/shard_map/ppermute | solution.py:20
  1.7 5.8 %collective-permute-start.1 = (bf16[2,64,256]{2,1,0:T(8,128)(2,1)S(1)}, bf16[2,64,256]{2,1,0:T(8,128)(2,1)S(1)}, u32[]{:S(2)}, u32[]{:S(2)}) collective-permute-start(bf16[2,64,256]{2,1,0:T(8,128)(2,1)S(1)} %pad_maximum_fusion.after_any.own_ref), channel_id=1, source_target_pairs={{1,0},{3,1},{0,2},{5,3},{2,4},{7,5},{4,6},{9,7},{6,8},{11,9},{8,10... | collective-permute-start | bytes 196616 | tf_op jit(solution)/shard_map/ppermute | solution.py:29
  2.0 5.4 %collective-permute-start.2 = (bf16[2,16,256]{2,1,0:T(8,128)(2,1)S(1)}, bf16[2,16,256]{2,1,0:T(8,128)(2,1)S(1)}, u32[]{:S(2)}, u32[]{:S(2)}) collective-permute-start(bf16[2,16,256]{2,1,0:T(8,128)(2,1)S(1)} %fusion), channel_id=1, source_target_pairs={{1,0},{5,1},{3,2},{7,3},{0,4},{9,5},{2,6},{11,7},{4,8},{13,9},{6,1... | collective-permute-start | bytes 49160 | tf_op jit(solution)/shard_map/ppermute | solution.py:29
  5.8 2.8 %collective-permute-start.6 = (bf16[288,128]{1,0:T(8,128)(2,1)S(1)}, bf16[288,128]{1,0:T(8,128)(2,1)S(1)}, u32[]{:S(2)}, u32[]{:S(2)}) collective-permute-start(bf16[288,128]{1,0:T(8,128)(2,1)S(1)} %get-tuple-element.23.own_ref), channel_id=1, source_target_pairs={{0,1},{1,0},{2,3},{3,2},{4,5},{5,4},{6,7},{7,6},{8,9},{9,8},{10,11... | collective-permute-start | bytes 221192 | tf_op jit(solution)/shard_map/ppermute | solution.py:20
  7.4 1.5 %collective-permute-start.4 = (bf16[2,64,256]{2,1,0:T(8,128)(2,1)S(1)}, bf16[2,64,256]{2,1,0:T(8,128)(2,1)S(1)}, u32[]{:S(2)}, u32[]{:S(2)}) collective-permute-start(bf16[2,64,256]{2,1,0:T(8,128)(2,1)S(1)} %collective-permute-done.1.r1_ref), channel_id=1, source_target_pairs={{0,1},{1,0},{2,3},{3,2},{4,5},{5,4},{6,7},{7,6},{8,9},{9,8},{10,11... | collective-permute-start | bytes 196616 | tf_op jit(solution)/shard_map/ppermute | solution.py:20
  7.7 1.2 %collective-permute-start.3 = (bf16[2,16,256]{2,1,0:T(8,128)(2,1)S(1)}, bf16[2,16,256]{2,1,0:T(8,128)(2,1)S(1)}, u32[]{:S(2)}, u32[]{:S(2)}) collective-permute-start(bf16[2,16,256]{2,1,0:T(8,128)(2,1)S(1)} %collective-permute-done.2.r2_ref), channel_id=1, source_target_pairs={{0,1},{1,0},{2,3},{3,2},{4,5},{5,4},{6,7},{7,6},{8,9},{9,8},{10,11... | collective-permute-start | bytes 49160 | tf_op jit(solution)/shard_map/ppermute | solution.py:20
  10.2 3.4 %collective-permute-start.7 = (bf16[160,128]{1,0:T(8,128)(2,1)S(1)}, bf16[160,128]{1,0:T(8,128)(2,1)S(1)}, u32[]{:S(2)}, u32[]{:S(2)}) collective-permute-start(bf16[160,128]{1,0:T(8,128)(2,1)S(1)} %get-tuple-element.24.refs_1_), channel_id=1, source_target_pairs={{1,0},{5,1},{3,2},{7,3},{0,4},{9,5},{2,6},{11,7},{4,8},{13,9},{6,1... | collective-permute-start | bytes 122888 | tf_op jit(solution)/shard_map/ppermute | solution.py:29

commit v6 on v5

--- a/solution.py
+++ b/solution.py
@@ -11,7 +11,8 @@
 BAND = 3
 CONV1 = 2
 D2 = 2
-HALO = 16
+HALO = 8
+RIM = 16
 F32 = jnp.float32
 BF16 = jnp.bfloat16
 
@@ -29,10 +30,32 @@
     return lax.ppermute(value, ("blk", "chan"), pairs)
 
 
-def front_kernel(own_any, own_ref, sem):
-    copy = pltpu.make_async_copy(own_any, own_ref, sem)
-    copy.start()
-    copy.wait()
+def pair_permute(value, low):
+    count = lax.axis_size("blk")
+    partner = {}
+    for i in range(low, count - 1, 2):
+        partner[i], partner[i + 1] = i + 1, i
+    pairs = []
+    for i in range(count):
+        for core in range(2):
+            source = partner[i] * 2 + core if i in partner else i * 2 + 1 - core
+            pairs.append((source, i * 2 + core))
+    return lax.ppermute(value, ("blk", "chan"), pairs)
+
+
+def front_kernel(own_any, cb_any, pb_any, own_ref, small_ref, cb_s, pb_s, sems):
+    pairs = ((cb_any, cb_s), (pb_any, pb_s), (own_any, own_ref))
+    copies = [
+        pltpu.make_async_copy(source, target, sems.at[at])
+        for at, (source, target) in enumerate(pairs)
+    ]
+    for copy in copies:
+        copy.start()
+    copies[0].wait()
+    copies[1].wait()
+    small_ref[0:CONV1, :] = cb_s[...].astype(F32)
+    small_ref[CONV1 : CONV1 + 1, : 2 * F2] = pb_s[...].astype(F32)
+    copies[2].wait()
 
 
 def pack_kernel(
@@ -41,27 +64,15 @@
     mw_any,
     mb_any,
     hw_any,
-    cb_any,
-    pb_any,
     mask_ref,
     packed_ref,
-    small_ref,
     mw_s,
     mb_s,
     hw_s,
-    cb_s,
-    pb_s,
     extra_s,
     sems,
 ):
-    pairs = (
-        (mw_any, mw_s),
-        (cb_any, cb_s),
-        (mb_any, mb_s),
-        (hw_any, hw_s),
-        (pb_any, pb_s),
-        (mask_any, mask_ref),
-    )
+    pairs = ((mw_any, mw_s), (mb_any, mb_s), (hw_any, hw_s), (mask_any, mask_ref))
     copies = [
         pltpu.make_async_copy(source, target, sems.at[at])
         for at, (source, target) in enumerate(pairs)
@@ -69,15 +80,10 @@
     for copy in copies:
         copy.start()
     extra_s[...] = jnp.zeros_like(extra_s)
-    for copy in copies[:5]:
+    for copy in copies:
         copy.wait()
 
     half = mw_any.shape[2]
-    biases = cb_s[...].astype(F32)
-    for layer in range(CONV1):
-        for quarter in range(4):
-            at = 4 * layer + quarter
-            extra_s[at : at + 1, :F2] = biases[layer : layer + 1, quarter * F2 : (quarter + 1) * F2]
     extra_s[8:9, :half] = mb_s[...].astype(F32)
     extra_s[9:10, :half] = hw_s[...].astype(F32)
     extra = pltpu.roll(extra_s[...], F2, axis=1)
@@ -86,10 +92,6 @@
             at = (3 * s + r) * half
             packed_ref[at : at + half, :F2] = mw_s[s, r]
     packed_ref[:32, F2:] = extra[:, F2:].astype(BF16)
-    small_ref[0:2, :] = biases
-    small_ref[2:3, : 2 * F2] = pb_s[...].astype(F32)
-    for copy in copies[5:]:
-        copy.wait()
 
 
 def prep_kernel(
@@ -184,63 +186,61 @@
     )
 
 
-def trunk_kernel(
+def window_kernel(own_ref, r2_ref, even_ref, odd_ref, h_ref):
+    core = lax.axis_index("chan")
+    parity = lax.rem(lax.axis_index("blk"), 2)
+    bins = own_ref.shape[1]
+    half = own_ref.shape[2]
+
+    def fill(before_ref, after_ref):
+        for part in range(2):
+            lanes = slice(part * half, (part + 1) * half)
+            held = 1 - part
+            before = before_ref[held, bins - RIM :, :].astype(F32)
+            h_ref[:HALO, lanes] = before[RIM - HALO :]
+            h_ref[HALO : HALO + bins, lanes] = own_ref[held].astype(F32)
+            h_ref[HALO + bins : HALO + 2 * bins, lanes] = after_ref[held].astype(F32)
+            h_ref[HALO + 2 * bins :, lanes] = r2_ref[held].astype(F32)[:HALO]
+
+    @pl.when((core == 1) & (parity == 0))
+    def _():
+        fill(odd_ref, even_ref)
+
+    @pl.when((core == 1) & (parity == 1))
+    def _():
+        fill(even_ref, odd_ref)
+
+
+def trunk_kernel(*refs):
+    @pl.when(lax.axis_index("chan") == 1)
+    def _():
+        trunk(*refs)
+
+
+def trunk(
     length_ref,
-    own_ref,
-    r2_ref,
-    s2_ref,
-    r1_ref,
-    s1_ref,
+    window_ref,
     w_own_ref,
     pw_ref,
     w_oth_ref,
     small_ref,
-    oth_ref,
+    cb_oth_ref,
     cols_ref,
-    rows_ref,
+    both_ref,
     h_s,
-    bias_s,
 ):
-    bins = own_ref.shape[1]
-    half = own_ref.shape[2]
-    rows = cols_ref.shape[0]
-    row_rows = rows_ref.shape[0]
+    rows = window_ref.shape[0]
+    half = window_ref.shape[1] // 2
+    held = cols_ref.shape[0]
+    bins = held - 2 * HALO
     count = lax.axis_size("blk")
     i = lax.axis_index("blk")
-    c = lax.axis_index("chan")
     bin_index = i * bins - HALO + lax.broadcasted_iota(jnp.int32, (rows, 2 * F2), 0)
     valid = (bin_index >= 0) & (bin_index < length_ref[0])
     inside = ((bin_index >= 0) & (bin_index < count * bins))[:, :1]
 
-    def put(start, number, ref, source, swapped=0):
-        keep = valid[start : start + number, :]
-        for part in range(2):
-            held = lax.rem(part + c + swapped, 2)
-            for at in range(0, half, 128):
-                h_s[start : start + number, part * half + at : part * half + at + 128] = jnp.where(
-                    keep, ref[held, source : source + number, at : at + 128].astype(F32), 0.0
-                )
-
-    tail = bins - HALO
-    put(HALO, bins, own_ref, 0)
-
-    @pl.when(c == 0)
-    def _():
-        put(0, HALO, r1_ref, tail)
-        put(HALO + bins, bins, s1_ref, 0, 1)
-        put(HALO + 2 * bins, HALO, s2_ref, 0, 1)
-
-    @pl.when(c == 1)
-    def _():
-        put(0, HALO, s1_ref, tail, 1)
-        put(HALO + bins, bins, r1_ref, 0)
-        put(HALO + 2 * bins, HALO, r2_ref, 0)
-
-    other = pltpu.roll(oth_ref[:16, :].astype(F32), F2, axis=1)
-    for layer in range(CONV1):
-        for quarter in range(4):
-            at = 4 * layer + quarter
-            bias_s[layer : layer + 1, quarter * F2 : (quarter + 1) * F2] = other[at : at + 1, :F2]
+    for at in range(0, 2 * half, 128):
+        h_s[:, at : at + 128] = jnp.where(valid, window_ref[:, at : at + 128], 0.0)
 
     for layer in range(CONV1):
         e = 2 ** (layer + 1)
@@ -249,24 +249,25 @@
             (hidden if t == 1 else pltpu.roll(hidden, ((1 - t) * e) % rows, axis=0)).astype(BF16)
             for t in range(3)
         ]
-        for w_ref, bias_ref, side in (
-            (w_own_ref, small_ref, c),
-            (w_oth_ref, bias_s, 1 - c),
-        ):
+        for at, w_ref, bias_ref in ((half, w_own_ref, small_ref), (0, w_oth_ref, cb_oth_ref)):
             q = jnp.dot(taps[0], w_ref[layer, 0], preferred_element_type=F32)
             q = q + jnp.dot(taps[1], w_ref[layer, 1], preferred_element_type=F32)
             q = q + jnp.dot(taps[2], w_ref[layer, 2], preferred_element_type=F32)
-            lanes = pl.ds(pl.multiple_of(side * half, half), half)
-            bias = bias_ref[layer : layer + 1, :]
+            bias = bias_ref[...].astype(F32)[layer : layer + 1, :]
+            lanes = slice(at, at + half)
             new = (h_s[:, lanes] + jnp.maximum(q + bias, 0.0)).astype(BF16).astype(F32)
             h_s[:, lanes] = jnp.where(inside, new, 0.0)
 
     proj = jnp.dot(h_s[...].astype(BF16), pw_ref[...], preferred_element_type=F32)
-    proj = (proj + small_ref[2:3, : 2 * F2]).astype(BF16).astype(F32)
+    proj = (proj + small_ref[CONV1 : CONV1 + 1, : 2 * F2]).astype(BF16).astype(F32)
     low = lax.broadcasted_iota(jnp.int32, (1, 2 * F2), 1) < F2
     turned = pltpu.roll(proj, F2, axis=1)
-    cols_ref[...] = jnp.where(low, turned, proj).astype(BF16)
-    rows_ref[...] = jnp.where(valid, jnp.where(low, proj, turned), -jnp.inf)[:row_rows]
+    cols = jnp.where(low, turned[:held], proj[rows - held :]).astype(BF16)
+    cols_ref[...] = cols
+    both_ref[:held, :] = cols
+    both_ref[held:, :] = jnp.where(valid, jnp.where(low, proj, turned), -jnp.inf)[:held].astype(
+        BF16
+    )
 
 
 def near_kernel(*refs):
@@ -295,16 +296,20 @@
     head_ref,
     out_ref,
     pa6_s,
-    x_s,
     mix_s,
 ):
     bins = out_ref.shape[0]
-    col_rows = cols_ref.shape[0]
-    row_rows = rows_ref.shape[0]
+    col_rows = 2 * bins + 2 * HALO
+    row_rows = bins + 2 * HALO
     i = lax.axis_index("blk")
 
     low = lax.broadcasted_iota(jnp.int32, (1, 2 * F2), 1) < F2
-    pcol = cols_ref[...].astype(F32)
+    held = bins + 2 * HALO
+    pcol = cols_ref[: bins + 2 * HALO, :].astype(F32)
+    turned = pltpu.roll(pcol, F2, axis=1)
+    pcol = jnp.concatenate(
+        [jnp.where(low, pcol, turned), jnp.where(low, turned, pcol)[2 * held - col_rows :]], axis=0
+    )
     shifted = [
         pltpu.roll(pcol, col_rows - HALO - (r - 1) * D2, axis=0)[: 2 * bins] for r in range(3)
     ]
@@ -320,28 +325,32 @@
     ]
     col_centre = shifted[1].astype(BF16).reshape(2 * bins // 16, 16, 2 * F2)
 
-    prow = rows_ref[...]
+    prow = rows_ref[row_rows:, :].astype(F32)
     prow_next = pltpu.roll(prow, row_rows - D2, axis=0)
     pa6_s[:, : 2 * F2] = prow
     pa6_s[:, 2 * F2 : 4 * F2] = jnp.where(low, prow, prow_next)
     pa6_s[:, 4 * F2 :] = prow_next
 
     groups = bins // 8
-    per_dot = x_s.shape[0] // (2 * bins)
+    per_dot = 4
     zero = jnp.zeros((), BF16)
     bias4 = side_ref[0:1, :]
     for v in range(2):
         for start in range(0, groups, per_dot):
+            values = {}
             for slot in range(2 * start, 2 * (start + per_dot) + 1):
                 at = HALO - D2 + v + 4 * slot
                 row = jnp.broadcast_to(pa6_s[at : at + 1, :], (16, 6 * F2)).astype(BF16)
                 cols = col_first if slot == 0 else col_last if slot == 2 * groups else col_mid
-                value = jnp.maximum(row[None] + cols, zero).reshape(2 * bins, 6 * F2)
-                for s in range(3):
-                    if (slot - s) % 2 == 0 and start <= (slot - s) // 2 < start + per_dot:
-                        at_row = ((slot - s) // 2 - start) * 2 * bins
-                        x_s[at_row : at_row + 2 * bins, s * 6 * F2 : (s + 1) * 6 * F2] = value
-            y = jnp.dot(x_s[...], wbig_ref[...], preferred_element_type=F32)
+                values[slot] = jnp.maximum(row[None] + cols, zero).reshape(2 * bins, 6 * F2)
+            x = jnp.concatenate(
+                [
+                    jnp.concatenate([values[2 * g + s] for s in range(3)], axis=1)
+                    for g in range(start, start + per_dot)
+                ],
+                axis=0,
+            )
+            y = jnp.dot(x, wbig_ref[...], preferred_element_type=F32)
             y = jnp.maximum(y + bias4, 0.0)
             for group in range(start, start + per_dot):
                 at = HALO + v + 8 * group
@@ -392,33 +401,64 @@
         return pltpu.with_memory_space_constraint(value, pltpu.HBM)
 
     other = chan_swap(features)
-    own = pl.pallas_call(
+    cb_oth = chan_swap(conv_bias)
+    own, small = pl.pallas_call(
         front_kernel,
-        out_shape=jax.ShapeDtypeStruct(features.shape, BF16),
-        in_specs=[anywhere],
-        out_specs=vmem,
-        scratch_shapes=[pltpu.SemaphoreType.DMA],
+        out_shape=[
+            jax.ShapeDtypeStruct(features.shape, BF16),
+            jax.ShapeDtypeStruct((8, half), F32),
+        ],
+        in_specs=[anywhere] * 3,
+        out_specs=[vmem] * 2,
+        scratch_shapes=[
+            pltpu.VMEM(conv_bias.shape, BF16),
+            pltpu.VMEM((1, 2 * F2), BF16),
+            pltpu.SemaphoreType.DMA((3,)),
+        ],
         cost_estimate=pl.CostEstimate(flops=4000000000, bytes_accessed=1000000, transcendentals=0),
         compiler_params=params,
-    )(in_hbm(features))
-    own = jnp.stack([own, other])
-    mask, packed, small = pl.pallas_call(
+    )(in_hbm(features), in_hbm(conv_bias), in_hbm(proj_bias[None]))
+    own, cb_oth = lax.optimization_barrier((jnp.stack([own, other]), cb_oth))
+    even = pair_permute(own, 0)
+    odd = pair_permute(own, 1)
+    r2 = line_permute(own[:, :RIM], 2)
+    w_in, own = lax.optimization_barrier((conv_weight, own))
+    w_oth = chan_swap(w_in)
+    window = pl.pallas_call(
+        window_kernel,
+        out_shape=jax.ShapeDtypeStruct((rows, 2 * half), F32),
+        in_specs=[vmem] * 4,
+        out_specs=vmem,
+        cost_estimate=pl.CostEstimate(flops=4000000000, bytes_accessed=1000000, transcendentals=0),
+        compiler_params=params,
+    )(own, r2, even, odd)
+    cols, both = pl.pallas_call(
+        trunk_kernel,
+        out_shape=[
+            jax.ShapeDtypeStruct((bins + 2 * HALO, 2 * F2), BF16),
+            jax.ShapeDtypeStruct((2 * bins + 4 * HALO, 2 * F2), BF16),
+        ],
+        in_specs=[smem] + [vmem] * 6,
+        out_specs=[vmem] * 2,
+        scratch_shapes=[pltpu.VMEM((rows, 2 * half), F32)],
+        compiler_params=params,
+    )(chrom_len, window, conv_weight, proj_weight, w_oth, small, cb_oth)
+    cols_far = line_permute(cols, 2)
+    near_both = chan_swap(both)
+    mask, packed = pl.pallas_call(
         pack_kernel,
         out_shape=[
             jax.ShapeDtypeStruct(band_mask.shape[::-1], jnp.int32),
             jax.ShapeDtypeStruct((9 * half_out, 2 * F2), BF16),
-            jax.ShapeDtypeStruct((8, half), F32),
-        ],
-        in_specs=[anywhere] * 7,
-        out_specs=[vmem] * 3,
+        ],
+        in_specs=[anywhere] * 5,
+        out_specs=[vmem] * 2,
         scratch_shapes=[
             pltpu.VMEM(map_weight.shape, BF16),
             pltpu.VMEM((1, half_out), BF16),
             pltpu.VMEM((1, half_out), BF16),
-            pltpu.VMEM(conv_bias.shape, BF16),
-            pltpu.VMEM((1, 2 * F2), BF16),
             pltpu.VMEM((32, 2 * F2), F32),
-            pltpu.SemaphoreType.DMA((6,)),
+            pltpu.SemaphoreType.DMA((4,)),
         ],
         compiler_params=params,
     )(
@@ -427,32 +467,8 @@
         in_hbm(map_weight),
         in_hbm(map_bias[None]),
         in_hbm(head_weight[None]),
-        in_hbm(conv_bias),
-        in_hbm(proj_bias[None]),
-    )
-    r1 = line_permute(own, 1)
-    r2 = line_permute(own[:, :HALO], 2)
-    r1, r2 = lax.optimization_barrier((r1, r2))
-    s1 = chan_swap(r1)
-    s2 = chan_swap(r2)
-    w_in, own = lax.optimization_barrier((conv_weight, own))
-    w_oth = chan_swap(w_in)
+    )
     oth = chan_swap(packed)
-    cols, row_features = pl.pallas_call(
-        trunk_kernel,
-        out_shape=[
-            jax.ShapeDtypeStruct((rows, 2 * F2), BF16),
-            jax.ShapeDtypeStruct((bins + 2 * HALO, 2 * F2), F32),
-        ],
-        in_specs=[smem] + [vmem] * 10,
-        out_specs=[vmem] * 2,
-        scratch_shapes=[
-            pltpu.VMEM((rows, 2 * half), F32),
-            pltpu.VMEM((8, half), F32),
-        ],
-        compiler_params=params,
-    )(chrom_len, own, r2, s2, r1, s1, conv_weight, proj_weight, w_oth, small, oth)
-    cols_far = line_permute(cols, 2)
     prepared = pl.pallas_call(
         prep_kernel,
         out_shape=[
@@ -475,16 +491,15 @@
         out_specs=vmem,
         scratch_shapes=[
             pltpu.VMEM((bins + 2 * HALO, 6 * F2), F32),
-            pltpu.VMEM((4 * 2 * bins, 18 * F2), BF16),
             pltpu.VMEM((bins // 8, 2 * bins, 8 * F2), BF16),
         ],
         compiler_params=params,
     )
     near = tiles(near_kernel, in_specs=[smem] + [vmem] * 6)(
-        chrom_len, cols, row_features, *prepared
+        chrom_len, near_both, near_both, *prepared
     )
     return tiles(far_kernel, in_specs=[vmem, smem] + [vmem] * 6)(
-        near, chrom_len, cols_far, row_features, *prepared
+        near, chrom_len, cols_far, both, *prepared
     )
 
 

time: 16.5 us -> 15.5 us (0.939)
  the two profiles are of different devices: /device:TPU:1 before, /device:TPU:7 now
where the time goes in v6:
time: 15.5 us; the launch traced here: 15.3 us
  starting transfers between devices  6.44 us (42%)
  Pallas kernels  5.93 us (38%)
  waiting for transfers between devices  2.09 us (13%)
  between operations  0.74 us (5%)
    ppermute x5, starting transfers between devices, chan_swap(): return lax.ppermute(value, 'chan', [(0, 1), (1, 0)])  2.9 us
    pallas_call x1, Pallas kernels, local(): tiles(far_kernel, in_specs=[vmem, smem] + [vmem] * 6)  2.48 us
    ppermute x2, starting transfers between devices, pair_permute(): return lax.ppermute(value, ('blk', 'chan'), pairs)  2.48 us
    ppermute x2, waiting for transfers between devices, line_permute(): return lax.ppermute(value, ('blk', 'chan'), pairs)  1.44 us
    ppermute x2, starting transfers between devices, line_permute(): return lax.ppermute(value, ('blk', 'chan'), pairs)  1.06 us
    pallas_call x1, Pallas kernels, local(): pl.pallas_call(pack_kernel, out_shape=[jax.ShapeDtypeStruct(band_mask.sha...  1.01 us
    pallas_call x1, Pallas kernels, local(): pl.pallas_call(trunk_kernel, out_shape=[jax.ShapeDtypeStruct((bins + 2 *...  1.01 us
    pallas_call x1, Pallas kernels, local(): pl.pallas_call(front_kernel, out_shape=[jax.ShapeDtypeStruct(features.sha...  0.93 us
  transfers between devices with their start and end apart: 9, of which 4 were waited for; matrix products, arithmetic and copies ran while one was open for 0% of the time, Pallas kernels for 23%

profile of v6, /device:TPU:7, one launch (start us, length us, event | category | flops | bytes accessed | tf_op | source)
XLA Modules:
  0.0 15.3 jit_solution(16900019632985962561)
XLA Ops:
  0.0 0.7 %collective-permute-start = (bf16[64,256]{1,0:T(8,128)(2,1)}, bf16[64,256]{1,0:T(8,128)(2,1)S(1)}, u32[]{:S(2)}, u32[]{:S(2)}) collective-permute-start(bf16[64,256]{1,0:T(8,128)(2,1)} %own_any.1), channel_id=1, source_target_pairs={{0,1},{1,0},{2,3},{3,2},{4,5},{5,4},{6,7},{7,6},{8,9},{9,8},{10,11... | collective-permute-start | bytes 98312 | tf_op jit(solution)/shard_map/ppermute | solution.py:21
  0.7 0.0 collective-permute-start.1
  0.7 0.0 copy-start
  0.7 0.9 %shard_map.100 = (bf16[64,256]{1,0:T(8,128)(2,1)S(1)}, f32[8,256]{1,0:T(8,128)S(1)}) custom-call(bf16[64,256]{1,0:T(8,128)(2,1)} %own_any.1, bf16[2,256]{1,0:T(2,128)(2,1)} %cb_any.1, bf16[1,128]{1,0:T(2,128)(2,1)} %bitcast.11), custom_call_target="tpu_custom_call" | custom-call | flops 4000000000 | bytes 1000000 | tf_op jit(solution)/shard_map/pallas_call | solution.py:405
  1.6 0.1 collective-permute-done
  1.8 0.3 %collective-permute-done.1.refs_6_ = bf16[2,256]{1,0:T(2,128)(2,1)S(1)} collective-permute-done((bf16[2,256]{1,0:T(2,128)(2,1)}, bf16[2,256]{1,0:T(2,128)(2,1)S(1)}, u32[]{:S(2)}, u32[]{:S(2)}) %collective-permute-start.1) | collective-permute-done | bytes 1056 | tf_op jit(solution)/shard_map/ppermute | solution.py:21
  2.0 0.1 copy-done
  2.1 0.5 %collective-permute-start.5 = (bf16[2,3,512,256]{3,2,1,0:T(8,128)(2,1)S(1)}, bf16[2,3,512,256]{3,2,1,0:T(8,128)(2,1)S(1)}, u32[]{:S(2)}, u32[]{:S(2)}) collective-permute-start(bf16[2,3,512,256]{3,2,1,0:T(8,128)(2,1)S(1)} %copy-done), channel_id=1, source_target_pairs={{0,1},{1,0},{2,3},{3,2},{4,5},{5,4},{6,7},{7,6},{8,9},{9,8},{10,11... | collective-permute-start | bytes 4718600 | tf_op jit(solution)/shard_map/ppermute | solution.py:21
  2.6 0.3 %collective-permute-start.3 = (bf16[2,64,256]{2,1,0:T(8,128)(2,1)S(1)}, bf16[2,64,256]{2,1,0:T(8,128)(2,1)S(1)}, u32[]{:S(2)}, u32[]{:S(2)}) collective-permute-start(bf16[2,64,256]{2,1,0:T(8,128)(2,1)S(1)} %pad_maximum_fusion.own_ref.after_any), channel_id=1, source_target_pairs={{2,0},{3,1},{0,2},{1,3},{6,4},{7,5},{4,6},{5,7},{10,8},{11,9},{8,1... | collective-permute-start | bytes 196616 | tf_op jit(solution)/shard_map/ppermute | solution.py:43
  2.9 2.2 %collective-permute-start.4 = (bf16[2,64,256]{2,1,0:T(8,128)(2,1)S(1)}, bf16[2,64,256]{2,1,0:T(8,128)(2,1)S(1)}, u32[]{:S(2)}, u32[]{:S(2)}) collective-permute-start(bf16[2,64,256]{2,1,0:T(8,128)(2,1)S(1)} %pad_maximum_fusion.own_ref.after_any), channel_id=1, source_target_pairs={{1,0},{0,1},{4,2},{5,3},{2,4},{3,5},{8,6},{9,7},{6,8},{7,9},{12,10... | collective-permute-start | bytes 196616 | tf_op jit(solution)/shard_map/ppermute | solution.py:43
  5.1 0.6 %collective-permute-start.2 = (bf16[2,16,256]{2,1,0:T(8,128)(2,1)S(1)}, bf16[2,16,256]{2,1,0:T(8,128)(2,1)S(1)}, u32[]{:S(2)}, u32[]{:S(2)}) collective-permute-start(bf16[2,16,256]{2,1,0:T(8,128)(2,1)S(1)} %slice.3), channel_id=1, source_target_pairs={{1,0},{5,1},{3,2},{7,3},{0,4},{9,5},{2,6},{11,7},{4,8},{13,9},{6,1... | collective-permute-start | bytes 49160 | tf_op jit(solution)/shard_map/ppermute | solution.py:30
  6.3 1.0 %shard_map.103 = (s32[4,8]{1,0:T(4,128)S(1)}, bf16[288,128]{1,0:T(8,128)(2,1)S(1)}) custom-call(bf16[2,64,256]{2,1,0:T(8,128)(2,1)S(1)} %pad_maximum_fusion.own_ref.after_any, s32[4,8]{1,0:T(4,128)} %bitcast.8, bf16[3,3,32,64]{3,2,1,0:T(8,128)(2,1)} %mw_any.1, bf16[1,32]{1,0:T(2,128)(2,1)} %bitcast.9, bf16[1,32]{1,0:T(2,128)(2,1)} %bitcast.10), custom_call_target="tpu_custom_call" | custom-call | tf_op jit(solution)/shard_map/pallas_call | solution.py:448
  7.4 0.0 copy-start.1
  7.4 1.6 %collective-permute-start.7 = (bf16[288,128]{1,0:T(8,128)(2,1)S(1)}, bf16[288,128]{1,0:T(8,128)(2,1)S(1)}, u32[]{:S(2)}, u32[]{:S(2)}) collective-permute-start(bf16[288,128]{1,0:T(8,128)(2,1)S(1)} %get-tuple-element.27.own_ref), channel_id=1, source_target_pairs={{0,1},{1,0},{2,3},{3,2},{4,5},{5,4},{6,7},{7,6},{8,9},{9,8},{10,11... | collective-permute-start | bytes 221192 | tf_op jit(solution)/shard_map/ppermute | solution.py:21
  9.0 0.0 collective-permute-done.2.r2_ref
  9.0 0.0 collective-permute-done.3.even_ref
  9.0 0.0 collective-permute-done.4.odd_ref
  9.1 0.0 collective-permute-done.5.refs_4_
  9.1 0.0 copy-done.1
  9.1 1.0 %shard_map.102 = (bf16[80,128]{1,0:T(8,128)(2,1)S(1)}, bf16[160,128]{1,0:T(8,128)(2,1)S(1)}) custom-call(s32[1]{0:T(128)S(6)} %copy.11.refs_0_.length_ref, f32[144,512]{1,0:T(8,128)S(1)} %shard_map.101.refs_1_, bf16[2,3,512,256]{3,2,1,0:T(8,128)(2,1)S(1)} %copy-done, bf16[512,128]{1,0:T(8,128)(2,1)S(1)} %copy-done.1, ...), custom_call_target="tpu_custom_call" | custom-call | tf_op jit(solution)/shard_map/pallas_call | solution.py:435
  10.1 0.1 collective-permute-start.6
  10.2 0.5 %collective-permute-start.8 = (bf16[80,128]{1,0:T(8,128)(2,1)S(1)}, bf16[80,128]{1,0:T(8,128)(2,1)S(1)}, u32[]{:S(2)}, u32[]{:S(2)}) collective-permute-start(bf16[80,128]{1,0:T(8,128)(2,1)S(1)} %get-tuple-element.32), channel_id=1, source_target_pairs={{1,0},{5,1},{3,2},{7,3},{0,4},{9,5},{2,6},{11,7},{4,8},{13,9},{6,1... | collective-permute-start | bytes 61448 | tf_op jit(solution)/shard_map/ppermute | solution.py:30
  10.7 0.0 collective-permute-done.7.oth_ref
  10.7 0.5 %shard_map.104 = (f32[3,128,384]{2,1,0:T(8,128)S(1)}, bf16[1152,256]{1,0:T(8,128)(2,1)S(1)}, f32[8,256]{1,0:T(8,128)S(1)}, bf16[16,512]{1,0:T(8,128)(2,1)S(1)}) custom-call(s32[1]{0:T(128)S(6)} %copy.11.refs_0_.length_ref, s32[4,8]{1,0:T(4,128)S(1)} %get-tuple-element.26.mask_ref, bf16[288,128]{1,0:T(8,128)(2,1)S(1)} %get-tuple-element.27.own_ref, ...), custom_call_target="tpu_custom_call" | custom-call | tf_op jit(solution)/shard_map/pallas_call | solution.py:472
  11.2 0.2 %collective-permute-done.6.refs_1_.refs_2_ = bf16[160,128]{1,0:T(8,128)(2,1)S(1)} collective-permute-done((bf16[160,128]{1,0:T(8,128)(2,1)S(1)}, bf16[160,128]{1,0:T(8,128)(2,1)S(1)}, u32[]{:S(2)}, u32[]{:S(2)}) %collective-permute-start.6) | collective-permute-done | bytes 40992 | tf_op jit(solution)/shard_map/ppermute | solution.py:21
  11.4 1.4 %collective-permute-done.8.refs_1_ = bf16[80,128]{1,0:T(8,128)(2,1)S(1)} collective-permute-done((bf16[80,128]{1,0:T(8,128)(2,1)S(1)}, bf16[80,128]{1,0:T(8,128)(2,1)S(1)}, u32[]{:S(2)}, u32[]{:S(2)}) %collective-permute-start.8) | collective-permute-done | bytes 20512 | tf_op jit(solution)/shard_map/ppermute | solution.py:30
  12.8 2.5 %shard_map.106 = f32[64,128]{1,0:T(8,128)} custom-call(f32[64,128]{1,0:T(8,128)S(1)} %shard_map.105.near_ref, s32[1]{0:T(128)S(6)} %copy.11.refs_0_.length_ref, bf16[80,128]{1,0:T(8,128)(2,1)S(1)} %collective-permute-done.8.refs_1_, bf16[160,128]{1,0:T(8,128)(2,1)S(1)} %get-tuple-element.25.refs_2_, f32[3,128,384]{2,1,0:T(8,128)S(1)} %get-tuple-element.28.refs_3_, ...), custom_call_target="tpu_custom_call" | custom-call | tf_op jit(solution)/shard_map/pallas_call | solution.py:501
  (4 shorter events, 0.1 us)
Async XLA Ops:
  0.0 1.7 %collective-permute-start = (bf16[64,256]{1,0:T(8,128)(2,1)}, bf16[64,256]{1,0:T(8,128)(2,1)S(1)}, u32[]{:S(2)}, u32[]{:S(2)}) collective-permute-start(bf16[64,256]{1,0:T(8,128)(2,1)} %own_any.1), channel_id=1, source_target_pairs={{0,1},{1,0},{2,3},{3,2},{4,5},{5,4},{6,7},{7,6},{8,9},{9,8},{10,11... | collective-permute-start | bytes 98312 | tf_op jit(solution)/shard_map/ppermute | solution.py:21
  0.7 1.4 %collective-permute-start.1 = (bf16[2,256]{1,0:T(2,128)(2,1)}, bf16[2,256]{1,0:T(2,128)(2,1)S(1)}, u32[]{:S(2)}, u32[]{:S(2)}) collective-permute-start(bf16[2,256]{1,0:T(2,128)(2,1)} %cb_any.1), channel_id=1, source_target_pairs={{0,1},{1,0},{2,3},{3,2},{4,5},{5,4},{6,7},{7,6},{8,9},{9,8},{10,11... | collective-permute-start | bytes 3080 | tf_op jit(solution)/shard_map/ppermute | solution.py:21
  0.7 1.5 %copy-start = (bf16[2,3,512,256]{3,2,1,0:T(8,128)(2,1)S(1)}, bf16[2,3,512,256]{3,2,1,0:T(8,128)(2,1)}, u32[]{:S(2)}) copy-start(bf16[2,3,512,256]{3,2,1,0:T(8,128)(2,1)} %refs_2_.1) | copy-start | bytes 4718596
  2.1 6.9 %collective-permute-start.5 = (bf16[2,3,512,256]{3,2,1,0:T(8,128)(2,1)S(1)}, bf16[2,3,512,256]{3,2,1,0:T(8,128)(2,1)S(1)}, u32[]{:S(2)}, u32[]{:S(2)}) collective-permute-start(bf16[2,3,512,256]{3,2,1,0:T(8,128)(2,1)S(1)} %copy-done), channel_id=1, source_target_pairs={{0,1},{1,0},{2,3},{3,2},{4,5},{5,4},{6,7},{7,6},{8,9},{9,8},{10,11... | collective-permute-start | bytes 4718600 | tf_op jit(solution)/shard_map/ppermute | solution.py:21
  2.6 6.4 %collective-permute-start.3 = (bf16[2,64,256]{2,1,0:T(8,128)(2,1)S(1)}, bf16[2,64,256]{2,1,0:T(8,128)(2,1)S(1)}, u32[]{:S(2)}, u32[]{:S(2)}) collective-permute-start(bf16[2,64,256]{2,1,0:T(8,128)(2,1)S(1)} %pad_maximum_fusion.own_ref.after_any), channel_id=1, source_target_pairs={{2,0},{3,1},{0,2},{1,3},{6,4},{7,5},{4,6},{5,7},{10,8},{11,9},{8,1... | collective-permute-start | bytes 196616 | tf_op jit(solution)/shard_map/ppermute | solution.py:43
  2.9 6.1 %collective-permute-start.4 = (bf16[2,64,256]{2,1,0:T(8,128)(2,1)S(1)}, bf16[2,64,256]{2,1,0:T(8,128)(2,1)S(1)}, u32[]{:S(2)}, u32[]{:S(2)}) collective-permute-start(bf16[2,64,256]{2,1,0:T(8,128)(2,1)S(1)} %pad_maximum_fusion.own_ref.after_any), channel_id=1, source_target_pairs={{1,0},{0,1},{4,2},{5,3},{2,4},{3,5},{8,6},{9,7},{6,8},{7,9},{12,10... | collective-permute-start | bytes 196616 | tf_op jit(solution)/shard_map/ppermute | solution.py:43
  5.1 3.9 %collective-permute-start.2 = (bf16[2,16,256]{2,1,0:T(8,128)(2,1)S(1)}, bf16[2,16,256]{2,1,0:T(8,128)(2,1)S(1)}, u32[]{:S(2)}, u32[]{:S(2)}) collective-permute-start(bf16[2,16,256]{2,1,0:T(8,128)(2,1)S(1)} %slice.3), channel_id=1, source_target_pairs={{1,0},{5,1},{3,2},{7,3},{0,4},{9,5},{2,6},{11,7},{4,8},{13,9},{6,1... | collective-permute-start | bytes 49160 | tf_op jit(solution)/shard_map/ppermute | solution.py:30
  7.4 1.7 %copy-start.1 = (bf16[512,128]{1,0:T(8,128)(2,1)S(1)}, bf16[512,128]{1,0:T(8,128)(2,1)}, u32[]{:S(2)}) copy-start(bf16[512,128]{1,0:T(8,128)(2,1)} %refs_3_.1) | copy-start | bytes 393220
  7.4 3.3 %collective-permute-start.7 = (bf16[288,128]{1,0:T(8,128)(2,1)S(1)}, bf16[288,128]{1,0:T(8,128)(2,1)S(1)}, u32[]{:S(2)}, u32[]{:S(2)}) collective-permute-start(bf16[288,128]{1,0:T(8,128)(2,1)S(1)} %get-tuple-element.27.own_ref), channel_id=1, source_target_pairs={{0,1},{1,0},{2,3},{3,2},{4,5},{5,4},{6,7},{7,6},{8,9},{9,8},{10,11... | collective-permute-start | bytes 221192 | tf_op jit(solution)/shard_map/ppermute | solution.py:21
  10.1 1.3 %collective-permute-start.6 = (bf16[160,128]{1,0:T(8,128)(2,1)S(1)}, bf16[160,128]{1,0:T(8,128)(2,1)S(1)}, u32[]{:S(2)}, u32[]{:S(2)}) collective-permute-start(bf16[160,128]{1,0:T(8,128)(2,1)S(1)} %get-tuple-element.25.refs_2_), channel_id=1, source_target_pairs={{0,1},{1,0},{2,3},{3,2},{4,5},{5,4},{6,7},{7,6},{8,9},{9,8},{10,11... | collective-permute-start | bytes 122888 | tf_op jit(solution)/shard_map/ppermute | solution.py:21
  10.2 2.6 %collective-permute-start.8 = (bf16[80,128]{1,0:T(8,128)(2,1)S(1)}, bf16[80,128]{1,0:T(8,128)(2,1)S(1)}, u32[]{:S(2)}, u32[]{:S(2)}) collective-permute-start(bf16[80,128]{1,0:T(8,128)(2,1)S(1)} %get-tuple-element.32), channel_id=1, source_target_pairs={{1,0},{5,1},{3,2},{7,3},{0,4},{9,5},{2,6},{11,7},{4,8},{13,9},{6,1... | collective-permute-start | bytes 61448 | tf_op jit(solution)/shard_map/ppermute | solution.py:30

commit v7 on v6

--- a/solution.py
+++ b/solution.py
@@ -32,14 +32,16 @@
 
 def pair_permute(value, low):
     count = lax.axis_size("blk")
-    partner = {}
+    source = {}
+    for i in range(count):
+        source[i, 0] = (i ^ 1, 0)
     for i in range(low, count - 1, 2):
-        partner[i], partner[i + 1] = i + 1, i
-    pairs = []
+        source[i, 1], source[i + 1, 1] = (i + 1, 1), (i, 1)
     for i in range(count):
-        for core in range(2):
-            source = partner[i] * 2 + core if i in partner else i * 2 + 1 - core
-            pairs.append((source, i * 2 + core))
+        if (i, 1) not in source:
+            source[i, 1] = (i ^ 1, 0)
+            source[i, 0] = (i, 1)
+    pairs = [(j * 2 + d, i * 2 + c) for (i, c), (j, d) in source.items()]
     return lax.ppermute(value, ("blk", "chan"), pairs)
 
 
@@ -212,6 +214,11 @@
 
 
 def trunk_kernel(*refs):
+    @pl.when(lax.axis_index("chan") == 0)
+    def _():
+        for ref in refs[-3:-1]:
+            ref[...] = jnp.zeros_like(ref)
+
     @pl.when(lax.axis_index("chan") == 1)
     def _():
         trunk(*refs)

time: 15.5 us -> 15.3 us (0.987)
  the two profiles are of different devices: /device:TPU:7 before, /device:TPU:1 now
where the time goes in v7:
time: 15.3 us; the launch traced here: 15.1 us
  starting transfers between devices  6.25 us (41%)
  Pallas kernels  5.93 us (39%)
  waiting for transfers between devices  1.76 us (12%)
  between operations  0.75 us (5%)
  local copies, waits for them, and re-layouts  0.43 us (3%)
    ppermute x2, starting transfers between devices, pair_permute(): return lax.ppermute(value, ('blk', 'chan'), pairs)  2.94 us
    ppermute x5, starting transfers between devices, chan_swap(): return lax.ppermute(value, 'chan', [(0, 1), (1, 0)])  2.78 us
    pallas_call x1, Pallas kernels, local(): tiles(far_kernel, in_specs=[vmem, smem] + [vmem] * 6)  2.48 us
    ppermute x2, waiting for transfers between devices, line_permute(): return lax.ppermute(value, ('blk', 'chan'), pairs)  1.44 us
    pallas_call x1, Pallas kernels, local(): pl.pallas_call(pack_kernel, out_shape=[jax.ShapeDtypeStruct(band_mask.sha...  1.01 us
    pallas_call x1, Pallas kernels, local(): pl.pallas_call(trunk_kernel, out_shape=[jax.ShapeDtypeStruct((bins + 2 *...  1.01 us
    pallas_call x1, Pallas kernels, local(): pl.pallas_call(front_kernel, out_shape=[jax.ShapeDtypeStruct(features.sha...  0.93 us
    ppermute x2, starting transfers between devices, line_permute(): return lax.ppermute(value, ('blk', 'chan'), pairs)  0.53 us
  transfers between devices with their start and end apart: 9, of which 3 were waited for; matrix products, arithmetic and copies ran while one was open for 0% of the time, Pallas kernels for 23%

profile of v7, /device:TPU:1, one launch (start us, length us, event | category | flops | bytes accessed | tf_op | source)
XLA Modules:
  0.0 15.1 jit_solution(11245108597574989199)
XLA Ops:
  0.0 0.1 collective-permute-start
  0.1 0.5 %collective-permute-start.1 = (bf16[2,256]{1,0:T(2,128)(2,1)}, bf16[2,256]{1,0:T(2,128)(2,1)S(1)}, u32[]{:S(2)}, u32[]{:S(2)}) collective-permute-start(bf16[2,256]{1,0:T(2,128)(2,1)} %cb_any.1), channel_id=1, source_target_pairs={{0,1},{1,0},{2,3},{3,2},{4,5},{5,4},{6,7},{7,6},{8,9},{9,8},{10,11... | collective-permute-start | bytes 3080 | tf_op jit(solution)/shard_map/ppermute | solution.py:21
  0.5 0.0 copy-start
  0.5 0.9 %shard_map.100 = (bf16[64,256]{1,0:T(8,128)(2,1)S(1)}, f32[8,256]{1,0:T(8,128)S(1)}) custom-call(bf16[64,256]{1,0:T(8,128)(2,1)} %own_any.1, bf16[2,256]{1,0:T(2,128)(2,1)} %cb_any.1, bf16[1,128]{1,0:T(2,128)(2,1)} %bitcast.11), custom_call_target="tpu_custom_call" | custom-call | flops 4000000000 | bytes 1000000 | tf_op jit(solution)/shard_map/pallas_call | solution.py:412
  1.5 0.0 collective-permute-done
  1.5 0.1 collective-permute-done.1.refs_6_
  1.5 0.4 %copy-done = bf16[2,3,512,256]{3,2,1,0:T(8,128)(2,1)S(1)} copy-done((bf16[2,3,512,256]{3,2,1,0:T(8,128)(2,1)S(1)}, bf16[2,3,512,256]{3,2,1,0:T(8,128)(2,1)}, u32[]{:S(2)}) %copy-start) | copy-done | bytes 1572888
  2.0 0.1 collective-permute-start.5
  2.0 2.7 %collective-permute-start.3 = (bf16[2,64,256]{2,1,0:T(8,128)(2,1)S(1)}, bf16[2,64,256]{2,1,0:T(8,128)(2,1)S(1)}, u32[]{:S(2)}, u32[]{:S(2)}) collective-permute-start(bf16[2,64,256]{2,1,0:T(8,128)(2,1)S(1)} %pad_maximum_fusion.own_ref.after_any), channel_id=1, source_target_pairs={{2,0},{0,2},{6,4},{4,6},{10,8},{8,10},{14,12},{12,14},{3,1},{1,3},... | collective-permute-start | bytes 196616 | tf_op jit(solution)/shard_map/ppermute | solution.py:45
  4.7 0.3 %collective-permute-start.4 = (bf16[2,64,256]{2,1,0:T(8,128)(2,1)S(1)}, bf16[2,64,256]{2,1,0:T(8,128)(2,1)S(1)}, u32[]{:S(2)}, u32[]{:S(2)}) collective-permute-start(bf16[2,64,256]{2,1,0:T(8,128)(2,1)S(1)} %pad_maximum_fusion.own_ref.after_any), channel_id=1, source_target_pairs={{1,0},{0,2},{6,4},{4,6},{10,8},{8,10},{14,12},{15,14},{5,3},{3,5},... | collective-permute-start | bytes 196616 | tf_op jit(solution)/shard_map/ppermute | solution.py:45
  5.0 0.0 collective-permute-start.2
  5.7 1.0 %shard_map.103 = (s32[4,8]{1,0:T(4,128)S(1)}, bf16[288,128]{1,0:T(8,128)(2,1)S(1)}) custom-call(bf16[2,64,256]{2,1,0:T(8,128)(2,1)S(1)} %pad_maximum_fusion.own_ref.after_any, s32[4,8]{1,0:T(4,128)} %bitcast.8, bf16[3,3,32,64]{3,2,1,0:T(8,128)(2,1)} %mw_any.1, bf16[1,32]{1,0:T(2,128)(2,1)} %bitcast.9, bf16[1,32]{1,0:T(2,128)(2,1)} %bitcast.10), custom_call_target="tpu_custom_call" | custom-call | tf_op jit(solution)/shard_map/pallas_call | solution.py:455
  6.7 0.0 copy-start.1
  6.7 2.1 %collective-permute-start.7 = (bf16[288,128]{1,0:T(8,128)(2,1)S(1)}, bf16[288,128]{1,0:T(8,128)(2,1)S(1)}, u32[]{:S(2)}, u32[]{:S(2)}) collective-permute-start(bf16[288,128]{1,0:T(8,128)(2,1)S(1)} %get-tuple-element.27.own_ref), channel_id=1, source_target_pairs={{0,1},{1,0},{2,3},{3,2},{4,5},{5,4},{6,7},{7,6},{8,9},{9,8},{10,11... | collective-permute-start | bytes 221192 | tf_op jit(solution)/shard_map/ppermute | solution.py:21
  8.8 0.0 collective-permute-done.2.r2_ref
  8.8 0.0 collective-permute-done.3.even_ref
  8.8 0.0 collective-permute-done.4.odd_ref
  8.9 0.0 collective-permute-done.5.refs_4_
  8.9 0.0 copy-done.1
  8.9 1.0 %shard_map.102 = (bf16[80,128]{1,0:T(8,128)(2,1)S(1)}, bf16[160,128]{1,0:T(8,128)(2,1)S(1)}) custom-call(s32[1]{0:T(128)S(6)} %copy.11.refs_0_.length_ref, f32[144,512]{1,0:T(8,128)S(1)} %shard_map.101.refs_1_, bf16[2,3,512,256]{3,2,1,0:T(8,128)(2,1)S(1)} %copy-done, bf16[512,128]{1,0:T(8,128)(2,1)S(1)} %copy-done.1, ...), custom_call_target="tpu_custom_call" | custom-call | tf_op jit(solution)/shard_map/pallas_call | solution.py:442
  9.9 0.1 collective-permute-start.6
  10.0 0.5 %collective-permute-start.8 = (bf16[80,128]{1,0:T(8,128)(2,1)S(1)}, bf16[80,128]{1,0:T(8,128)(2,1)S(1)}, u32[]{:S(2)}, u32[]{:S(2)}) collective-permute-start(bf16[80,128]{1,0:T(8,128)(2,1)S(1)} %get-tuple-element.32), channel_id=1, source_target_pairs={{1,0},{5,1},{3,2},{7,3},{0,4},{9,5},{2,6},{11,7},{4,8},{13,9},{6,1... | collective-permute-start | bytes 61448 | tf_op jit(solution)/shard_map/ppermute | solution.py:30
  10.5 0.0 collective-permute-done.7.oth_ref
  10.5 0.5 %shard_map.104 = (f32[3,128,384]{2,1,0:T(8,128)S(1)}, bf16[1152,256]{1,0:T(8,128)(2,1)S(1)}, f32[8,256]{1,0:T(8,128)S(1)}, bf16[16,512]{1,0:T(8,128)(2,1)S(1)}) custom-call(s32[1]{0:T(128)S(6)} %copy.11.refs_0_.length_ref, s32[4,8]{1,0:T(4,128)S(1)} %get-tuple-element.26.mask_ref, bf16[288,128]{1,0:T(8,128)(2,1)S(1)} %get-tuple-element.27.own_ref, ...), custom_call_target="tpu_custom_call" | custom-call | tf_op jit(solution)/shard_map/pallas_call | solution.py:479
  11.0 0.2 %collective-permute-done.6.refs_1_.refs_2_ = bf16[160,128]{1,0:T(8,128)(2,1)S(1)} collective-permute-done((bf16[160,128]{1,0:T(8,128)(2,1)S(1)}, bf16[160,128]{1,0:T(8,128)(2,1)S(1)}, u32[]{:S(2)}, u32[]{:S(2)}) %collective-permute-start.6) | collective-permute-done | bytes 40992 | tf_op jit(solution)/shard_map/ppermute | solution.py:21
  11.2 1.4 %collective-permute-done.8.refs_1_ = bf16[80,128]{1,0:T(8,128)(2,1)S(1)} collective-permute-done((bf16[80,128]{1,0:T(8,128)(2,1)S(1)}, bf16[80,128]{1,0:T(8,128)(2,1)S(1)}, u32[]{:S(2)}, u32[]{:S(2)}) %collective-permute-start.8) | collective-permute-done | bytes 20512 | tf_op jit(solution)/shard_map/ppermute | solution.py:30
  12.7 2.5 %shard_map.106 = f32[64,128]{1,0:T(8,128)} custom-call(f32[64,128]{1,0:T(8,128)S(1)} %shard_map.105.near_ref, s32[1]{0:T(128)S(6)} %copy.11.refs_0_.length_ref, bf16[80,128]{1,0:T(8,128)(2,1)S(1)} %collective-permute-done.8.refs_1_, bf16[160,128]{1,0:T(8,128)(2,1)S(1)} %get-tuple-element.25.refs_2_, f32[3,128,384]{2,1,0:T(8,128)S(1)} %get-tuple-element.28.refs_3_, ...), custom_call_target="tpu_custom_call" | custom-call | tf_op jit(solution)/shard_map/pallas_call | solution.py:508
  (4 shorter events, 0.1 us)
Async XLA Ops:
  0.0 1.5 %collective-permute-start = (bf16[64,256]{1,0:T(8,128)(2,1)}, bf16[64,256]{1,0:T(8,128)(2,1)S(1)}, u32[]{:S(2)}, u32[]{:S(2)}) collective-permute-start(bf16[64,256]{1,0:T(8,128)(2,1)} %own_any.1), channel_id=1, source_target_pairs={{0,1},{1,0},{2,3},{3,2},{4,5},{5,4},{6,7},{7,6},{8,9},{9,8},{10,11... | collective-permute-start | bytes 98312 | tf_op jit(solution)/shard_map/ppermute | solution.py:21
  0.1 1.5 %collective-permute-start.1 = (bf16[2,256]{1,0:T(2,128)(2,1)}, bf16[2,256]{1,0:T(2,128)(2,1)S(1)}, u32[]{:S(2)}, u32[]{:S(2)}) collective-permute-start(bf16[2,256]{1,0:T(2,128)(2,1)} %cb_any.1), channel_id=1, source_target_pairs={{0,1},{1,0},{2,3},{3,2},{4,5},{5,4},{6,7},{7,6},{8,9},{9,8},{10,11... | collective-permute-start | bytes 3080 | tf_op jit(solution)/shard_map/ppermute | solution.py:21
  0.5 1.5 %copy-start = (bf16[2,3,512,256]{3,2,1,0:T(8,128)(2,1)S(1)}, bf16[2,3,512,256]{3,2,1,0:T(8,128)(2,1)}, u32[]{:S(2)}) copy-start(bf16[2,3,512,256]{3,2,1,0:T(8,128)(2,1)} %refs_2_.1) | copy-start | bytes 4718596
  2.0 6.9 %collective-permute-start.5 = (bf16[2,3,512,256]{3,2,1,0:T(8,128)(2,1)S(1)}, bf16[2,3,512,256]{3,2,1,0:T(8,128)(2,1)S(1)}, u32[]{:S(2)}, u32[]{:S(2)}) collective-permute-start(bf16[2,3,512,256]{3,2,1,0:T(8,128)(2,1)S(1)} %copy-done), channel_id=1, source_target_pairs={{0,1},{1,0},{2,3},{3,2},{4,5},{5,4},{6,7},{7,6},{8,9},{9,8},{10,11... | collective-permute-start | bytes 4718600 | tf_op jit(solution)/shard_map/ppermute | solution.py:21
  2.0 6.8 %collective-permute-start.3 = (bf16[2,64,256]{2,1,0:T(8,128)(2,1)S(1)}, bf16[2,64,256]{2,1,0:T(8,128)(2,1)S(1)}, u32[]{:S(2)}, u32[]{:S(2)}) collective-permute-start(bf16[2,64,256]{2,1,0:T(8,128)(2,1)S(1)} %pad_maximum_fusion.own_ref.after_any), channel_id=1, source_target_pairs={{2,0},{0,2},{6,4},{4,6},{10,8},{8,10},{14,12},{12,14},{3,1},{1,3},... | collective-permute-start | bytes 196616 | tf_op jit(solution)/shard_map/ppermute | solution.py:45
  4.7 4.2 %collective-permute-start.4 = (bf16[2,64,256]{2,1,0:T(8,128)(2,1)S(1)}, bf16[2,64,256]{2,1,0:T(8,128)(2,1)S(1)}, u32[]{:S(2)}, u32[]{:S(2)}) collective-permute-start(bf16[2,64,256]{2,1,0:T(8,128)(2,1)S(1)} %pad_maximum_fusion.own_ref.after_any), channel_id=1, source_target_pairs={{1,0},{0,2},{6,4},{4,6},{10,8},{8,10},{14,12},{15,14},{5,3},{3,5},... | collective-permute-start | bytes 196616 | tf_op jit(solution)/shard_map/ppermute | solution.py:45
  5.0 3.9 %collective-permute-start.2 = (bf16[2,16,256]{2,1,0:T(8,128)(2,1)S(1)}, bf16[2,16,256]{2,1,0:T(8,128)(2,1)S(1)}, u32[]{:S(2)}, u32[]{:S(2)}) collective-permute-start(bf16[2,16,256]{2,1,0:T(8,128)(2,1)S(1)} %slice.3), channel_id=1, source_target_pairs={{1,0},{5,1},{3,2},{7,3},{0,4},{9,5},{2,6},{11,7},{4,8},{13,9},{6,1... | collective-permute-start | bytes 49160 | tf_op jit(solution)/shard_map/ppermute | solution.py:30
  6.7 2.2 %copy-start.1 = (bf16[512,128]{1,0:T(8,128)(2,1)S(1)}, bf16[512,128]{1,0:T(8,128)(2,1)}, u32[]{:S(2)}) copy-start(bf16[512,128]{1,0:T(8,128)(2,1)} %refs_3_.1) | copy-start | bytes 393220
  6.7 3.8 %collective-permute-start.7 = (bf16[288,128]{1,0:T(8,128)(2,1)S(1)}, bf16[288,128]{1,0:T(8,128)(2,1)S(1)}, u32[]{:S(2)}, u32[]{:S(2)}) collective-permute-start(bf16[288,128]{1,0:T(8,128)(2,1)S(1)} %get-tuple-element.27.own_ref), channel_id=1, source_target_pairs={{0,1},{1,0},{2,3},{3,2},{4,5},{5,4},{6,7},{7,6},{8,9},{9,8},{10,11... | collective-permute-start | bytes 221192 | tf_op jit(solution)/shard_map/ppermute | solution.py:21
  9.9 1.3 %collective-permute-start.6 = (bf16[160,128]{1,0:T(8,128)(2,1)S(1)}, bf16[160,128]{1,0:T(8,128)(2,1)S(1)}, u32[]{:S(2)}, u32[]{:S(2)}) collective-permute-start(bf16[160,128]{1,0:T(8,128)(2,1)S(1)} %get-tuple-element.25.refs_2_), channel_id=1, source_target_pairs={{0,1},{1,0},{2,3},{3,2},{4,5},{5,4},{6,7},{7,6},{8,9},{9,8},{10,11... | collective-permute-start | bytes 122888 | tf_op jit(solution)/shard_map/ppermute | solution.py:21
  10.0 2.6 %collective-permute-start.8 = (bf16[80,128]{1,0:T(8,128)(2,1)S(1)}, bf16[80,128]{1,0:T(8,128)(2,1)S(1)}, u32[]{:S(2)}, u32[]{:S(2)}) collective-permute-start(bf16[80,128]{1,0:T(8,128)(2,1)S(1)} %get-tuple-element.32), channel_id=1, source_target_pairs={{1,0},{5,1},{3,2},{7,3},{0,4},{9,5},{2,6},{11,7},{4,8},{13,9},{6,1... | collective-permute-start | bytes 61448 | tf_op jit(solution)/shard_map/ppermute | solution.py:30

commit v8 on v7

--- a/solution.py
+++ b/solution.py
@@ -109,6 +109,7 @@
     taps_s,
 ):
     half = own_ref.shape[0] // 9
+    behind = oth_ref.shape[0] - own_ref.shape[0]
     columns = col_mask_ref.shape[1]
     bins = columns // 2
     count = lax.axis_size("blk")
@@ -117,10 +118,11 @@
     first_col = i * bins + c * columns
     length = length_ref[0]
 
-    for source, side in ((own_ref, c), (oth_ref, 1 - c)):
+    for source, skip, side in ((own_ref, 0, c), (oth_ref, behind, 1 - c)):
         at = pl.ds(pl.multiple_of(side * half, half), half)
         for tap in range(9):
-            taps_s[tap, at, :] = source[tap * half : (tap + 1) * half, :F2].astype(F32)
+            row = skip + tap * half
+            taps_s[tap, at, :] = source[row : row + half, :F2].astype(F32)
     blank = jnp.zeros((F2, F2), F32)
     for j in range(4):
         pieces = []
@@ -137,9 +139,9 @@
         o = lax.broadcasted_iota(jnp.int32, (2 * F2, repeats * F2), 0)
         lane = lax.broadcasted_iota(jnp.int32, (2 * F2, repeats * F2), 1) % F2
         total = jnp.zeros((16, repeats * F2), F32)
-        for ref, side in ((own_ref, c), (oth_ref, 1 - c)):
+        for ref, skip, side in ((own_ref, 0, c), (oth_ref, behind, 1 - c)):
             pick = ((lane == side * half + o - F2) & (o >= F2) & (o < F2 + half)).astype(BF16)
-            value = ref[:16, :].astype(F32)[row : row + 1]
+            value = ref[skip : skip + 16, :].astype(F32)[row : row + 1]
             value = jnp.broadcast_to(value, (16, 2 * F2)).astype(BF16)
             total = total + jnp.dot(value, pick, preferred_element_type=F32)
         return total
@@ -188,7 +190,7 @@
     )
 
 
-def window_kernel(own_ref, r2_ref, even_ref, odd_ref, h_ref):
+def window_kernel(own_ref, r2_ref, odd_ref, even_ref, h_ref):
     core = lax.axis_index("chan")
     parity = lax.rem(lax.axis_index("blk"), 2)
     bins = own_ref.shape[1]
@@ -214,10 +216,14 @@
 
 
 def trunk_kernel(*refs):
+    packed_ref, cols_ref, both_ref = refs[-4:-1]
+    ready = both_ref.shape[0] - packed_ref.shape[0]
+    both_ref[ready:, :] = packed_ref[...]
+
     @pl.when(lax.axis_index("chan") == 0)
     def _():
-        for ref in refs[-3:-1]:
-            ref[...] = jnp.zeros_like(ref)
+        cols_ref[...] = jnp.zeros_like(cols_ref)
+        both_ref[:ready, :] = jnp.zeros((ready, 2 * F2), BF16)
 
     @pl.when(lax.axis_index("chan") == 1)
     def _():
@@ -232,6 +238,7 @@
     w_oth_ref,
     small_ref,
     cb_oth_ref,
+    packed_ref,
     cols_ref,
     both_ref,
     h_s,
@@ -272,7 +279,7 @@
     cols = jnp.where(low, turned[:held], proj[rows - held :]).astype(BF16)
     cols_ref[...] = cols
     both_ref[:held, :] = cols
-    both_ref[held:, :] = jnp.where(valid, jnp.where(low, proj, turned), -jnp.inf)[:held].astype(
+    both_ref[held : 2 * held, :] = jnp.where(valid, jnp.where(low, proj, turned), -jnp.inf)[:held].astype(
         BF16
     )
 
@@ -332,7 +339,7 @@
     ]
     col_centre = shifted[1].astype(BF16).reshape(2 * bins // 16, 16, 2 * F2)
 
-    prow = rows_ref[row_rows:, :].astype(F32)
+    prow = rows_ref[row_rows : 2 * row_rows, :].astype(F32)
     prow_next = pltpu.roll(prow, row_rows - D2, axis=0)
     pa6_s[:, : 2 * F2] = prow
     pa6_s[:, 2 * F2 : 4 * F2] = jnp.where(low, prow, prow_next)
@@ -422,7 +429,7 @@
             pltpu.VMEM((1, 2 * F2), BF16),
             pltpu.SemaphoreType.DMA((3,)),
         ],
-        cost_estimate=pl.CostEstimate(flops=4000000000, bytes_accessed=1000000, transcendentals=0),
+        cost_estimate=pl.CostEstimate(flops=500000000, bytes_accessed=1000000, transcendentals=0),
         compiler_params=params,
     )(in_hbm(features), in_hbm(conv_bias), in_hbm(proj_bias[None]))
     own, cb_oth = lax.optimization_barrier((jnp.stack([own, other]), cb_oth))
@@ -438,20 +445,7 @@
         out_specs=vmem,
         cost_estimate=pl.CostEstimate(flops=4000000000, bytes_accessed=1000000, transcendentals=0),
         compiler_params=params,
-    )(own, r2, even, odd)
-    cols, both = pl.pallas_call(
-        trunk_kernel,
-        out_shape=[
-            jax.ShapeDtypeStruct((bins + 2 * HALO, 2 * F2), BF16),
-            jax.ShapeDtypeStruct((2 * bins + 4 * HALO, 2 * F2), BF16),
-        ],
-        in_specs=[smem] + [vmem] * 6,
-        out_specs=[vmem] * 2,
-        scratch_shapes=[pltpu.VMEM((rows, 2 * half), F32)],
-        compiler_params=params,
-    )(chrom_len, window, conv_weight, proj_weight, w_oth, small, cb_oth)
-    cols_far = line_permute(cols, 2)
-    near_both = chan_swap(both)
+    )(own, r2, odd, even)
     mask, packed = pl.pallas_call(
         pack_kernel,
         out_shape=[
@@ -475,7 +469,19 @@
         in_hbm(map_bias[None]),
         in_hbm(head_weight[None]),
     )
-    oth = chan_swap(packed)
+    cols, both = pl.pallas_call(
+        trunk_kernel,
+        out_shape=[
+            jax.ShapeDtypeStruct((bins + 2 * HALO, 2 * F2), BF16),
+            jax.ShapeDtypeStruct((2 * bins + 4 * HALO + 9 * half_out, 2 * F2), BF16),
+        ],
+        in_specs=[smem] + [vmem] * 7,
+        out_specs=[vmem] * 2,
+        scratch_shapes=[pltpu.VMEM((rows, 2 * half), F32)],
+        compiler_params=params,
+    )(chrom_len, window, conv_weight, proj_weight, w_oth, small, cb_oth, packed)
+    cols_far = line_permute(cols, 2)
+    near_both = chan_swap(both)
     prepared = pl.pallas_call(
         prep_kernel,
         out_shape=[
@@ -491,7 +497,7 @@
             pltpu.VMEM((9, F2, F2), F32),
         ],
         compiler_params=params,
-    )(chrom_len, mask, packed, oth)
+    )(chrom_len, mask, packed, near_both)
     tiles = functools.partial(
         pl.pallas_call,
         out_shape=jax.ShapeDtypeStruct((bins, 2 * bins), F32),

time: 15.3 us -> 15.1 us (0.987)
  waiting for transfers between devices: 1.76 us -> 3.71 us
  starting transfers between devices: 6.25 us -> 4.64 us
  local copies, waits for them, and re-layouts: 0.43 us -> 0.01 us
    ppermute x5 -> x4, starting transfers between devices: 2.78 us -> 1.58 us  [chan_swap(): return lax.ppermute(value, 'chan', [(0, 1), (1, 0)])]
    ppermute x5 -> x4, waiting for transfers between devices: 0.31 us -> 1.19 us  [chan_swap(): return lax.ppermute(value, 'chan', [(0, 1), (1, 0)])]
    ppermute x2, waiting for transfers between devices: 1.44 us -> 2.05 us  [line_permute(): return lax.ppermute(value, ('blk', 'chan'), pairs)]
    ppermute x2, starting transfers between devices: 0.53 us -> 0.06 us  [line_permute(): return lax.ppermute(value, ('blk', 'chan'), pairs)]
    ppermute x2, waiting for transfers between devices: 0.01 us -> 0.46 us  [pair_permute(): return lax.ppermute(value, ('blk', 'chan'), pairs)]
    unnamed x4, local copies, waits for them, and re-layouts: 0.43 us -> 0.01 us
  transfers between devices with their start and end apart: 9 -> 8, of which waited for: 3 -> 5; matrix products, arithmetic and copies ran while one was open for 0% -> 0% of each run, Pallas kernels for 23% -> 16%
where the time goes in v8:
time: 15.1 us; the launch traced here: 14.9 us
  Pallas kernels  5.81 us (38%)
  starting transfers between devices  4.64 us (31%)
  waiting for transfers between devices  3.71 us (25%)
  between operations  0.74 us (5%)
    ppermute x2, starting transfers between devices, pair_permute(): return lax.ppermute(value, ('blk', 'chan'), pairs)  3 us
    pallas_call x1, Pallas kernels, local(): tiles(far_kernel, in_specs=[vmem, smem] + [vmem] * 6)  2.48 us
    ppermute x2, waiting for transfers between devices, line_permute(): return lax.ppermute(value, ('blk', 'chan'), pairs)  2.05 us
    ppermute x4, starting transfers between devices, chan_swap(): return lax.ppermute(value, 'chan', [(0, 1), (1, 0)])  1.58 us
    ppermute x4, waiting for transfers between devices, chan_swap(): return lax.ppermute(value, 'chan', [(0, 1), (1, 0)])  1.19 us
    pallas_call x1, Pallas kernels, local(): pl.pallas_call(trunk_kernel, out_shape=[jax.ShapeDtypeStruct((bins + 2 *...  1.02 us
    pallas_call x1, Pallas kernels, local(): pl.pallas_call(pack_kernel, out_shape=[jax.ShapeDtypeStruct(band_mask.sha...  1.01 us
    pallas_call x1, Pallas kernels, local(): pl.pallas_call(front_kernel, out_shape=[jax.ShapeDtypeStruct(features.sha...  0.81 us
  transfers between devices with their start and end apart: 8, of which 5 were waited for; matrix products, arithmetic and copies ran while one was open for 0% of the time, Pallas kernels for 16%

profile of v8, /device:TPU:1, one launch (start us, length us, event | category | flops | bytes accessed | tf_op | source)
XLA Modules:
  0.0 14.9 jit_solution(14210251939883129303)
XLA Ops:
  0.0 0.0 copy-start
  0.0 0.1 collective-permute-start.1
  0.1 0.5 %collective-permute-start = (bf16[64,256]{1,0:T(8,128)(2,1)}, bf16[64,256]{1,0:T(8,128)(2,1)S(1)}, u32[]{:S(2)}, u32[]{:S(2)}) collective-permute-start(bf16[64,256]{1,0:T(8,128)(2,1)} %own_any.1), channel_id=1, source_target_pairs={{0,1},{1,0},{2,3},{3,2},{4,5},{5,4},{6,7},{7,6},{8,9},{9,8},{10,11... | collective-permute-start | bytes 98312 | tf_op jit(solution)/shard_map/ppermute | solution.py:21
  0.5 0.8 %shard_map.100 = (bf16[64,256]{1,0:T(8,128)(2,1)S(1)}, f32[8,256]{1,0:T(8,128)S(1)}) custom-call(bf16[64,256]{1,0:T(8,128)(2,1)} %own_any.1, bf16[2,256]{1,0:T(2,128)(2,1)} %cb_any.1, bf16[1,128]{1,0:T(2,128)(2,1)} %bitcast.11), custom_call_target="tpu_custom_call" | custom-call | flops 500000000 | bytes 1000000 | tf_op jit(solution)/shard_map/pallas_call | solution.py:419
  1.3 0.2 %collective-permute-done = bf16[64,256]{1,0:T(8,128)(2,1)S(1)} collective-permute-done((bf16[64,256]{1,0:T(8,128)(2,1)}, bf16[64,256]{1,0:T(8,128)(2,1)S(1)}, u32[]{:S(2)}, u32[]{:S(2)}) %collective-permute-start) | collective-permute-done | bytes 32800 | tf_op jit(solution)/shard_map/ppermute | solution.py:21
  1.6 0.0 collective-permute-done.1.refs_6_
  1.6 0.0 copy-done
  1.6 0.4 %collective-permute-start.5 = (bf16[2,3,512,256]{3,2,1,0:T(8,128)(2,1)S(1)}, bf16[2,3,512,256]{3,2,1,0:T(8,128)(2,1)S(1)}, u32[]{:S(2)}, u32[]{:S(2)}) collective-permute-start(bf16[2,3,512,256]{3,2,1,0:T(8,128)(2,1)S(1)} %copy-done), channel_id=1, source_target_pairs={{0,1},{1,0},{2,3},{3,2},{4,5},{5,4},{6,7},{7,6},{8,9},{9,8},{10,11... | collective-permute-start | bytes 4718600 | tf_op jit(solution)/shard_map/ppermute | solution.py:21
  2.0 2.4 %collective-permute-start.4 = (bf16[2,64,256]{2,1,0:T(8,128)(2,1)S(1)}, bf16[2,64,256]{2,1,0:T(8,128)(2,1)S(1)}, u32[]{:S(2)}, u32[]{:S(2)}) collective-permute-start(bf16[2,64,256]{2,1,0:T(8,128)(2,1)S(1)} %pad_maximum_fusion.own_ref.after_any), channel_id=1, source_target_pairs={{2,0},{0,2},{6,4},{4,6},{10,8},{8,10},{14,12},{12,14},{3,1},{1,3},... | collective-permute-start | bytes 196616 | tf_op jit(solution)/shard_map/ppermute | solution.py:45
  4.4 0.6 %collective-permute-start.3 = (bf16[2,64,256]{2,1,0:T(8,128)(2,1)S(1)}, bf16[2,64,256]{2,1,0:T(8,128)(2,1)S(1)}, u32[]{:S(2)}, u32[]{:S(2)}) collective-permute-start(bf16[2,64,256]{2,1,0:T(8,128)(2,1)S(1)} %pad_maximum_fusion.own_ref.after_any), channel_id=1, source_target_pairs={{1,0},{0,2},{6,4},{4,6},{10,8},{8,10},{14,12},{15,14},{5,3},{3,5},... | collective-permute-start | bytes 196616 | tf_op jit(solution)/shard_map/ppermute | solution.py:45
  5.0 0.0 collective-permute-start.2
  5.7 1.0 %shard_map.102 = (s32[4,8]{1,0:T(4,128)S(1)}, bf16[288,128]{1,0:T(8,128)(2,1)S(1)}) custom-call(bf16[2,64,256]{2,1,0:T(8,128)(2,1)S(1)} %pad_maximum_fusion.own_ref.after_any, s32[4,8]{1,0:T(4,128)} %bitcast.8, bf16[3,3,32,64]{3,2,1,0:T(8,128)(2,1)} %mw_any.1, bf16[1,32]{1,0:T(2,128)(2,1)} %bitcast.9, bf16[1,32]{1,0:T(2,128)(2,1)} %bitcast.10), custom_call_target="tpu_custom_call" | custom-call | tf_op jit(solution)/shard_map/pallas_call | solution.py:449
  6.7 0.0 copy-start.1
  6.7 0.9 %collective-permute-done.2.r2_ref = bf16[2,16,256]{2,1,0:T(8,128)(2,1)S(1)} collective-permute-done((bf16[2,16,256]{2,1,0:T(8,128)(2,1)S(1)}, bf16[2,16,256]{2,1,0:T(8,128)(2,1)S(1)}, u32[]{:S(2)}, u32[]{:S(2)}) %collective-permute-start.2) | collective-permute-done | bytes 16416 | tf_op jit(solution)/shard_map/ppermute | solution.py:30
  7.6 0.0 collective-permute-done.4.even_ref
  7.6 0.5 %collective-permute-done.3.odd_ref = bf16[2,64,256]{2,1,0:T(8,128)(2,1)S(1)} collective-permute-done((bf16[2,64,256]{2,1,0:T(8,128)(2,1)S(1)}, bf16[2,64,256]{2,1,0:T(8,128)(2,1)S(1)}, u32[]{:S(2)}, u32[]{:S(2)}) %collective-permute-start.3) | collective-permute-done | bytes 65568 | tf_op jit(solution)/shard_map/ppermute | solution.py:45
  8.1 0.0 collective-permute-done.5.refs_4_
  8.1 0.0 copy-done.1
  8.1 1.0 %shard_map.103 = (bf16[80,128]{1,0:T(8,128)(2,1)S(1)}, bf16[448,128]{1,0:T(8,128)(2,1)S(1)}) custom-call(s32[1]{0:T(128)S(6)} %copy.11.refs_0_.length_ref, f32[144,512]{1,0:T(8,128)S(1)} %shard_map.101.refs_1_, bf16[2,3,512,256]{3,2,1,0:T(8,128)(2,1)S(1)} %copy-done, bf16[512,128]{1,0:T(8,128)(2,1)S(1)} %copy-done.1, ...), custom_call_target="tpu_custom_call" | custom-call | tf_op jit(solution)/shard_map/pallas_call | solution.py:472
  9.2 0.7 %collective-permute-start.6 = (bf16[448,128]{1,0:T(8,128)(2,1)S(1)}, bf16[448,128]{1,0:T(8,128)(2,1)S(1)}, u32[]{:S(2)}, u32[]{:S(2)}) collective-permute-start(bf16[448,128]{1,0:T(8,128)(2,1)S(1)} %get-tuple-element.26.refs_2_), channel_id=1, source_target_pairs={{0,1},{1,0},{2,3},{3,2},{4,5},{5,4},{6,7},{7,6},{8,9},{9,8},{10,11... | collective-permute-start | bytes 344072 | tf_op jit(solution)/shard_map/ppermute | solution.py:21
  9.8 0.0 collective-permute-start.7
  9.8 0.9 %collective-permute-done.6.oth_ref.refs_1_.refs_2_ = bf16[448,128]{1,0:T(8,128)(2,1)S(1)} collective-permute-done((bf16[448,128]{1,0:T(8,128)(2,1)S(1)}, bf16[448,128]{1,0:T(8,128)(2,1)S(1)}, u32[]{:S(2)}, u32[]{:S(2)}) %collective-permute-start.6) | collective-permute-done | bytes 114720 | tf_op jit(solution)/shard_map/ppermute | solution.py:21
  10.8 0.5 %shard_map.104 = (f32[3,128,384]{2,1,0:T(8,128)S(1)}, bf16[1152,256]{1,0:T(8,128)(2,1)S(1)}, f32[8,256]{1,0:T(8,128)S(1)}, bf16[16,512]{1,0:T(8,128)(2,1)S(1)}) custom-call(s32[1]{0:T(128)S(6)} %copy.11.refs_0_.length_ref, s32[4,8]{1,0:T(4,128)S(1)} %get-tuple-element.27.mask_ref, bf16[288,128]{1,0:T(8,128)(2,1)S(1)} %get-tuple-element.25.refs_7_.own_ref, ...), custom_call_target="tpu_custom_call" | custom-call | tf_op jit(solution)/shard_map/pallas_call | solution.py:485
  11.3 1.2 %collective-permute-done.7.refs_1_ = bf16[80,128]{1,0:T(8,128)(2,1)S(1)} collective-permute-done((bf16[80,128]{1,0:T(8,128)(2,1)S(1)}, bf16[80,128]{1,0:T(8,128)(2,1)S(1)}, u32[]{:S(2)}, u32[]{:S(2)}) %collective-permute-start.7) | collective-permute-done | bytes 20512 | tf_op jit(solution)/shard_map/ppermute | solution.py:30
  12.4 2.5 %shard_map.106 = f32[64,128]{1,0:T(8,128)} custom-call(f32[64,128]{1,0:T(8,128)S(1)} %shard_map.105.near_ref, s32[1]{0:T(128)S(6)} %copy.11.refs_0_.length_ref, bf16[80,128]{1,0:T(8,128)(2,1)S(1)} %collective-permute-done.7.refs_1_, bf16[448,128]{1,0:T(8,128)(2,1)S(1)} %get-tuple-element.26.refs_2_, f32[3,128,384]{2,1,0:T(8,128)S(1)} %get-tuple-element.28.refs_3_, ...), custom_call_target="tpu_custom_call" | custom-call | tf_op jit(solution)/shard_map/pallas_call | solution.py:514
  (4 shorter events, 0.0 us)
Async XLA Ops:
  0.0 1.6 %copy-start = (bf16[2,3,512,256]{3,2,1,0:T(8,128)(2,1)S(1)}, bf16[2,3,512,256]{3,2,1,0:T(8,128)(2,1)}, u32[]{:S(2)}) copy-start(bf16[2,3,512,256]{3,2,1,0:T(8,128)(2,1)} %refs_2_.1) | copy-start | bytes 4718596
  0.0 1.6 %collective-permute-start.1 = (bf16[2,256]{1,0:T(2,128)(2,1)}, bf16[2,256]{1,0:T(2,128)(2,1)S(1)}, u32[]{:S(2)}, u32[]{:S(2)}) collective-permute-start(bf16[2,256]{1,0:T(2,128)(2,1)} %cb_any.1), channel_id=1, source_target_pairs={{0,1},{1,0},{2,3},{3,2},{4,5},{5,4},{6,7},{7,6},{8,9},{9,8},{10,11... | collective-permute-start | bytes 3080 | tf_op jit(solution)/shard_map/ppermute | solution.py:21
  0.1 1.5 %collective-permute-start = (bf16[64,256]{1,0:T(8,128)(2,1)}, bf16[64,256]{1,0:T(8,128)(2,1)S(1)}, u32[]{:S(2)}, u32[]{:S(2)}) collective-permute-start(bf16[64,256]{1,0:T(8,128)(2,1)} %own_any.1), channel_id=1, source_target_pairs={{0,1},{1,0},{2,3},{3,2},{4,5},{5,4},{6,7},{7,6},{8,9},{9,8},{10,11... | collective-permute-start | bytes 98312 | tf_op jit(solution)/shard_map/ppermute | solution.py:21
  1.6 6.5 %collective-permute-start.5 = (bf16[2,3,512,256]{3,2,1,0:T(8,128)(2,1)S(1)}, bf16[2,3,512,256]{3,2,1,0:T(8,128)(2,1)S(1)}, u32[]{:S(2)}, u32[]{:S(2)}) collective-permute-start(bf16[2,3,512,256]{3,2,1,0:T(8,128)(2,1)S(1)} %copy-done), channel_id=1, source_target_pairs={{0,1},{1,0},{2,3},{3,2},{4,5},{5,4},{6,7},{7,6},{8,9},{9,8},{10,11... | collective-permute-start | bytes 4718600 | tf_op jit(solution)/shard_map/ppermute | solution.py:21
  2.0 5.6 %collective-permute-start.4 = (bf16[2,64,256]{2,1,0:T(8,128)(2,1)S(1)}, bf16[2,64,256]{2,1,0:T(8,128)(2,1)S(1)}, u32[]{:S(2)}, u32[]{:S(2)}) collective-permute-start(bf16[2,64,256]{2,1,0:T(8,128)(2,1)S(1)} %pad_maximum_fusion.own_ref.after_any), channel_id=1, source_target_pairs={{2,0},{0,2},{6,4},{4,6},{10,8},{8,10},{14,12},{12,14},{3,1},{1,3},... | collective-permute-start | bytes 196616 | tf_op jit(solution)/shard_map/ppermute | solution.py:45
  4.4 3.7 %collective-permute-start.3 = (bf16[2,64,256]{2,1,0:T(8,128)(2,1)S(1)}, bf16[2,64,256]{2,1,0:T(8,128)(2,1)S(1)}, u32[]{:S(2)}, u32[]{:S(2)}) collective-permute-start(bf16[2,64,256]{2,1,0:T(8,128)(2,1)S(1)} %pad_maximum_fusion.own_ref.after_any), channel_id=1, source_target_pairs={{1,0},{0,2},{6,4},{4,6},{10,8},{8,10},{14,12},{15,14},{5,3},{3,5},... | collective-permute-start | bytes 196616 | tf_op jit(solution)/shard_map/ppermute | solution.py:45
  5.0 2.6 %collective-permute-start.2 = (bf16[2,16,256]{2,1,0:T(8,128)(2,1)S(1)}, bf16[2,16,256]{2,1,0:T(8,128)(2,1)S(1)}, u32[]{:S(2)}, u32[]{:S(2)}) collective-permute-start(bf16[2,16,256]{2,1,0:T(8,128)(2,1)S(1)} %slice.3), channel_id=1, source_target_pairs={{1,0},{5,1},{3,2},{7,3},{0,4},{9,5},{2,6},{11,7},{4,8},{13,9},{6,1... | collective-permute-start | bytes 49160 | tf_op jit(solution)/shard_map/ppermute | solution.py:30
  6.7 1.4 %copy-start.1 = (bf16[512,128]{1,0:T(8,128)(2,1)S(1)}, bf16[512,128]{1,0:T(8,128)(2,1)}, u32[]{:S(2)}) copy-start(bf16[512,128]{1,0:T(8,128)(2,1)} %refs_3_.1) | copy-start | bytes 393220
  9.2 1.6 %collective-permute-start.6 = (bf16[448,128]{1,0:T(8,128)(2,1)S(1)}, bf16[448,128]{1,0:T(8,128)(2,1)S(1)}, u32[]{:S(2)}, u32[]{:S(2)}) collective-permute-start(bf16[448,128]{1,0:T(8,128)(2,1)S(1)} %get-tuple-element.26.refs_2_), channel_id=1, source_target_pairs={{0,1},{1,0},{2,3},{3,2},{4,5},{5,4},{6,7},{7,6},{8,9},{9,8},{10,11... | collective-permute-start | bytes 344072 | tf_op jit(solution)/shard_map/ppermute | solution.py:21
  9.8 2.6 %collective-permute-start.7 = (bf16[80,128]{1,0:T(8,128)(2,1)S(1)}, bf16[80,128]{1,0:T(8,128)(2,1)S(1)}, u32[]{:S(2)}, u32[]{:S(2)}) collective-permute-start(bf16[80,128]{1,0:T(8,128)(2,1)S(1)} %get-tuple-element.32), channel_id=1, source_target_pairs={{1,0},{5,1},{3,2},{7,3},{0,4},{9,5},{2,6},{11,7},{4,8},{13,9},{6,1... | collective-permute-start | bytes 61448 | tf_op jit(solution)/shard_map/ppermute | solution.py:30

commit v9 on v8

--- a/solution.py
+++ b/solution.py
@@ -45,8 +45,10 @@
     return lax.ppermute(value, ("blk", "chan"), pairs)
 
 
-def front_kernel(own_any, cb_any, pb_any, own_ref, small_ref, cb_s, pb_s, sems):
-    pairs = ((cb_any, cb_s), (pb_any, pb_s), (own_any, own_ref))
+def front_kernel(
+    own_any, cb_any, pb_any, pw_any, own_ref, small_ref, pw_ref, cb_s, pb_s, sems
+):
+    pairs = ((cb_any, cb_s), (pb_any, pb_s), (own_any, own_ref), (pw_any, pw_ref))
     copies = [
         pltpu.make_async_copy(source, target, sems.at[at])
         for at, (source, target) in enumerate(pairs)
@@ -57,7 +59,8 @@
     copies[1].wait()
     small_ref[0:CONV1, :] = cb_s[...].astype(F32)
     small_ref[CONV1 : CONV1 + 1, : 2 * F2] = pb_s[...].astype(F32)
-    copies[2].wait()
+    for copy in copies[2:]:
+        copy.wait()
 
 
 def pack_kernel(
@@ -381,13 +384,18 @@
                 mix_s[group, :, v * 4 * F2 : (v + 1) * 4 * F2] = mixed.astype(BF16)
 
     lane_live = side_ref[1:2, : 2 * F2] != 0
+    value = lax.dot_general(
+        head_ref[...],
+        mix_s[...].reshape(groups * 2 * bins, 8 * F2),
+        (((1,), (1,)), ((), ())),
+        preferred_element_type=F32,
+    )
     for group in range(groups):
-        value = lax.dot_general(
-            head_ref[...], mix_s[group], (((1,), (1,)), ((), ())), preferred_element_type=F32
-        )[:8]
         bin_index = i * bins + 8 * group + lax.broadcasted_iota(jnp.int32, (8, 2 * bins), 0)
         out_ref[8 * group : 8 * group + 8, :] = jnp.where(
-            lane_live & (bin_index < length_ref[0]), value, 0.0
+            lane_live & (bin_index < length_ref[0]),
+            value[:8, 2 * bins * group : 2 * bins * (group + 1)],
+            0.0,
         )
 
 
@@ -416,22 +424,23 @@
 
     other = chan_swap(features)
     cb_oth = chan_swap(conv_bias)
-    own, small = pl.pallas_call(
+    own, small, pw = pl.pallas_call(
         front_kernel,
         out_shape=[
             jax.ShapeDtypeStruct(features.shape, BF16),
             jax.ShapeDtypeStruct((8, half), F32),
-        ],
-        in_specs=[anywhere] * 3,
-        out_specs=[vmem] * 2,
+            jax.ShapeDtypeStruct(proj_weight.shape, BF16),
+        ],
+        in_specs=[anywhere] * 4,
+        out_specs=[vmem] * 3,
         scratch_shapes=[
             pltpu.VMEM(conv_bias.shape, BF16),
             pltpu.VMEM((1, 2 * F2), BF16),
-            pltpu.SemaphoreType.DMA((3,)),
+            pltpu.SemaphoreType.DMA((4,)),
         ],
         cost_estimate=pl.CostEstimate(flops=500000000, bytes_accessed=1000000, transcendentals=0),
         compiler_params=params,
-    )(in_hbm(features), in_hbm(conv_bias), in_hbm(proj_bias[None]))
+    )(in_hbm(features), in_hbm(conv_bias), in_hbm(proj_bias[None]), in_hbm(proj_weight))
     own, cb_oth = lax.optimization_barrier((jnp.stack([own, other]), cb_oth))
     even = pair_permute(own, 0)
     odd = pair_permute(own, 1)
@@ -479,7 +488,7 @@
         out_specs=[vmem] * 2,
         scratch_shapes=[pltpu.VMEM((rows, 2 * half), F32)],
         compiler_params=params,
-    )(chrom_len, window, conv_weight, proj_weight, w_oth, small, cb_oth, packed)
+    )(chrom_len, window, conv_weight, pw, w_oth, small, cb_oth, packed)
     cols_far = line_permute(cols, 2)
     near_both = chan_swap(both)
     prepared = pl.pallas_call(

time: 15.1 us -> 15 us (level)
  Pallas kernels: 5.81 us -> 5.99 us
    ppermute x4, starting transfers between devices: 1.58 us -> 1 us  [chan_swap(): return lax.ppermute(value, 'chan', [(0, 1), (1, 0)])]
    ppermute x2, starting transfers between devices: 0.06 us -> 0.53 us  [line_permute(): return lax.ppermute(value, ('blk', 'chan'), pairs)]
    ppermute x4, waiting for transfers between devices: 1.19 us -> 0.89 us  [chan_swap(): return lax.ppermute(value, 'chan', [(0, 1), (1, 0)])]
    ppermute x2, waiting for transfers between devices: 2.05 us -> 2.23 us  [line_permute(): return lax.ppermute(value, ('blk', 'chan'), pairs)]
    pallas_call x1, Pallas kernels: 0.81 us -> 0.99 us  [local(): pl.pallas_call(front_kernel, out_shape=[jax.ShapeDtypeStruct(features.sha...]
  transfers between devices with their start and end apart: 8 -> 8, of which waited for: 5 -> 5; matrix products, arithmetic and copies ran while one was open for 0% -> 0% of each run, Pallas kernels for 16% -> 17%
where the time goes in v9:
time: 15 us; the launch traced here: 14.8 us
  Pallas kernels  5.99 us (40%)
  starting transfers between devices  4.53 us (30%)
  waiting for transfers between devices  3.58 us (24%)
  between operations  0.74 us (5%)
    ppermute x2, starting transfers between devices, pair_permute(): return lax.ppermute(value, ('blk', 'chan'), pairs)  3 us
    pallas_call x1, Pallas kernels, local(): tiles(far_kernel, in_specs=[vmem, smem] + [vmem] * 6)  2.49 us
    ppermute x2, waiting for transfers between devices, line_permute(): return lax.ppermute(value, ('blk', 'chan'), pairs)  2.23 us
    pallas_call x1, Pallas kernels, local(): pl.pallas_call(pack_kernel, out_shape=[jax.ShapeDtypeStruct(band_mask.sha...  1.01 us
    pallas_call x1, Pallas kernels, local(): pl.pallas_call(trunk_kernel, out_shape=[jax.ShapeDtypeStruct((bins + 2 *...  1.01 us
    ppermute x4, starting transfers between devices, chan_swap(): return lax.ppermute(value, 'chan', [(0, 1), (1, 0)])  1 us
    pallas_call x1, Pallas kernels, local(): pl.pallas_call(front_kernel, out_shape=[jax.ShapeDtypeStruct(features.sha...  0.99 us
    ppermute x4, waiting for transfers between devices, chan_swap(): return lax.ppermute(value, 'chan', [(0, 1), (1, 0)])  0.89 us
  transfers between devices with their start and end apart: 8, of which 5 were waited for; matrix products, arithmetic and copies ran while one was open for 0% of the time, Pallas kernels for 17%

profile of v9, /device:TPU:1, one launch (start us, length us, event | category | flops | bytes accessed | tf_op | source)
XLA Modules:
  0.0 14.8 jit_solution(14689230144607928795)
XLA Ops:
  0.0 0.0 copy-start
  0.0 0.1 collective-permute-start.1
  0.1 0.5 %collective-permute-start = (bf16[64,256]{1,0:T(8,128)(2,1)}, bf16[64,256]{1,0:T(8,128)(2,1)S(1)}, u32[]{:S(2)}, u32[]{:S(2)}) collective-permute-start(bf16[64,256]{1,0:T(8,128)(2,1)} %own_any.1), channel_id=1, source_target_pairs={{0,1},{1,0},{2,3},{3,2},{4,5},{5,4},{6,7},{7,6},{8,9},{9,8},{10,11... | collective-permute-start | bytes 98312 | tf_op jit(solution)/shard_map/ppermute | solution.py:21
  0.5 1.0 %shard_map.100 = (bf16[64,256]{1,0:T(8,128)(2,1)S(1)}, f32[8,256]{1,0:T(8,128)S(1)}, bf16[512,128]{1,0:T(8,128)(2,1)S(1)}) custom-call(bf16[64,256]{1,0:T(8,128)(2,1)} %own_any.1, bf16[2,256]{1,0:T(2,128)(2,1)} %cb_any.1, bf16[1,128]{1,0:T(2,128)(2,1)} %bitcast.11, bf16[512,128]{1,0:T(8,128)(2,1)} %pw_any.1), custom_call_target="tpu_custom_call" | custom-call | flops 500000000 | bytes 1000000 | tf_op jit(solution)/shard_map/pallas_call | solution.py:427
  1.5 0.1 collective-permute-done
  1.6 0.0 collective-permute-done.1.refs_6_
  1.6 0.0 copy-done
  1.6 0.4 %collective-permute-start.5 = (bf16[2,3,512,256]{3,2,1,0:T(8,128)(2,1)S(1)}, bf16[2,3,512,256]{3,2,1,0:T(8,128)(2,1)S(1)}, u32[]{:S(2)}, u32[]{:S(2)}) collective-permute-start(bf16[2,3,512,256]{3,2,1,0:T(8,128)(2,1)S(1)} %copy-done), channel_id=1, source_target_pairs={{0,1},{1,0},{2,3},{3,2},{4,5},{5,4},{6,7},{7,6},{8,9},{9,8},{10,11... | collective-permute-start | bytes 4718600 | tf_op jit(solution)/shard_map/ppermute | solution.py:21
  2.0 2.4 %collective-permute-start.4 = (bf16[2,64,256]{2,1,0:T(8,128)(2,1)S(1)}, bf16[2,64,256]{2,1,0:T(8,128)(2,1)S(1)}, u32[]{:S(2)}, u32[]{:S(2)}) collective-permute-start(bf16[2,64,256]{2,1,0:T(8,128)(2,1)S(1)} %pad_maximum_fusion.own_ref.after_any), channel_id=1, source_target_pairs={{2,0},{0,2},{6,4},{4,6},{10,8},{8,10},{14,12},{12,14},{3,1},{1,3},... | collective-permute-start | bytes 196616 | tf_op jit(solution)/shard_map/ppermute | solution.py:45
  4.4 0.6 %collective-permute-start.3 = (bf16[2,64,256]{2,1,0:T(8,128)(2,1)S(1)}, bf16[2,64,256]{2,1,0:T(8,128)(2,1)S(1)}, u32[]{:S(2)}, u32[]{:S(2)}) collective-permute-start(bf16[2,64,256]{2,1,0:T(8,128)(2,1)S(1)} %pad_maximum_fusion.own_ref.after_any), channel_id=1, source_target_pairs={{1,0},{0,2},{6,4},{4,6},{10,8},{8,10},{14,12},{15,14},{5,3},{3,5},... | collective-permute-start | bytes 196616 | tf_op jit(solution)/shard_map/ppermute | solution.py:45
  5.0 0.0 collective-permute-start.2
  5.7 1.0 %shard_map.102 = (s32[4,8]{1,0:T(4,128)S(1)}, bf16[288,128]{1,0:T(8,128)(2,1)S(1)}) custom-call(bf16[2,64,256]{2,1,0:T(8,128)(2,1)S(1)} %pad_maximum_fusion.own_ref.after_any, s32[4,8]{1,0:T(4,128)} %bitcast.8, bf16[3,3,32,64]{3,2,1,0:T(8,128)(2,1)} %mw_any.1, bf16[1,32]{1,0:T(2,128)(2,1)} %bitcast.9, bf16[1,32]{1,0:T(2,128)(2,1)} %bitcast.10), custom_call_target="tpu_custom_call" | custom-call | tf_op jit(solution)/shard_map/pallas_call | solution.py:458
  6.7 0.9 %collective-permute-done.2.r2_ref = bf16[2,16,256]{2,1,0:T(8,128)(2,1)S(1)} collective-permute-done((bf16[2,16,256]{2,1,0:T(8,128)(2,1)S(1)}, bf16[2,16,256]{2,1,0:T(8,128)(2,1)S(1)}, u32[]{:S(2)}, u32[]{:S(2)}) %collective-permute-start.2) | collective-permute-done | bytes 16416 | tf_op jit(solution)/shard_map/ppermute | solution.py:30
  7.6 0.0 collective-permute-done.4.even_ref
  7.6 0.5 %collective-permute-done.3.odd_ref = bf16[2,64,256]{2,1,0:T(8,128)(2,1)S(1)} collective-permute-done((bf16[2,64,256]{2,1,0:T(8,128)(2,1)S(1)}, bf16[2,64,256]{2,1,0:T(8,128)(2,1)S(1)}, u32[]{:S(2)}, u32[]{:S(2)}) %collective-permute-start.3) | collective-permute-done | bytes 65568 | tf_op jit(solution)/shard_map/ppermute | solution.py:45
  8.1 0.0 collective-permute-done.5.refs_4_
  8.1 1.0 %shard_map.103 = (bf16[80,128]{1,0:T(8,128)(2,1)S(1)}, bf16[448,128]{1,0:T(8,128)(2,1)S(1)}) custom-call(s32[1]{0:T(128)S(6)} %copy.11.refs_0_.length_ref, f32[144,512]{1,0:T(8,128)S(1)} %shard_map.101.refs_1_, bf16[2,3,512,256]{3,2,1,0:T(8,128)(2,1)S(1)} %copy-done, bf16[512,128]{1,0:T(8,128)(2,1)S(1)} %get-tuple-element.23.refs_3_, ...), custom_call_target="tpu_custom_call" | custom-call | tf_op jit(solution)/shard_map/pallas_call | solution.py:481
  9.1 0.1 collective-permute-start.6
  9.2 0.5 %collective-permute-start.7 = (bf16[80,128]{1,0:T(8,128)(2,1)S(1)}, bf16[80,128]{1,0:T(8,128)(2,1)S(1)}, u32[]{:S(2)}, u32[]{:S(2)}) collective-permute-start(bf16[80,128]{1,0:T(8,128)(2,1)S(1)} %get-tuple-element.34), channel_id=1, source_target_pairs={{1,0},{5,1},{3,2},{7,3},{0,4},{9,5},{2,6},{11,7},{4,8},{13,9},{6,1... | collective-permute-start | bytes 61448 | tf_op jit(solution)/shard_map/ppermute | solution.py:30
  9.7 0.8 %collective-permute-done.6.oth_ref.refs_1_.refs_2_ = bf16[448,128]{1,0:T(8,128)(2,1)S(1)} collective-permute-done((bf16[448,128]{1,0:T(8,128)(2,1)S(1)}, bf16[448,128]{1,0:T(8,128)(2,1)S(1)}, u32[]{:S(2)}, u32[]{:S(2)}) %collective-permute-start.6) | collective-permute-done | bytes 114720 | tf_op jit(solution)/shard_map/ppermute | solution.py:21
  10.5 0.5 %shard_map.104 = (f32[3,128,384]{2,1,0:T(8,128)S(1)}, bf16[1152,256]{1,0:T(8,128)(2,1)S(1)}, f32[8,256]{1,0:T(8,128)S(1)}, bf16[16,512]{1,0:T(8,128)(2,1)S(1)}) custom-call(s32[1]{0:T(128)S(6)} %copy.11.refs_0_.length_ref, s32[4,8]{1,0:T(4,128)S(1)} %get-tuple-element.29.mask_ref, bf16[288,128]{1,0:T(8,128)(2,1)S(1)} %get-tuple-element.27.refs_7_.own_ref, ...), custom_call_target="tpu_custom_call" | custom-call | tf_op jit(solution)/shard_map/pallas_call | solution.py:494
  11.0 1.3 %collective-permute-done.7.refs_1_ = bf16[80,128]{1,0:T(8,128)(2,1)S(1)} collective-permute-done((bf16[80,128]{1,0:T(8,128)(2,1)S(1)}, bf16[80,128]{1,0:T(8,128)(2,1)S(1)}, u32[]{:S(2)}, u32[]{:S(2)}) %collective-permute-start.7) | collective-permute-done | bytes 20512 | tf_op jit(solution)/shard_map/ppermute | solution.py:30
  12.4 2.5 %shard_map.106 = f32[64,128]{1,0:T(8,128)} custom-call(f32[64,128]{1,0:T(8,128)S(1)} %shard_map.105.near_ref, s32[1]{0:T(128)S(6)} %copy.11.refs_0_.length_ref, bf16[80,128]{1,0:T(8,128)(2,1)S(1)} %collective-permute-done.7.refs_1_, bf16[448,128]{1,0:T(8,128)(2,1)S(1)} %get-tuple-element.28.refs_2_, f32[3,128,384]{2,1,0:T(8,128)S(1)} %get-tuple-element.30.refs_3_, ...), custom_call_target="tpu_custom_call" | custom-call | tf_op jit(solution)/shard_map/pallas_call | solution.py:523
  (4 shorter events, 0.0 us)
Async XLA Ops:
  0.0 1.6 %copy-start = (bf16[2,3,512,256]{3,2,1,0:T(8,128)(2,1)S(1)}, bf16[2,3,512,256]{3,2,1,0:T(8,128)(2,1)}, u32[]{:S(2)}) copy-start(bf16[2,3,512,256]{3,2,1,0:T(8,128)(2,1)} %refs_2_.1) | copy-start | bytes 4718596
  0.0 1.6 %collective-permute-start.1 = (bf16[2,256]{1,0:T(2,128)(2,1)}, bf16[2,256]{1,0:T(2,128)(2,1)S(1)}, u32[]{:S(2)}, u32[]{:S(2)}) collective-permute-start(bf16[2,256]{1,0:T(2,128)(2,1)} %cb_any.1), channel_id=1, source_target_pairs={{0,1},{1,0},{2,3},{3,2},{4,5},{5,4},{6,7},{7,6},{8,9},{9,8},{10,11... | collective-permute-start | bytes 3080 | tf_op jit(solution)/shard_map/ppermute | solution.py:21
  0.1 1.5 %collective-permute-start = (bf16[64,256]{1,0:T(8,128)(2,1)}, bf16[64,256]{1,0:T(8,128)(2,1)S(1)}, u32[]{:S(2)}, u32[]{:S(2)}) collective-permute-start(bf16[64,256]{1,0:T(8,128)(2,1)} %own_any.1), channel_id=1, source_target_pairs={{0,1},{1,0},{2,3},{3,2},{4,5},{5,4},{6,7},{7,6},{8,9},{9,8},{10,11... | collective-permute-start | bytes 98312 | tf_op jit(solution)/shard_map/ppermute | solution.py:21
  1.6 6.5 %collective-permute-start.5 = (bf16[2,3,512,256]{3,2,1,0:T(8,128)(2,1)S(1)}, bf16[2,3,512,256]{3,2,1,0:T(8,128)(2,1)S(1)}, u32[]{:S(2)}, u32[]{:S(2)}) collective-permute-start(bf16[2,3,512,256]{3,2,1,0:T(8,128)(2,1)S(1)} %copy-done), channel_id=1, source_target_pairs={{0,1},{1,0},{2,3},{3,2},{4,5},{5,4},{6,7},{7,6},{8,9},{9,8},{10,11... | collective-permute-start | bytes 4718600 | tf_op jit(solution)/shard_map/ppermute | solution.py:21
  2.0 5.6 %collective-permute-start.4 = (bf16[2,64,256]{2,1,0:T(8,128)(2,1)S(1)}, bf16[2,64,256]{2,1,0:T(8,128)(2,1)S(1)}, u32[]{:S(2)}, u32[]{:S(2)}) collective-permute-start(bf16[2,64,256]{2,1,0:T(8,128)(2,1)S(1)} %pad_maximum_fusion.own_ref.after_any), channel_id=1, source_target_pairs={{2,0},{0,2},{6,4},{4,6},{10,8},{8,10},{14,12},{12,14},{3,1},{1,3},... | collective-permute-start | bytes 196616 | tf_op jit(solution)/shard_map/ppermute | solution.py:45
  4.4 3.7 %collective-permute-start.3 = (bf16[2,64,256]{2,1,0:T(8,128)(2,1)S(1)}, bf16[2,64,256]{2,1,0:T(8,128)(2,1)S(1)}, u32[]{:S(2)}, u32[]{:S(2)}) collective-permute-start(bf16[2,64,256]{2,1,0:T(8,128)(2,1)S(1)} %pad_maximum_fusion.own_ref.after_any), channel_id=1, source_target_pairs={{1,0},{0,2},{6,4},{4,6},{10,8},{8,10},{14,12},{15,14},{5,3},{3,5},... | collective-permute-start | bytes 196616 | tf_op jit(solution)/shard_map/ppermute | solution.py:45
  5.0 2.6 %collective-permute-start.2 = (bf16[2,16,256]{2,1,0:T(8,128)(2,1)S(1)}, bf16[2,16,256]{2,1,0:T(8,128)(2,1)S(1)}, u32[]{:S(2)}, u32[]{:S(2)}) collective-permute-start(bf16[2,16,256]{2,1,0:T(8,128)(2,1)S(1)} %slice.3), channel_id=1, source_target_pairs={{1,0},{5,1},{3,2},{7,3},{0,4},{9,5},{2,6},{11,7},{4,8},{13,9},{6,1... | collective-permute-start | bytes 49160 | tf_op jit(solution)/shard_map/ppermute | solution.py:30
  9.1 1.4 %collective-permute-start.6 = (bf16[448,128]{1,0:T(8,128)(2,1)S(1)}, bf16[448,128]{1,0:T(8,128)(2,1)S(1)}, u32[]{:S(2)}, u32[]{:S(2)}) collective-permute-start(bf16[448,128]{1,0:T(8,128)(2,1)S(1)} %get-tuple-element.28.refs_2_), channel_id=1, source_target_pairs={{0,1},{1,0},{2,3},{3,2},{4,5},{5,4},{6,7},{7,6},{8,9},{9,8},{10,11... | collective-permute-start | bytes 344072 | tf_op jit(solution)/shard_map/ppermute | solution.py:21
  9.2 3.1 %collective-permute-start.7 = (bf16[80,128]{1,0:T(8,128)(2,1)S(1)}, bf16[80,128]{1,0:T(8,128)(2,1)S(1)}, u32[]{:S(2)}, u32[]{:S(2)}) collective-permute-start(bf16[80,128]{1,0:T(8,128)(2,1)S(1)} %get-tuple-element.34), channel_id=1, source_target_pairs={{1,0},{5,1},{3,2},{7,3},{0,4},{9,5},{2,6},{11,7},{4,8},{13,9},{6,1... | collective-permute-start | bytes 61448 | tf_op jit(solution)/shard_map/ppermute | solution.py:30

commit v10 on v8

--- a/solution.py
+++ b/solution.py
@@ -216,7 +216,7 @@
 
 
 def trunk_kernel(*refs):
-    packed_ref, cols_ref, both_ref = refs[-4:-1]
+    packed_ref, cols_ref, both_ref = refs[-3:]
     ready = both_ref.shape[0] - packed_ref.shape[0]
     both_ref[ready:, :] = packed_ref[...]
 
@@ -241,7 +241,6 @@
     packed_ref,
     cols_ref,
     both_ref,
-    h_s,
 ):
     rows = window_ref.shape[0]
     half = window_ref.shape[1] // 2
@@ -253,26 +252,25 @@
     valid = (bin_index >= 0) & (bin_index < length_ref[0])
     inside = ((bin_index >= 0) & (bin_index < count * bins))[:, :1]
 
-    for at in range(0, 2 * half, 128):
-        h_s[:, at : at + 128] = jnp.where(valid, window_ref[:, at : at + 128], 0.0)
-
+    wide = jnp.concatenate([valid] * (2 * half // 128), axis=1)
+    hidden = jnp.where(wide, window_ref[...], 0.0)
     for layer in range(CONV1):
         e = 2 ** (layer + 1)
-        hidden = h_s[...]
         taps = [
             (hidden if t == 1 else pltpu.roll(hidden, ((1 - t) * e) % rows, axis=0)).astype(BF16)
             for t in range(3)
         ]
-        for at, w_ref, bias_ref in ((half, w_own_ref, small_ref), (0, w_oth_ref, cb_oth_ref)):
+        sides = []
+        for at, w_ref, bias_ref in ((0, w_oth_ref, cb_oth_ref), (half, w_own_ref, small_ref)):
             q = jnp.dot(taps[0], w_ref[layer, 0], preferred_element_type=F32)
             q = q + jnp.dot(taps[1], w_ref[layer, 1], preferred_element_type=F32)
             q = q + jnp.dot(taps[2], w_ref[layer, 2], preferred_element_type=F32)
             bias = bias_ref[...].astype(F32)[layer : layer + 1, :]
-            lanes = slice(at, at + half)
-            new = (h_s[:, lanes] + jnp.maximum(q + bias, 0.0)).astype(BF16).astype(F32)
-            h_s[:, lanes] = jnp.where(inside, new, 0.0)
-
-    proj = jnp.dot(h_s[...].astype(BF16), pw_ref[...], preferred_element_type=F32)
+            new = (hidden[:, at : at + half] + jnp.maximum(q + bias, 0.0)).astype(BF16)
+            sides.append(jnp.where(inside, new.astype(F32), 0.0))
+        hidden = jnp.concatenate(sides, axis=1)
+
+    proj = jnp.dot(hidden.astype(BF16), pw_ref[...], preferred_element_type=F32)
     proj = (proj + small_ref[CONV1 : CONV1 + 1, : 2 * F2]).astype(BF16).astype(F32)
     low = lax.broadcasted_iota(jnp.int32, (1, 2 * F2), 1) < F2
     turned = pltpu.roll(proj, F2, axis=1)
@@ -477,7 +475,6 @@
         ],
         in_specs=[smem] + [vmem] * 7,
         out_specs=[vmem] * 2,
-        scratch_shapes=[pltpu.VMEM((rows, 2 * half), F32)],
         compiler_params=params,
     )(chrom_len, window, conv_weight, proj_weight, w_oth, small, cb_oth, packed)
     cols_far = line_permute(cols, 2)

time: 15.1 us -> 15.1 us (level)
  no operation moved by 1% of the time
where the time goes in v10:
time: 15.1 us; the launch traced here: 14.9 us
  Pallas kernels  5.8 us (38%)
  starting transfers between devices  4.65 us (31%)
  waiting for transfers between devices  3.71 us (25%)
  between operations  0.74 us (5%)
    ppermute x2, starting transfers between devices, pair_permute(): return lax.ppermute(value, ('blk', 'chan'), pairs)  3 us
    pallas_call x1, Pallas kernels, local(): tiles(far_kernel, in_specs=[vmem, smem] + [vmem] * 6)  2.48 us
    ppermute x2, waiting for transfers between devices, line_permute(): return lax.ppermute(value, ('blk', 'chan'), pairs)  2.05 us
    ppermute x4, starting transfers between devices, chan_swap(): return lax.ppermute(value, 'chan', [(0, 1), (1, 0)])  1.59 us
    ppermute x4, waiting for transfers between devices, chan_swap(): return lax.ppermute(value, 'chan', [(0, 1), (1, 0)])  1.19 us
    pallas_call x1, Pallas kernels, local(): pl.pallas_call(pack_kernel, out_shape=[jax.ShapeDtypeStruct(band_mask.sha...  1.01 us
    pallas_call x1, Pallas kernels, local(): pl.pallas_call(trunk_kernel, out_shape=[jax.ShapeDtypeStruct((bins + 2 *...  1 us
    pallas_call x1, Pallas kernels, local(): pl.pallas_call(front_kernel, out_shape=[jax.ShapeDtypeStruct(features.sha...  0.81 us
  transfers between devices with their start and end apart: 8, of which 5 were waited for; matrix products, arithmetic and copies ran while one was open for 0% of the time, Pallas kernels for 16%

profile of v10, /device:TPU:1, one launch (start us, length us, event | category | flops | bytes accessed | tf_op | source)
XLA Modules:
  0.0 14.9 jit_solution(4353736750569945403)
XLA Ops:
  0.0 0.0 copy-start
  0.0 0.1 collective-permute-start.1
  0.1 0.5 %collective-permute-start = (bf16[64,256]{1,0:T(8,128)(2,1)}, bf16[64,256]{1,0:T(8,128)(2,1)S(1)}, u32[]{:S(2)}, u32[]{:S(2)}) collective-permute-start(bf16[64,256]{1,0:T(8,128)(2,1)} %own_any.1), channel_id=1, source_target_pairs={{0,1},{1,0},{2,3},{3,2},{4,5},{5,4},{6,7},{7,6},{8,9},{9,8},{10,11... | collective-permute-start | bytes 98312 | tf_op jit(solution)/shard_map/ppermute | solution.py:21
  0.5 0.8 %shard_map.100 = (bf16[64,256]{1,0:T(8,128)(2,1)S(1)}, f32[8,256]{1,0:T(8,128)S(1)}) custom-call(bf16[64,256]{1,0:T(8,128)(2,1)} %own_any.1, bf16[2,256]{1,0:T(2,128)(2,1)} %cb_any.1, bf16[1,128]{1,0:T(2,128)(2,1)} %bitcast.11), custom_call_target="tpu_custom_call" | custom-call | flops 500000000 | bytes 1000000 | tf_op jit(solution)/shard_map/pallas_call | solution.py:417
  1.3 0.2 %collective-permute-done = bf16[64,256]{1,0:T(8,128)(2,1)S(1)} collective-permute-done((bf16[64,256]{1,0:T(8,128)(2,1)}, bf16[64,256]{1,0:T(8,128)(2,1)S(1)}, u32[]{:S(2)}, u32[]{:S(2)}) %collective-permute-start) | collective-permute-done | bytes 32800 | tf_op jit(solution)/shard_map/ppermute | solution.py:21
  1.6 0.0 collective-permute-done.1.refs_6_
  1.6 0.0 copy-done
  1.6 0.4 %collective-permute-start.5 = (bf16[2,3,512,256]{3,2,1,0:T(8,128)(2,1)S(1)}, bf16[2,3,512,256]{3,2,1,0:T(8,128)(2,1)S(1)}, u32[]{:S(2)}, u32[]{:S(2)}) collective-permute-start(bf16[2,3,512,256]{3,2,1,0:T(8,128)(2,1)S(1)} %copy-done), channel_id=1, source_target_pairs={{0,1},{1,0},{2,3},{3,2},{4,5},{5,4},{6,7},{7,6},{8,9},{9,8},{10,11... | collective-permute-start | bytes 4718600 | tf_op jit(solution)/shard_map/ppermute | solution.py:21
  2.0 2.4 %collective-permute-start.4 = (bf16[2,64,256]{2,1,0:T(8,128)(2,1)S(1)}, bf16[2,64,256]{2,1,0:T(8,128)(2,1)S(1)}, u32[]{:S(2)}, u32[]{:S(2)}) collective-permute-start(bf16[2,64,256]{2,1,0:T(8,128)(2,1)S(1)} %pad_maximum_fusion.own_ref.after_any), channel_id=1, source_target_pairs={{2,0},{0,2},{6,4},{4,6},{10,8},{8,10},{14,12},{12,14},{3,1},{1,3},... | collective-permute-start | bytes 196616 | tf_op jit(solution)/shard_map/ppermute | solution.py:45
  4.4 0.6 %collective-permute-start.3 = (bf16[2,64,256]{2,1,0:T(8,128)(2,1)S(1)}, bf16[2,64,256]{2,1,0:T(8,128)(2,1)S(1)}, u32[]{:S(2)}, u32[]{:S(2)}) collective-permute-start(bf16[2,64,256]{2,1,0:T(8,128)(2,1)S(1)} %pad_maximum_fusion.own_ref.after_any), channel_id=1, source_target_pairs={{1,0},{0,2},{6,4},{4,6},{10,8},{8,10},{14,12},{15,14},{5,3},{3,5},... | collective-permute-start | bytes 196616 | tf_op jit(solution)/shard_map/ppermute | solution.py:45
  5.0 0.0 collective-permute-start.2
  5.7 1.0 %shard_map.102 = (s32[4,8]{1,0:T(4,128)S(1)}, bf16[288,128]{1,0:T(8,128)(2,1)S(1)}) custom-call(bf16[2,64,256]{2,1,0:T(8,128)(2,1)S(1)} %pad_maximum_fusion.own_ref.after_any, s32[4,8]{1,0:T(4,128)} %bitcast.8, bf16[3,3,32,64]{3,2,1,0:T(8,128)(2,1)} %mw_any.1, bf16[1,32]{1,0:T(2,128)(2,1)} %bitcast.9, bf16[1,32]{1,0:T(2,128)(2,1)} %bitcast.10), custom_call_target="tpu_custom_call" | custom-call | tf_op jit(solution)/shard_map/pallas_call | solution.py:447
  6.7 0.0 copy-start.1
  6.7 0.9 %collective-permute-done.2.r2_ref = bf16[2,16,256]{2,1,0:T(8,128)(2,1)S(1)} collective-permute-done((bf16[2,16,256]{2,1,0:T(8,128)(2,1)S(1)}, bf16[2,16,256]{2,1,0:T(8,128)(2,1)S(1)}, u32[]{:S(2)}, u32[]{:S(2)}) %collective-permute-start.2) | collective-permute-done | bytes 16416 | tf_op jit(solution)/shard_map/ppermute | solution.py:30
  7.6 0.0 collective-permute-done.4.even_ref
  7.6 0.5 %collective-permute-done.3.odd_ref = bf16[2,64,256]{2,1,0:T(8,128)(2,1)S(1)} collective-permute-done((bf16[2,64,256]{2,1,0:T(8,128)(2,1)S(1)}, bf16[2,64,256]{2,1,0:T(8,128)(2,1)S(1)}, u32[]{:S(2)}, u32[]{:S(2)}) %collective-permute-start.3) | collective-permute-done | bytes 65568 | tf_op jit(solution)/shard_map/ppermute | solution.py:45
  8.1 0.0 collective-permute-done.5.refs_4_
  8.1 0.0 copy-done.1
  8.1 1.0 %shard_map.103 = (bf16[80,128]{1,0:T(8,128)(2,1)S(1)}, bf16[448,128]{1,0:T(8,128)(2,1)S(1)}) custom-call(s32[1]{0:T(128)S(6)} %copy.11.refs_0_.length_ref, f32[144,512]{1,0:T(8,128)S(1)} %shard_map.101.refs_1_, bf16[2,3,512,256]{3,2,1,0:T(8,128)(2,1)S(1)} %copy-done, bf16[512,128]{1,0:T(8,128)(2,1)S(1)} %copy-done.1, ...), custom_call_target="tpu_custom_call" | custom-call | tf_op jit(solution)/shard_map/pallas_call | solution.py:470
  9.1 0.7 %collective-permute-start.6 = (bf16[448,128]{1,0:T(8,128)(2,1)S(1)}, bf16[448,128]{1,0:T(8,128)(2,1)S(1)}, u32[]{:S(2)}, u32[]{:S(2)}) collective-permute-start(bf16[448,128]{1,0:T(8,128)(2,1)S(1)} %get-tuple-element.26.refs_2_), channel_id=1, source_target_pairs={{0,1},{1,0},{2,3},{3,2},{4,5},{5,4},{6,7},{7,6},{8,9},{9,8},{10,11... | collective-permute-start | bytes 344072 | tf_op jit(solution)/shard_map/ppermute | solution.py:21
  9.8 0.0 collective-permute-start.7
  9.8 0.9 %collective-permute-done.6.oth_ref.refs_1_.refs_2_ = bf16[448,128]{1,0:T(8,128)(2,1)S(1)} collective-permute-done((bf16[448,128]{1,0:T(8,128)(2,1)S(1)}, bf16[448,128]{1,0:T(8,128)(2,1)S(1)}, u32[]{:S(2)}, u32[]{:S(2)}) %collective-permute-start.6) | collective-permute-done | bytes 114720 | tf_op jit(solution)/shard_map/ppermute | solution.py:21
  10.8 0.5 %shard_map.104 = (f32[3,128,384]{2,1,0:T(8,128)S(1)}, bf16[1152,256]{1,0:T(8,128)(2,1)S(1)}, f32[8,256]{1,0:T(8,128)S(1)}, bf16[16,512]{1,0:T(8,128)(2,1)S(1)}) custom-call(s32[1]{0:T(128)S(6)} %copy.11.refs_0_.length_ref, s32[4,8]{1,0:T(4,128)S(1)} %get-tuple-element.27.mask_ref, bf16[288,128]{1,0:T(8,128)(2,1)S(1)} %get-tuple-element.25.refs_7_.own_ref, ...), custom_call_target="tpu_custom_call" | custom-call | tf_op jit(solution)/shard_map/pallas_call | solution.py:482
  11.3 1.2 %collective-permute-done.7.refs_1_ = bf16[80,128]{1,0:T(8,128)(2,1)S(1)} collective-permute-done((bf16[80,128]{1,0:T(8,128)(2,1)S(1)}, bf16[80,128]{1,0:T(8,128)(2,1)S(1)}, u32[]{:S(2)}, u32[]{:S(2)}) %collective-permute-start.7) | collective-permute-done | bytes 20512 | tf_op jit(solution)/shard_map/ppermute | solution.py:30
  12.4 2.5 %shard_map.106 = f32[64,128]{1,0:T(8,128)} custom-call(f32[64,128]{1,0:T(8,128)S(1)} %shard_map.105.near_ref, s32[1]{0:T(128)S(6)} %copy.11.refs_0_.length_ref, bf16[80,128]{1,0:T(8,128)(2,1)S(1)} %collective-permute-done.7.refs_1_, bf16[448,128]{1,0:T(8,128)(2,1)S(1)} %get-tuple-element.26.refs_2_, f32[3,128,384]{2,1,0:T(8,128)S(1)} %get-tuple-element.28.refs_3_, ...), custom_call_target="tpu_custom_call" | custom-call | tf_op jit(solution)/shard_map/pallas_call | solution.py:511
  (4 shorter events, 0.0 us)
Async XLA Ops:
  0.0 1.6 %copy-start = (bf16[2,3,512,256]{3,2,1,0:T(8,128)(2,1)S(1)}, bf16[2,3,512,256]{3,2,1,0:T(8,128)(2,1)}, u32[]{:S(2)}) copy-start(bf16[2,3,512,256]{3,2,1,0:T(8,128)(2,1)} %refs_2_.1) | copy-start | bytes 4718596
  0.0 1.6 %collective-permute-start.1 = (bf16[2,256]{1,0:T(2,128)(2,1)}, bf16[2,256]{1,0:T(2,128)(2,1)S(1)}, u32[]{:S(2)}, u32[]{:S(2)}) collective-permute-start(bf16[2,256]{1,0:T(2,128)(2,1)} %cb_any.1), channel_id=1, source_target_pairs={{0,1},{1,0},{2,3},{3,2},{4,5},{5,4},{6,7},{7,6},{8,9},{9,8},{10,11... | collective-permute-start | bytes 3080 | tf_op jit(solution)/shard_map/ppermute | solution.py:21
  0.1 1.5 %collective-permute-start = (bf16[64,256]{1,0:T(8,128)(2,1)}, bf16[64,256]{1,0:T(8,128)(2,1)S(1)}, u32[]{:S(2)}, u32[]{:S(2)}) collective-permute-start(bf16[64,256]{1,0:T(8,128)(2,1)} %own_any.1), channel_id=1, source_target_pairs={{0,1},{1,0},{2,3},{3,2},{4,5},{5,4},{6,7},{7,6},{8,9},{9,8},{10,11... | collective-permute-start | bytes 98312 | tf_op jit(solution)/shard_map/ppermute | solution.py:21
  1.6 6.5 %collective-permute-start.5 = (bf16[2,3,512,256]{3,2,1,0:T(8,128)(2,1)S(1)}, bf16[2,3,512,256]{3,2,1,0:T(8,128)(2,1)S(1)}, u32[]{:S(2)}, u32[]{:S(2)}) collective-permute-start(bf16[2,3,512,256]{3,2,1,0:T(8,128)(2,1)S(1)} %copy-done), channel_id=1, source_target_pairs={{0,1},{1,0},{2,3},{3,2},{4,5},{5,4},{6,7},{7,6},{8,9},{9,8},{10,11... | collective-permute-start | bytes 4718600 | tf_op jit(solution)/shard_map/ppermute | solution.py:21
  2.0 5.6 %collective-permute-start.4 = (bf16[2,64,256]{2,1,0:T(8,128)(2,1)S(1)}, bf16[2,64,256]{2,1,0:T(8,128)(2,1)S(1)}, u32[]{:S(2)}, u32[]{:S(2)}) collective-permute-start(bf16[2,64,256]{2,1,0:T(8,128)(2,1)S(1)} %pad_maximum_fusion.own_ref.after_any), channel_id=1, source_target_pairs={{2,0},{0,2},{6,4},{4,6},{10,8},{8,10},{14,12},{12,14},{3,1},{1,3},... | collective-permute-start | bytes 196616 | tf_op jit(solution)/shard_map/ppermute | solution.py:45
  4.4 3.7 %collective-permute-start.3 = (bf16[2,64,256]{2,1,0:T(8,128)(2,1)S(1)}, bf16[2,64,256]{2,1,0:T(8,128)(2,1)S(1)}, u32[]{:S(2)}, u32[]{:S(2)}) collective-permute-start(bf16[2,64,256]{2,1,0:T(8,128)(2,1)S(1)} %pad_maximum_fusion.own_ref.after_any), channel_id=1, source_target_pairs={{1,0},{0,2},{6,4},{4,6},{10,8},{8,10},{14,12},{15,14},{5,3},{3,5},... | collective-permute-start | bytes 196616 | tf_op jit(solution)/shard_map/ppermute | solution.py:45
  5.0 2.6 %collective-permute-start.2 = (bf16[2,16,256]{2,1,0:T(8,128)(2,1)S(1)}, bf16[2,16,256]{2,1,0:T(8,128)(2,1)S(1)}, u32[]{:S(2)}, u32[]{:S(2)}) collective-permute-start(bf16[2,16,256]{2,1,0:T(8,128)(2,1)S(1)} %slice.3), channel_id=1, source_target_pairs={{1,0},{5,1},{3,2},{7,3},{0,4},{9,5},{2,6},{11,7},{4,8},{13,9},{6,1... | collective-permute-start | bytes 49160 | tf_op jit(solution)/shard_map/ppermute | solution.py:30
  6.7 1.4 %copy-start.1 = (bf16[512,128]{1,0:T(8,128)(2,1)S(1)}, bf16[512,128]{1,0:T(8,128)(2,1)}, u32[]{:S(2)}) copy-start(bf16[512,128]{1,0:T(8,128)(2,1)} %refs_3_.1) | copy-start | bytes 393220
  9.1 1.6 %collective-permute-start.6 = (bf16[448,128]{1,0:T(8,128)(2,1)S(1)}, bf16[448,128]{1,0:T(8,128)(2,1)S(1)}, u32[]{:S(2)}, u32[]{:S(2)}) collective-permute-start(bf16[448,128]{1,0:T(8,128)(2,1)S(1)} %get-tuple-element.26.refs_2_), channel_id=1, source_target_pairs={{0,1},{1,0},{2,3},{3,2},{4,5},{5,4},{6,7},{7,6},{8,9},{9,8},{10,11... | collective-permute-start | bytes 344072 | tf_op jit(solution)/shard_map/ppermute | solution.py:21
  9.8 2.6 %collective-permute-start.7 = (bf16[80,128]{1,0:T(8,128)(2,1)S(1)}, bf16[80,128]{1,0:T(8,128)(2,1)S(1)}, u32[]{:S(2)}, u32[]{:S(2)}) collective-permute-start(bf16[80,128]{1,0:T(8,128)(2,1)S(1)} %get-tuple-element.32), channel_id=1, source_target_pairs={{1,0},{5,1},{3,2},{7,3},{0,4},{9,5},{2,6},{11,7},{4,8},{13,9},{6,1... | collective-permute-start | bytes 61448 | tf_op jit(solution)/shard_map/ppermute | solution.py:30
